TPU v7x, 32 devices: a whole 2x2x4 slice. The times are simulated.
32 devices in a mesh: dp: 8 (over z, core), fsdp: 4 (over y, x).
Axes of the slice: x: 2, y: 2, z: 4, core: 2. Of those that a mesh axis runs over, the one named last changes fastest.
Arguments:
- media: bfloat16 [64, 256, 1536], P(('dp', 'fsdp')), may hold values from -6 to 6
- latents: bfloat16 [64, 64, 1536], P(('dp', 'fsdp')), may hold values from -6 to 6
- upstream: bfloat16 [64, 64, 1536], P(('dp', 'fsdp')), may hold values from -6 to 6
- time_index: int32 [64], P(('dp', 'fsdp')), may hold values from 0 to 7
- live_count: int32 [32], P(('dp', 'fsdp')), may hold values from 0 to 2, as said below
- time_table: bfloat16 [8, 1536], P(None, ('dp', 'fsdp')), may hold values from -5 to 5
- media_gain: bfloat16 [1536], P(('dp', 'fsdp')), may hold values from 0.099609375 to 1.8984375
- media_bias: bfloat16 [1536], P(('dp', 'fsdp')), may hold values from -3 to 3
- latent_gain: bfloat16 [1536], P(('dp', 'fsdp')), may hold values from 0.099609375 to 1.8984375
- latent_bias: bfloat16 [1536], P(('dp', 'fsdp')), may hold values from -3 to 3
- ff_gain: bfloat16 [1536], P(('dp', 'fsdp')), may hold values from 0.099609375 to 1.8984375
- ff_bias: bfloat16 [1536], P(('dp', 'fsdp')), may hold values from -3 to 3
- w_query: bfloat16 [1536, 1536], P(('dp', 'fsdp')), may hold values from -0.15625 to 0.15625
- w_keyval: bfloat16 [1536, 3072], P(('dp', 'fsdp')), may hold values from -0.15625 to 0.15625
- w_out: bfloat16 [1536, 1536], P(('dp', 'fsdp')), may hold values from -0.625 to 0.625
- w_up: bfloat16 [1536, 6144], P(('dp', 'fsdp')), may hold values from -0.15625 to 0.15625
- w_down: bfloat16 [6144, 1536], P(('dp', 'fsdp')), may hold values from -0.078125 to 0.078125
Outputs:
- latents_out: bfloat16 [64, 64, 1536], P(('dp', 'fsdp'))
- media_grad: float32 [64, 256, 1536], P(('dp', 'fsdp'))
- latent_grad: float32 [64, 64, 1536], P(('dp', 'fsdp'))
- table_grad: float32 [8, 1536], P(None, ('dp', 'fsdp'))
- media_gain_grad: float32 [1536], P(('dp', 'fsdp'))
- media_bias_grad: float32 [1536], P(('dp', 'fsdp'))
- latent_gain_grad: float32 [1536], P(('dp', 'fsdp'))
- latent_bias_grad: float32 [1536], P(('dp', 'fsdp'))
- ff_gain_grad: float32 [1536], P(('dp', 'fsdp'))
- ff_bias_grad: float32 [1536], P(('dp', 'fsdp'))
- w_query_grad: float32 [1536, 1536], P(('dp', 'fsdp'))
- w_keyval_grad: float32 [1536, 3072], P(('dp', 'fsdp'))
- w_out_grad: float32 [1536, 1536], P(('dp', 'fsdp'))
- w_up_grad: float32 [1536, 6144], P(('dp', 'fsdp'))
- w_down_grad: float32 [6144, 1536], P(('dp', 'fsdp'))
Inputs may be any that keep to these rules, and one draw needn't show every extreme that they name: live_count[i] images are live on device i, the devices ordered dp first; the counts sum to 32; a quarter of the devices hold 2 live images and another quarter none.
All inputs are finite; a program needn't handle non-finite values.
Results may differ from a plain program's by a relative error of at most 0.012.
Values may be sent and summed in bfloat16 or wider, within the bound.
No kernel may reach another device: no remote copies, remote signals or barrier semaphores. Data moves between devices by JAX's collectives and lax.ppermute only.
A program may use at most 320 MiB of HBM per device.

v0:
```python
import math

import jax
import jax.numpy as jnp
from jax import lax
from jax.sharding import PartitionSpec as P

HEADS = 16
HEAD = 96


norm_eps = 1e-05
highest = lax.Precision.HIGHEST


def norm_rows(inputs, gain, shift):
    row_mean = jnp.mean(inputs, axis=-1, keepdims=True)
    centered = inputs - row_mean
    variance = jnp.mean(centered * centered, axis=-1, keepdims=True)
    return centered * lax.rsqrt(variance + norm_eps) * gain + shift


def exact_gelu(inputs):
    return jax.nn.gelu(inputs, approximate=False)


def mat_rows(left, right):
    return jnp.einsum("crd,de->cre", left, right, preferred_element_type=jnp.float32)


def mat_back(left, right):
    return jnp.einsum("cre,de->crd", left, right, preferred_element_type=jnp.float32)


def mat_outer(left, right):
    return jnp.einsum("crd,cre->de", left, right, preferred_element_type=jnp.float32)


def on_device(
    media,
    latents,
    upstream,
    time_index,
    live_count,
    time_table,
    media_gain,
    media_bias,
    latent_gain,
    latent_bias,
    ff_gain,
    ff_bias,
    w_query,
    w_keyval,
    w_out,
    w_up,
    w_down,
):
    lowtype = jnp.bfloat16
    wide = jnp.float32
    images, patches, model_width = media.shape
    lat_rows = latents.shape[1]
    key_rows = patches + lat_rows
    scale = 1.0 / math.sqrt(HEAD)
    attention_set = (
        lax.all_gather(time_table, ("dp", "fsdp"), axis=1, tiled=True),
        lax.all_gather(media_gain, ("dp", "fsdp"), axis=0, tiled=True),
        lax.all_gather(media_bias, ("dp", "fsdp"), axis=0, tiled=True),
        lax.all_gather(latent_gain, ("dp", "fsdp"), axis=0, tiled=True),
        lax.all_gather(latent_bias, ("dp", "fsdp"), axis=0, tiled=True),
        lax.all_gather(w_query, ("dp", "fsdp"), axis=0, tiled=True),
        lax.all_gather(w_keyval, ("dp", "fsdp"), axis=0, tiled=True),
        lax.all_gather(w_out, ("dp", "fsdp"), axis=0, tiled=True),
    )
    (
        table_full,
        media_gain_full,
        media_bias_full,
        latent_gain_full,
        latent_bias_full,
        query_full,
        keyval_full,
        out_full,
    ) = attention_set
    mixer_set = (
        lax.all_gather(ff_gain, ("dp", "fsdp"), axis=0, tiled=True),
        lax.all_gather(ff_bias, ("dp", "fsdp"), axis=0, tiled=True),
        lax.all_gather(w_up, ("dp", "fsdp"), axis=0, tiled=True),
        lax.all_gather(w_down, ("dp", "fsdp"), axis=0, tiled=True),
    )
    ff_gain_full, ff_bias_full, up_full, down_full = mixer_set
    alive = (jnp.arange(images) < live_count[0]).astype(wide)
    one_hot = (time_index[:, None] == jnp.arange(table_full.shape[0])[None, :]).astype(wide)
    time_rows = jnp.dot(one_hot, table_full.astype(wide), precision=highest)
    media_in = media.astype(wide) + time_rows[:, None, :]
    media_normed, media_norm_back = jax.vjp(
        norm_rows, media_in, media_gain_full.astype(wide), media_bias_full.astype(wide)
    )
    media_norm = media_normed.astype(lowtype)
    latent_normed, latent_norm_back = jax.vjp(
        norm_rows,
        latents.astype(wide),
        latent_gain_full.astype(wide),
        latent_bias_full.astype(wide),
    )
    latent_norm = latent_normed.astype(lowtype)
    query_rows = mat_rows(latent_norm, query_full).astype(lowtype)
    sources = jnp.concatenate([media_norm, latent_norm], axis=1)
    keyval = mat_rows(sources, keyval_full).astype(lowtype)
    key_heads = keyval[:, :, :model_width].reshape(images, key_rows, HEADS, HEAD)
    value_heads = keyval[:, :, model_width:].reshape(images, key_rows, HEADS, HEAD)
    query_heads = query_rows.reshape(images, lat_rows, HEADS, HEAD)

    def score_rows():
        raw = (
            jnp.einsum("cqhe,ckhe->ckhq", query_heads, key_heads, preferred_element_type=wide)
            * scale
        )
        return raw.reshape(images, key_rows, HEADS * lat_rows)

    scores = score_rows()
    row_top = jnp.max(scores, axis=1, keepdims=True)
    exps = jnp.exp(scores - row_top)
    sums = jnp.sum(exps, axis=1, keepdims=True)
    attention = exps / sums
    log_total = row_top + jnp.log(sums)
    attention_low = attention.reshape(images, key_rows, HEADS, lat_rows).astype(lowtype)
    mixed_rows = jnp.einsum(
        "ckhq,ckhe->cqhe", attention_low, value_heads, preferred_element_type=wide
    )
    mixed_rows = mixed_rows.reshape(images, lat_rows, model_width).astype(lowtype)
    middle = latents.astype(wide) + mat_rows(mixed_rows, out_full)
    ffn_normed, ffn_norm_back = jax.vjp(
        norm_rows, middle, ff_gain_full.astype(wide), ff_bias_full.astype(wide)
    )
    ffn_input = ffn_normed.astype(lowtype)
    pre_act = mat_rows(ffn_input, up_full)
    activated, gelu_back = jax.vjp(exact_gelu, pre_act)
    hidden = activated.astype(lowtype)
    result = middle + mat_rows(hidden, down_full)
    live_mask = alive[:, None, None]
    latents_out = (result * live_mask).astype(lowtype)
    up_full, down_full = (
        lax.all_gather(w_up, ("dp", "fsdp"), axis=0, tiled=True),
        lax.all_gather(w_down, ("dp", "fsdp"), axis=0, tiled=True),
    )
    d_out = upstream.astype(wide) * live_mask
    d_out_low = d_out.astype(lowtype)
    down_grad = mat_outer(hidden, d_out_low)
    d_hidden = mat_back(d_out_low, down_full)
    (d_pre,) = gelu_back(d_hidden)
    d_pre_low = d_pre.astype(lowtype)
    up_grad = mat_outer(ffn_input, d_pre_low)
    d_ffn_input = mat_back(d_pre_low, up_full)
    d_middle_norm, ff_gain_grad, ff_bias_grad = ffn_norm_back(d_ffn_input)
    d_middle = d_out + d_middle_norm
    mixer_grads = (
        lax.psum_scatter(ff_gain_grad, ("dp", "fsdp"), scatter_dimension=0, tiled=True),
        lax.psum_scatter(ff_bias_grad, ("dp", "fsdp"), scatter_dimension=0, tiled=True),
        lax.psum_scatter(up_grad, ("dp", "fsdp"), scatter_dimension=0, tiled=True),
        lax.psum_scatter(down_grad, ("dp", "fsdp"), scatter_dimension=0, tiled=True),
    )
    query_full, keyval_full, out_full = (
        lax.all_gather(w_query, ("dp", "fsdp"), axis=0, tiled=True),
        lax.all_gather(w_keyval, ("dp", "fsdp"), axis=0, tiled=True),
        lax.all_gather(w_out, ("dp", "fsdp"), axis=0, tiled=True),
    )
    d_branch = d_middle.astype(lowtype)
    out_grad_weight = mat_outer(mixed_rows, d_branch)
    d_mixed = mat_back(d_branch, out_full).astype(lowtype)
    d_mixed_heads = d_mixed.reshape(images, lat_rows, HEADS, HEAD)
    attention = jnp.exp(score_rows() - log_total)
    attention_low = attention.reshape(images, key_rows, HEADS, lat_rows).astype(lowtype)
    d_attention = jnp.einsum(
        "cqhe,ckhe->ckhq", d_mixed_heads, value_heads, preferred_element_type=wide
    )
    d_attention = d_attention.reshape(images, key_rows, HEADS * lat_rows)
    d_values = jnp.einsum(
        "ckhq,cqhe->ckhe", attention_low, d_mixed_heads, preferred_element_type=wide
    )
    row_delta = jnp.sum(attention * d_attention, axis=1, keepdims=True)
    d_scores = (attention * (d_attention - row_delta)).reshape(images, key_rows, HEADS, lat_rows)
    d_scores = d_scores.astype(lowtype)
    d_query = (
        jnp.einsum("ckhq,ckhe->cqhe", d_scores, key_heads, preferred_element_type=wide) * scale
    )
    d_query = d_query.reshape(images, lat_rows, model_width).astype(lowtype)
    d_keys = (
        jnp.einsum("ckhq,cqhe->ckhe", d_scores, query_heads, preferred_element_type=wide) * scale
    )
    d_keyval = jnp.concatenate(
        [
            d_keys.reshape(images, key_rows, model_width),
            d_values.reshape(images, key_rows, model_width),
        ],
        axis=2,
    ).astype(lowtype)
    query_grad = mat_outer(latent_norm, d_query)
    keyval_grad = mat_outer(sources, d_keyval)
    d_sources = mat_back(d_keyval, keyval_full)
    d_latent_norm = mat_back(d_query, query_full) + d_sources[:, patches:, :]
    d_latent_in, latent_gain_grad, latent_bias_grad = latent_norm_back(d_latent_norm)
    d_media_in, media_gain_grad, media_bias_grad = media_norm_back(d_sources[:, :patches, :])
    latent_grad = d_middle + d_latent_in
    table_cols = jnp.dot(jnp.sum(d_media_in, axis=1).T, one_hot, precision=highest)
    attention_grads = (
        lax.psum_scatter(table_cols, ("dp", "fsdp"), scatter_dimension=0, tiled=True),
        lax.psum_scatter(media_gain_grad, ("dp", "fsdp"), scatter_dimension=0, tiled=True),
        lax.psum_scatter(media_bias_grad, ("dp", "fsdp"), scatter_dimension=0, tiled=True),
        lax.psum_scatter(latent_gain_grad, ("dp", "fsdp"), scatter_dimension=0, tiled=True),
        lax.psum_scatter(latent_bias_grad, ("dp", "fsdp"), scatter_dimension=0, tiled=True),
        lax.psum_scatter(query_grad, ("dp", "fsdp"), scatter_dimension=0, tiled=True),
        lax.psum_scatter(keyval_grad, ("dp", "fsdp"), scatter_dimension=0, tiled=True),
        lax.psum_scatter(out_grad_weight, ("dp", "fsdp"), scatter_dimension=0, tiled=True),
    )
    table_grad = attention_grads[0].T
    return (
        latents_out,
        d_media_in,
        latent_grad,
        table_grad,
        attention_grads[1],
        attention_grads[2],
        attention_grads[3],
        attention_grads[4],
        mixer_grads[0],
        mixer_grads[1],
        attention_grads[5],
        attention_grads[6],
        attention_grads[7],
        mixer_grads[2],
        mixer_grads[3],
    )


def solution(mesh):
    placed = (
        P(("dp", "fsdp"), None, None),
        P(("dp", "fsdp"), None, None),
        P(("dp", "fsdp"), None, None),
        P(("dp", "fsdp")),
        P(("dp", "fsdp")),
        P(None, ("dp", "fsdp")),
        P(("dp", "fsdp")),
        P(("dp", "fsdp")),
        P(("dp", "fsdp")),
        P(("dp", "fsdp")),
        P(("dp", "fsdp")),
        P(("dp", "fsdp")),
        P(("dp", "fsdp"), None),
        P(("dp", "fsdp"), None),
        P(("dp", "fsdp"), None),
        P(("dp", "fsdp"), None),
        P(("dp", "fsdp"), None),
    )
    return jax.shard_map(
        on_device,
        mesh=mesh,
        in_specs=placed,
        out_specs=(
            P(("dp", "fsdp"), None, None),
            P(("dp", "fsdp"), None, None),
            P(("dp", "fsdp"), None, None),
            P(None, ("dp", "fsdp")),
            P(("dp", "fsdp")),
            P(("dp", "fsdp")),
            P(("dp", "fsdp")),
            P(("dp", "fsdp")),
            P(("dp", "fsdp")),
            P(("dp", "fsdp")),
            P(("dp", "fsdp"), None),
            P(("dp", "fsdp"), None),
            P(("dp", "fsdp"), None),
            P(("dp", "fsdp"), None),
            P(("dp", "fsdp"), None),
        ),
        check_vma=False,
    )
```

profile of v0, /device:TPU:0, one launch (start us, length us, event | category | flops | bytes accessed | tf_op | source)
XLA Modules:
  0.0 1863.5 jit_solution(8463081267660879541)
XLA Ops:
  15.7 42.8 %all-reduce.13 = (bf16[1536]{0:T(1024)(128)(2,1)S(1)}, bf16[1536]{0:T(1024)(128)(2,1)S(1)}, bf16[1536]{0:T(1024)(128)(2,1)S(1)}, bf16[1536]{0:T(1024)(128)(2,1)S...) all-reduce(bf16[1536]{0:T(1024)(128)(2,1)S(1)} %dynamic-update-slic, ...), channel_id=1, replica_groups=mesh['dp'=8,'fsdp'=4] {'dp','fsdp'}, use_global_device_ids=true, to_apply=%add.3 | all-reduce | flops 9216 | bytes 36864
  58.6 66.8 %all-gather = bf16[32,48,8]{1,2,0:T(8,128)(2,1)S(1)} all-gather(bf16[1,48,8]{1,2,0:T(8,128)(2,1)} %bitcast.144), channel_id=1, replica_groups=mesh['dp'=8,'fsdp'=4] {'dp','fsdp'}, dimensions={0}, use_global_device_ids=true | all-gather | bytes 25344 | tf_op jit(solution)/shard_map/all_gather | solution.py:65
  129.1 1.4 fusion.80
  133.3 2.0 add_convert_fusion.1
  135.3 3.3 fusion.52
  138.6 1.3 reshape.200
  139.8 21.8 %all-gather.7.cloned.1.call-done = bf16[1536,3072]{1,0:T(8,128)(2,1)} async-done(((bf16[48,3072]{1,0:T(8,128)(2,1)}), bf16[1536,3072]{1,0:T(8,128)(2,1)}) %all-gather.7.cloned.1.call-update) | async-done | bytes 9437200 | tf_op jit(solution)/shard_map/all_gather | solution.py:71
  161.6 9.1 fusion.12
  170.8 1.7 fusion.110
  172.5 4.1 copy.54
  176.6 2.5 copy.55
  179.0 2.7 bitcast_reduce_fusion
  182.8 1.6 fusion.68
  185.5 2.3 convert_element_type.111
  187.9 38.8 %all-gather.11.cloned.1.call-done = bf16[1536,1536]{1,0:T(8,128)(2,1)} async-done(((bf16[48,1536]{1,0:T(8,128)(2,1)}), bf16[1536,1536]{1,0:T(8,128)(2,1)}) %all-gather.11.cloned.1.call-update) | async-done | bytes 4718608 | tf_op jit(solution)/shard_map/all_gather | solution.py:72
  226.7 3.4 fusion.111
  232.4 120.5 %all-gather.13.cloned.1.call-done = bf16[1536,6144]{1,0:T(8,128)(2,1)} async-done(((bf16[48,6144]{1,0:T(8,128)(2,1)}), bf16[1536,6144]{1,0:T(8,128)(2,1)}) %all-gather.13.cloned.1.call-update) | async-done | bytes 18874384 | tf_op jit(solution)/shard_map/all_gather | solution.py:87
  352.9 13.4 fusion.84
  366.4 112.2 %all-gather.15.cloned.1.call-done = bf16[6144,1536]{1,0:T(8,128)(2,1)} async-done(((bf16[192,1536]{1,0:T(8,128)(2,1)}), bf16[6144,1536]{1,0:T(8,128)(2,1)}) %all-gather.15.cloned.1.call-update) | async-done | bytes 18874384 | tf_op jit(solution)/shard_map/all_gather | solution.py:88
  478.5 18.2 add_convert_fusion
  496.8 14.9 multiply_reduce_fusion.3
  511.7 1.7 fusion.109
  515.5 4.7 fusion.55
  520.2 2.2 reshape.201
  522.4 3.6 convolution_convert_fusion
  526.1 1.4 fusion.24
  531.4 4.1 copy.62
  535.6 2.5 copy.61
  538.1 10.3 fusion.8
  549.2 2.3 multiply_reduce_fusion
  551.5 2.4 fusion.108
  554.9 1.7 fusion.96
  556.7 5.0 convolution_bitcast_fusion.4
  562.6 5.1 convolution_bitcast_fusion.3
  567.8 1.5 copy-done.18
  569.2 13.1 convolution_bitcast_fusion.2
  584.1 14.9 convolution_bitcast_fusion.1
  600.2 19.6 %convolution_bitcast_fusion = f32[6144,1536]{1,0:T(8,128)} fusion(bf16[2,64,1536]{2,1,0:T(8,128)(2,1)S(1)} %copy-done.21, f32[2]{0:T(128)S(1)} %copy-done.52, f32[2,64,6144]{2,1,0:T(8,128)} %get-tuple-element.49, u8[64,6144]{1,0:T(8,128)(4,1)S(1)} %copy-done.57, u8[64,6144]{1,0:T(8,128)(4,1)S(1)} %copy-done.56), kind=kOutput, calls=%fused_computation | convolution fusion | flops 2471559168 | bytes 42074120 | tf_op jit(solution)/shard_map/crd,cre->de/dot_general | solution.py:36
  620.8 5.0 fusion.107
  626.2 39.5 %all-reduce.12 = (f32[1536]{0:T(1024)S(1)}, f32[1536]{0:T(1024)S(1)}, f32[1536]{0:T(1024)S(1)}, f32[1536]{0:T(1024)S(1)}, f32[1536]{0:T(1024)S(1)}, /*index=5*/f32[1536]{0:T(1024)S(1)}) all-reduce(f32[1536]{0:T(1024)} %get-tuple-element.15, f32[1536]{0:T(1024)} %get-tuple-element.17, ...), channel_id=3, replica_groups=mesh['dp'=8,'fsdp'=4] {'dp','fsdp'}, use_global_device_ids=true, to_apply=%region_18.0.clone | all-reduce | flops 9216 | bytes 73728
  669.3 1.9 add_add_fusion.3
  671.2 13.4 fusion.58
  684.6 1.4 copy.65
  686.0 105.6 %reduce-scatter.9.cloned.1.call-done = f32[48,1536]{1,0:T(8,128)} async-done(((f32[1536,1536]{1,0:T(8,128)}), f32[48,1536]{1,0:T(8,128)}) %reduce-scatter.9.cloned.1.call-update) | async-done | bytes 294928 | tf_op jit(solution)/shard_map/reduce_scatter | solution.py:211
  791.6 142.3 %reduce-scatter.13.cloned.1.call-done = f32[48,1536]{1,0:T(8,128)} async-done(((f32[1536,1536]{1,0:T(8,128)}), f32[48,1536]{1,0:T(8,128)}) %reduce-scatter.13.cloned.1.call-update) | async-done | bytes 294928 | tf_op jit(solution)/shard_map/reduce_scatter | solution.py:213
  933.8 212.6 %reduce-scatter.11.cloned.1.call-done = f32[48,3072]{1,0:T(8,128)} async-done(((f32[1536,3072]{1,0:T(8,128)}), f32[48,3072]{1,0:T(8,128)}) %reduce-scatter.11.cloned.1.call-update) | async-done | bytes 589840 | tf_op jit(solution)/shard_map/reduce_scatter | solution.py:212
  1146.4 354.3 %reduce-scatter.15.cloned.1.call-done = f32[48,6144]{1,0:T(8,128)} async-done(((f32[1536,6144]{1,0:T(8,128)}), f32[48,6144]{1,0:T(8,128)}) %reduce-scatter.15.cloned.1.call-update) | async-done | bytes 1179664 | tf_op jit(solution)/shard_map/reduce_scatter | solution.py:159
  1500.7 356.1 %reduce-scatter.17.cloned.1.call-done = f32[192,1536]{1,0:T(8,128)} async-done(((f32[6144,1536]{1,0:T(8,128)}), f32[192,1536]{1,0:T(8,128)}) %reduce-scatter.17.cloned.1.call-update) | async-done | bytes 1179664 | tf_op jit(solution)/shard_map/reduce_scatter | solution.py:160
  (195 shorter events, 35.4 us)
Async XLA Ops:
  7.2 125.8 %copy-start.6 = (bf16[2,64,1536]{2,1,0:T(8,128)(2,1)S(1)}, bf16[2,64,1536]{2,1,0:T(8,128)(2,1)}, u32[]{:S(2)}) copy-start(bf16[2,64,1536]{2,1,0:T(8,128)(2,1)} %param.18) | copy-start | bytes 1179652
  7.2 124.1 %copy-start = (bf16[2,256,1536]{2,1,0:T(8,128)(2,1)S(1)}, bf16[2,256,1536]{2,1,0:T(8,128)(2,1)}, u32[]{:S(2)}) copy-start(bf16[2,256,1536]{2,1,0:T(8,128)(2,1)} %param.17) | copy-start | bytes 4718596
  7.2 128.1 %all-gather.9.cloned.1.call-start = ((), (), s32[]{:S(2)}) async-start(), calls=%async_computation.7 | async-start | bytes 4866048 | tf_op jit(solution)/shard_map/all_gather | solution.py:70
  7.9 153.7 %all-gather.7.cloned.1.call-start = ((), (), s32[]{:S(2)}) async-start(), calls=%async_computation.6 | async-start | bytes 9732096 | tf_op jit(solution)/shard_map/all_gather | solution.py:71
  8.7 218.0 %all-gather.11.cloned.1.call-start = ((), (), s32[]{:S(2)}) async-start(), calls=%async_computation.8 | async-start | bytes 4866048 | tf_op jit(solution)/shard_map/all_gather | solution.py:72
  9.4 343.5 %all-gather.13.cloned.1.call-start = ((), (), s32[]{:S(2)}) async-start(), calls=%async_computation.9 | async-start | bytes 19464192 | tf_op jit(solution)/shard_map/all_gather | solution.py:87
  10.0 468.5 %all-gather.15.cloned.1.call-start = ((), (), s32[]{:S(2)}) async-start(), calls=%async_computation.10 | async-start | bytes 19464192 | tf_op jit(solution)/shard_map/all_gather | solution.py:88
  10.6 674.0 %reduce-scatter.19.cloned.1.call-start = ((), (), s32[]{:S(2)}) async-start(), calls=%async_computation.16 | async-start | bytes 811008
  58.6 76.7 %copy-start.24 = (f32[1536]{0:T(1024)}, f32[1536]{0:T(1024)S(1)}, u32[]{:S(2)}) copy-start(f32[1536]{0:T(1024)S(1)} %convert_element_type.103) | copy-start | bytes 18436
  58.6 76.7 %copy-start.27 = (f32[1536]{0:T(1024)}, f32[1536]{0:T(1024)S(1)}, u32[]{:S(2)}) copy-start(f32[1536]{0:T(1024)S(1)} %convert_element_type.100) | copy-start | bytes 18436
  129.1 6.2 copy-start.34
  131.7 3.6 copy-start.45
  132.9 2.3 copy-start.41
  133.3 28.4 %copy-start.13 = (bf16[2,64,1536]{2,1,0:T(8,128)(2,1)}, bf16[2,64,1536]{2,1,0:T(8,128)(2,1)S(1)}, u32[]{:S(2)}) copy-start(bf16[2,64,1536]{2,1,0:T(8,128)(2,1)S(1)} %fusion.78) | copy-start | bytes 1179652
  135.3 26.3 %copy-start.19 = (bf16[2,256,1536]{2,1,0:T(8,128)(2,1)S(1)}, bf16[2,256,1536]{2,1,0:T(8,128)(2,1)}, u32[]{:S(2)}) copy-start(bf16[2,256,1536]{2,1,0:T(8,128)(2,1)} %add_convert_fusion.1) | copy-start | bytes 4718596
  179.0 3.7 copy-start.8
  181.7 2.7 copy-start.29
  226.7 5.1 copy-start.30
  226.7 5.1 copy-start.33
  230.1 1.7 copy-start.36
  232.4 246.1 %copy-start.20 = (bf16[2,64,1536]{2,1,0:T(8,128)(2,1)S(1)}, bf16[2,64,1536]{2,1,0:T(8,128)(2,1)}, u32[]{:S(2)}) copy-start(bf16[2,64,1536]{2,1,0:T(8,128)(2,1)} %param.19) | copy-start | bytes 1179652
  496.7 15.0 copy-start.51
  496.7 15.0 copy-start.22
  496.7 15.0 copy-start.37
  496.7 15.0 copy-start.39
  522.4 3.7 copy-start.9
  522.4 3.7 copy-start.16
  522.4 3.7 copy-start.26
  528.5 1.7 copy-start.5
  538.1 10.3 copy-start.1
  538.1 10.3 copy-start.28
  548.4 3.1 copy-start.2
  551.5 3.3 copy-start.54
  554.0 2.7 copy-start.14
  556.6 235.0 %reduce-scatter.9.cloned.1.call-start = ((), (), s32[]{:S(2)}) async-start(), calls=%async_computation.11 | async-start | bytes 9732096 | tf_op jit(solution)/shard_map/reduce_scatter | solution.py:211
  561.7 372.2 %reduce-scatter.13.cloned.1.call-start = ((), (), s32[]{:S(2)}) async-start(), calls=%async_computation.13 | async-start | bytes 9732096 | tf_op jit(solution)/shard_map/reduce_scatter | solution.py:213
  567.7 578.7 %reduce-scatter.11.cloned.1.call-start = ((), (), s32[]{:S(2)}) async-start(), calls=%async_computation.12 | async-start | bytes 19464192 | tf_op jit(solution)/shard_map/reduce_scatter | solution.py:212
  582.4 1.7 copy-start.12
  582.4 1.7 copy-start.23
  582.4 1.7 copy-start.31
  582.4 1.7 copy-start.38
  582.4 918.3 %reduce-scatter.15.cloned.1.call-start = ((), (), s32[]{:S(2)}) async-start(), calls=%async_computation.14 | async-start | bytes 38928384 | tf_op jit(solution)/shard_map/reduce_scatter | solution.py:159
  599.0 1257.8 %reduce-scatter.17.cloned.1.call-start = ((), (), s32[]{:S(2)}) async-start(), calls=%async_computation.15 | async-start | bytes 38928384 | tf_op jit(solution)/shard_map/reduce_scatter | solution.py:160
  620.8 5.0 copy-start.49
  620.8 5.0 copy-start.46
  620.8 48.4 %copy-start.11 = (f32[2,64,1536]{2,1,0:T(8,128)S(1)}, f32[2,64,1536]{2,1,0:T(8,128)}, u32[]{:S(2)}) copy-start(f32[2,64,1536]{2,1,0:T(8,128)} %copy-done.10) | copy-start | bytes 2359300
  625.8 45.4 %copy-start.53 = (f32[2]{0:T(128)S(1)}, f32[2]{0:T(128)}, u32[]{:S(2)}) copy-start(f32[2]{0:T(128)} %compare_convert_fusion) | copy-start | bytes 28
  665.7 5.5 copy-start.55
  (21 other events, 22.1 us)
Sparse Core Ops, SparseCore 0:
  10.9 66.6 all-gather.8
  80.5 81.0 all-gather.6
  164.5 62.1 all-gather.10
  229.4 123.4 all-gather.12
  355.7 122.8 all-gather.14
  556.7 93.6 reduce-scatter.18
  656.9 134.5 reduce-scatter.8
  799.0 134.7 reduce-scatter.12
  940.8 205.5 reduce-scatter.10
  1153.3 347.3 reduce-scatter.14
  1508.9 347.8 reduce-scatter.16
where the time goes:
time: 1870 us; the launch traced here: 1860 us
  waiting for transfers between devices  1470 us (79%)
  matrix products  167 us (9%)
  blocking collectives  149 us (8%)
  local copies, waits for them, and re-layouts  42.4 us (2%)
  other arithmetic  21.7 us (1%)
    reduce_scatter x1, waiting for transfers between devices, on_device(): lax.psum_scatter(down_grad, ('dp', 'fsdp'), scatter_dimension=0, tiled=True)  356 us
    reduce_scatter x1, waiting for transfers between devices, on_device(): lax.psum_scatter(up_grad, ('dp', 'fsdp'), scatter_dimension=0, tiled=True)  354 us
    reduce_scatter x1, waiting for transfers between devices, on_device(): lax.psum_scatter(keyval_grad, ('dp', 'fsdp'), scatter_dimension=0, tiled=...  213 us
    reduce_scatter x1, waiting for transfers between devices, on_device(): lax.psum_scatter(out_grad_weight, ('dp', 'fsdp'), scatter_dimension=0, ti...  142 us
    all_gather x1, waiting for transfers between devices, on_device(): lax.all_gather(w_up, ('dp', 'fsdp'), axis=0, tiled=True)  121 us
    all_gather x1, waiting for transfers between devices, on_device(): lax.all_gather(w_down, ('dp', 'fsdp'), axis=0, tiled=True)  112 us
    reduce_scatter x1, waiting for transfers between devices, on_device(): lax.psum_scatter(query_grad, ('dp', 'fsdp'), scatter_dimension=0, tiled=T...  106 us
    unnamed x2, blocking collectives  82.3 us
  transfers between devices with their start and end apart: 11, of which 9 were waited for; matrix products, arithmetic and copies ran while one was open for 8% of the time, Pallas kernels for 0%

commit v1 on v0

v1 whole, which is shorter than its diff:
```python
import functools
import math

import jax
import jax.numpy as jnp
from jax import lax
from jax.sharding import PartitionSpec as P

HEAD = 96
AXES = ("dp", "fsdp")
LOW = jnp.bfloat16
WIDE = jnp.float32
HIGHEST = lax.Precision.HIGHEST
NORM_EPS = 1e-05


def norm_rows(inputs, gain, shift):
    row_mean = jnp.mean(inputs, axis=-1, keepdims=True)
    centered = inputs - row_mean
    variance = jnp.mean(centered * centered, axis=-1, keepdims=True)
    return centered * lax.rsqrt(variance + NORM_EPS) * gain + shift


def exact_gelu(inputs):
    return jax.nn.gelu(inputs, approximate=False)


def dot(left, right, contract):
    return lax.dot_general(left, right, (contract, ((), ())), preferred_element_type=WIDE)


def rows_by(left, right):
    return dot(left, right, ((left.ndim - 1,), (0,)))


def rows_back(left, right):
    return dot(left, right, ((left.ndim - 1,), (1,)))


def outer(left, right):
    return dot(left, right, ((0,), (0,)))


class Wires:
    def __init__(self, mesh):
        self.deep = mesh.shape["dp"] // 2
        self.flat = mesh.shape["fsdp"]
        self.count = 2 * self.deep * self.flat
        places = [
            (z, c, f) for z in range(self.deep) for c in range(2) for f in range(self.flat)
        ]

        def number(z, c, f):
            return (z * 2 + c) * self.flat + f

        def moves(target):
            return [(number(*place), number(*target(*place))) for place in places]

        self.bits = [1 << k for k in range(self.flat.bit_length() - 1)]
        self.swap = moves(lambda z, c, f: (z, 1 - c, f))
        self.rise = moves(lambda z, c, f: ((z + 1) % self.deep, c, f))
        self.cross = {
            mask: moves(lambda z, c, f, mask=mask: (z, c, f ^ mask)) for mask in range(1, self.flat)
        }

    def place(self):
        outer_at = lax.axis_index("dp")
        self.z, self.c = outer_at // 2, outer_at % 2
        self.f = lax.axis_index("fsdp")

    def send(self, block, moves):
        return lax.ppermute(block, AXES, moves)

    def plane(self, step):
        return lax.rem(self.z + self.deep - step, self.deep)

    def bit(self, mask):
        return (self.f // mask) % 2


def at(array, index, axis):
    return lax.dynamic_index_in_dim(array, index, axis, keepdims=False)


def put(array, block, where):
    shape = []
    left = list(block.shape)
    for entry in where:
        shape.append(left.pop(0) if entry is None else 1)
    block = block.reshape(tuple(shape) + tuple(left))
    start = [0 if entry is None else entry for entry in where] + [0] * len(left)
    return lax.dynamic_update_slice(array, block, start)


def pair(mine, other, side, axis):
    return jnp.where(
        side == 0, jnp.stack([mine, other], axis=axis), jnp.stack([other, mine], axis=axis)
    )


def gather_plane(wires, block, rising, store):
    bits = wires.bits if rising else wires.bits[::-1]
    current = block
    for done, mask in enumerate(bits):
        arrived = wires.send(current, wires.cross[mask])
        side = wires.bit(mask)
        if done == len(bits) - 1:
            free = [None] * done
            for half, at_side in ((current, side), (arrived, 1 - side)):
                store(half, [at_side, *free] if rising else [*free, at_side])
        else:
            current = pair(current, arrived, side, 0 if rising else done)


def scatter_plane(wires, partial, rising):
    bits = list(wires.bits)
    order = bits if rising else bits[::-1]
    current, axes = partial, bits[::-1]
    for mask in order:
        axis = axes.index(mask)
        side = wires.bit(mask)
        leave = at(current, 1 - side, axis).astype(LOW)
        arrived = wires.send(leave, wires.cross[mask])
        current = at(current, side, axis).astype(WIDE) + arrived.astype(WIDE)
        axes.pop(axis)
    return current


def spread_rows(wires, block):
    parts = []
    for half, order in ((block[0], wires.bits), (block[1], wires.bits[::-1])):
        current = half[None]
        for mask in order:
            arrived = wires.send(current, wires.cross[mask])
            axis_new = jnp.stack([current, arrived], axis=1 if order is wires.bits else 0)
            current = (
                jnp.concatenate([current, arrived], axis=0)
                if order is wires.bits
                else axis_new.swapaxes(0, 1).reshape((-1,) + half.shape)
            )
        parts.append(current)
    own = jnp.stack(parts, axis=1)
    other = wires.send(own, wires.swap)
    return jnp.stack([own, other], axis=0)


def collect_rows(wires, partial):
    arrived = wires.send(partial[1].astype(LOW), wires.swap)
    both = partial[0] + arrived.astype(WIDE)
    halves = []
    for half, order in ((both[:, 0], wires.bits[::-1]), (both[:, 1], wires.bits)):
        shape = half.shape[1:]
        current = half.reshape((2,) * len(wires.bits) + shape)
        axes = wires.bits[::-1]
        for mask in order:
            axis = axes.index(mask)
            leave = lax.index_in_dim(current, 1, axis, keepdims=False).astype(LOW)
            arrived = wires.send(leave, wires.cross[mask])
            current = lax.index_in_dim(current, 0, axis, keepdims=False) + arrived.astype(WIDE)
            axes = [a for a in axes if a != mask]
        halves.append(current)
    return jnp.stack(halves, axis=0)


def gather_planes(wires, block):
    current = block
    for step in range(wires.deep):
        if step:
            current = wires.send(current, wires.rise)
        yield current, wires.plane(step)


def scatter_planes(wires, term):
    total = term(wires.plane(1)).astype(WIDE)
    for step in range(1, wires.deep):
        arrived = wires.send(total.astype(LOW), wires.rise)
        total = term(wires.plane(1 + step)).astype(WIDE) + arrived.astype(WIDE)
    return total


def on_device(
    wires,
    media,
    latents,
    upstream,
    time_index,
    live_count,
    time_table,
    media_gain,
    media_bias,
    latent_gain,
    latent_bias,
    ff_gain,
    ff_bias,
    w_query,
    w_keyval,
    w_out,
    w_up,
    w_down,
):
    wires.place()
    deep, flat, count = wires.deep, wires.flat, wires.count
    images, patches, model_width = media.shape
    lat_rows = latents.shape[1]
    key_rows = patches + lat_rows
    scale = 1.0 / math.sqrt(HEAD)
    table_rows, shard = time_table.shape
    group = model_width // (2 * deep)
    half_width = model_width // 2
    heads = half_width // HEAD
    bit_dims = (2,) * len(wires.bits)
    slots = 2 * images

    columns = jnp.concatenate([w_query, w_keyval], axis=1).reshape(shard, 3 * deep, 2, group)
    qkv_mine = at(columns, wires.c, 2).reshape(shard, 3 * half_width)
    qkv_other = at(columns, 1 - wires.c, 2).reshape(shard, 3 * half_width)
    qkv_arrived = wires.send(qkv_other, wires.swap)
    qkv_block = pair(qkv_mine, qkv_arrived, wires.c, 0)
    qkv_full = jnp.zeros((deep, 2) + bit_dims + (shard, 3 * half_width), LOW)
    box = [qkv_full]
    for block, plane in gather_planes(wires, qkv_block):
        for core in range(2):

            def store(half, where, core=core, plane=plane):
                box[0] = put(box[0], half, [plane, core, *where])

            gather_plane(wires, block[core], core == 0, store)
    qkv_full = box[0].reshape(model_width, 3 * half_width)
    query_full, keyval_full = qkv_full[:, :half_width], qkv_full[:, half_width:]

    smalls = jnp.concatenate(
        [time_table]
        + [
            v[None]
            for v in (media_gain, media_bias, latent_gain, latent_bias, ff_gain, ff_bias)
        ],
        axis=0,
    )
    smalls = jnp.broadcast_to(smalls[None], (count,) + smalls.shape)
    smalls = lax.all_to_all(smalls, AXES, 0, 0, tiled=True)
    smalls = smalls.transpose(1, 0, 2).reshape(-1, model_width).astype(WIDE)
    table_full = smalls[:table_rows]
    (
        media_gain_full,
        media_bias_full,
        latent_gain_full,
        latent_bias_full,
        ff_gain_full,
        ff_bias_full,
    ) = [smalls[table_rows + k] for k in range(6)]

    alive = (jnp.arange(images) < live_count[0]).astype(WIDE)
    live_mask = alive[:, None, None]
    one_hot = (time_index[:, None] == jnp.arange(table_rows)[None, :]).astype(WIDE)
    time_rows = jnp.dot(one_hot, table_full, precision=HIGHEST)
    media_in = media.astype(WIDE) + time_rows[:, None, :]
    media_normed, media_norm_back = jax.vjp(norm_rows, media_in, media_gain_full, media_bias_full)
    latents_wide = latents.astype(WIDE)
    latent_normed, latent_norm_back = jax.vjp(
        norm_rows, latents_wide, latent_gain_full, latent_bias_full
    )
    own_sources = jnp.concatenate([media_normed.astype(LOW), latent_normed.astype(LOW)], axis=1)
    sources = jnp.concatenate([own_sources, wires.send(own_sources, wires.swap)], axis=0)
    latent_norm = sources[:, patches:, :]

    down_full = jnp.zeros((deep,) + w_down.shape, LOW)
    for block, plane in gather_planes(wires, w_down):
        down_full = put(down_full, block, [plane])
    hidden_units = deep * w_down.shape[0]
    down_full = down_full.reshape(hidden_units, model_width)
    unit = w_down.shape[0]
    up_shards = w_up.reshape(shard, deep, 2, flat, unit)
    up_mine = at(up_shards, wires.c, 2)
    up_other = wires.send(at(up_shards, 1 - wires.c, 2), wires.swap)
    up_pair = pair(up_mine, up_other, wires.c, 0)
    up_block = jnp.zeros((2, flat, shard, hidden_units), LOW)
    for mask in range(flat):
        target = wires.f ^ mask
        part = at(up_pair, target, 3).reshape(2, shard, hidden_units)
        if mask:
            part = wires.send(part, wires.cross[mask])
        up_block = put(up_block, part, [None, target])
    up_full = jnp.zeros((deep, 2 * flat * shard, hidden_units), LOW)
    up_block = up_block.reshape(2 * flat * shard, hidden_units)
    for block, plane in gather_planes(wires, up_block):
        up_full = put(up_full, block, [plane])
    up_full = up_full.reshape(model_width, hidden_units)

    out_full = jnp.zeros((deep,) + bit_dims + (shard, model_width), LOW)
    out_column = jnp.zeros((deep, shard, model_width), LOW)
    for block, plane in gather_planes(wires, w_out):
        out_column = put(out_column, block, [plane])
    out_box = [jnp.zeros(bit_dims + (deep, 2, shard, half_width), LOW)]
    for side in range(2):

        def store_out(half, where, side=side):
            out_box[0] = put(out_box[0], half, [*where, None, side])

        gather_plane(
            wires, out_column[:, :, side * half_width : (side + 1) * half_width], side == 0, store_out
        )
    out_full = (
        out_box[0]
        .reshape(flat, deep, 2, shard, half_width)
        .transpose(1, 0, 3, 2, 4)
        .reshape(half_width, model_width)
    )

    query_rows = rows_by(latent_norm, query_full).astype(LOW)
    keyval = rows_by(sources, keyval_full).astype(LOW)
    key_heads = keyval[:, :, :half_width].reshape(slots, key_rows, heads, HEAD)
    value_heads = keyval[:, :, half_width:].reshape(slots, key_rows, heads, HEAD)
    query_heads = query_rows.reshape(slots, lat_rows, heads, HEAD)
    raw = jnp.einsum("cqhe,ckhe->ckhq", query_heads, key_heads, preferred_element_type=WIDE)
    scores = (raw * scale).reshape(slots, key_rows, heads * lat_rows)
    row_top = jnp.max(scores, axis=1, keepdims=True)
    exps = jnp.exp(scores - row_top)
    attention = exps / jnp.sum(exps, axis=1, keepdims=True)
    attention_low = attention.reshape(slots, key_rows, heads, lat_rows).astype(LOW)
    mixed = jnp.einsum("ckhq,ckhe->cqhe", attention_low, value_heads, preferred_element_type=WIDE)
    mixed = mixed.reshape(slots, lat_rows, half_width).astype(LOW)
    branch = rows_by(mixed, out_full)
    branch = branch[:images] + wires.send(branch[images:], wires.swap)
    middle = latents_wide + branch

    ffn_normed, ffn_norm_back = jax.vjp(norm_rows, middle, ff_gain_full, ff_bias_full)
    d_out = upstream.astype(WIDE) * live_mask
    plane_shape = (2, flat, images, lat_rows, model_width)
    d_out_rows = spread_rows(wires, d_out.astype(LOW)).reshape(-1, model_width)
    ffn_rows = spread_rows(wires, ffn_normed.astype(LOW)).reshape(-1, model_width)
    pre_act = rows_by(ffn_rows, up_full)
    activated, gelu_back = jax.vjp(exact_gelu, pre_act)
    hidden = activated.astype(LOW)
    d_hidden = rows_back(d_out_rows, down_full)
    (d_pre,) = gelu_back(d_hidden)
    d_pre_low = d_pre.astype(LOW)
    d_ffn_input = collect_rows(wires, rows_back(d_pre_low, up_full).reshape(plane_shape))
    d_middle_norm, ff_gain_grad, ff_bias_grad = ffn_norm_back(d_ffn_input)
    d_middle = d_out + d_middle_norm
    result = middle + collect_rows(wires, rows_by(hidden, down_full).reshape(plane_shape))
    latents_out = (result * live_mask).astype(LOW)

    down_partial = outer(hidden, d_out_rows).astype(LOW).reshape(deep, unit, model_width)
    w_down_grad = scatter_planes(wires, lambda plane: at(down_partial, plane, 0))
    up_partial = outer(ffn_rows, d_pre_low).astype(LOW)
    up_partial = up_partial.reshape(deep, 2, flat, shard, hidden_units)
    up_sum = scatter_planes(wires, lambda plane: at(up_partial, plane, 0)).astype(LOW)
    up_grad = jnp.zeros((2, shard, deep, flat, unit), LOW)
    for mask in range(flat):
        target = wires.f ^ mask
        part = at(up_sum, target, 1).reshape(2, shard, deep, unit)
        if mask:
            part = wires.send(part, wires.cross[mask])
        up_grad = put(up_grad, part, [None, None, None, target])
    up_mine = at(up_grad, wires.c, 0)
    up_other = wires.send(at(up_grad, 1 - wires.c, 0), wires.swap)
    w_up_grad = pair(up_mine, up_other, wires.c, 2).reshape(w_up.shape).astype(WIDE)

    own_branch = d_middle.astype(LOW)
    d_branch = jnp.concatenate([own_branch, wires.send(own_branch, wires.swap)], axis=0)
    d_mixed = rows_back(d_branch, out_full).astype(LOW)
    out_partial = outer(mixed.reshape(-1, half_width), d_branch.reshape(-1, model_width))
    out_partial = out_partial.astype(LOW).reshape((deep,) + bit_dims + (shard, model_width))
    d_mixed_heads = d_mixed.reshape(slots, lat_rows, heads, HEAD)
    d_attention = jnp.einsum(
        "cqhe,ckhe->ckhq", d_mixed_heads, value_heads, preferred_element_type=WIDE
    )
    d_attention = d_attention.reshape(slots, key_rows, heads * lat_rows)
    d_values = jnp.einsum(
        "ckhq,cqhe->ckhe", attention_low, d_mixed_heads, preferred_element_type=WIDE
    )
    row_delta = jnp.sum(attention * d_attention, axis=1, keepdims=True)
    d_scores = (attention * (d_attention - row_delta)).reshape(slots, key_rows, heads, lat_rows)
    d_scores = d_scores.astype(LOW)
    d_query = jnp.einsum("ckhq,ckhe->cqhe", d_scores, key_heads, preferred_element_type=WIDE)
    d_query = (d_query * scale).reshape(slots, lat_rows, half_width).astype(LOW)
    d_keys = jnp.einsum("ckhq,cqhe->ckhe", d_scores, query_heads, preferred_element_type=WIDE)
    d_keyval = jnp.concatenate(
        [
            (d_keys * scale).reshape(slots, key_rows, half_width),
            d_values.reshape(slots, key_rows, half_width),
        ],
        axis=2,
    ).astype(LOW)

    query_partial = outer(latent_norm.reshape(-1, model_width), d_query.reshape(-1, half_width))
    keyval_partial = outer(sources.reshape(-1, model_width), d_keyval.reshape(-1, model_width))
    qkv_partial = jnp.concatenate([query_partial.astype(LOW), keyval_partial.astype(LOW)], axis=1)
    qkv_partial = qkv_partial.reshape((deep, 2) + bit_dims + (shard, 3 * half_width))

    def qkv_term(plane):
        block = at(qkv_partial, plane, 0)
        return jnp.stack([scatter_plane(wires, block[core], core == 0) for core in range(2)])

    qkv_sum = scatter_planes(wires, qkv_term)
    qkv_own = at(qkv_sum, wires.c, 0)
    qkv_far = wires.send(at(qkv_sum, 1 - wires.c, 0), wires.swap)
    halves = [part.reshape(shard, 3 * deep, group) for part in (qkv_own, qkv_far)]
    qkv_grad = pair(halves[0], halves[1], wires.c, 2).reshape(shard, 3 * model_width)
    w_query_grad, w_keyval_grad = qkv_grad[:, :model_width], qkv_grad[:, model_width:]

    def out_term(side):
        return scatter_plane(
            wires,
            jnp.moveaxis(out_partial, 0, len(bit_dims))[
                ..., side * half_width : (side + 1) * half_width
            ],
            side == 0,
        )

    out_sums = jnp.concatenate([out_term(side) for side in range(2)], axis=-1)
    w_out_grad = scatter_planes(wires, lambda plane: at(out_sums, plane, 0))

    d_sources = rows_back(d_keyval, keyval_full)
    d_latent_part = rows_back(d_query, query_full) + d_sources[:, patches:, :]
    d_sources = jnp.concatenate([d_sources[:, :patches, :], d_latent_part], axis=1)
    d_sources = d_sources[:images] + wires.send(d_sources[images:], wires.swap)
    d_latent_in, latent_gain_grad, latent_bias_grad = latent_norm_back(d_sources[:, patches:, :])
    media_grad, media_gain_grad, media_bias_grad = media_norm_back(d_sources[:, :patches, :])
    latent_grad = d_middle + d_latent_in
    table_part = jnp.dot(one_hot.T, jnp.sum(media_grad, axis=1), precision=HIGHEST)

    small_grads = jnp.concatenate(
        [table_part]
        + [
            v[None]
            for v in (
                media_gain_grad,
                media_bias_grad,
                latent_gain_grad,
                latent_bias_grad,
                ff_gain_grad,
                ff_bias_grad,
            )
        ],
        axis=0,
    )
    small_grads = small_grads.reshape(-1, count, shard).transpose(1, 0, 2)
    small_grads = lax.all_to_all(small_grads, AXES, 0, 0, tiled=True)
    small_grads = jnp.sum(small_grads, axis=0)
    return (
        latents_out,
        media_grad,
        latent_grad,
        small_grads[:table_rows],
        *[small_grads[table_rows + k] for k in range(6)],
        w_query_grad,
        w_keyval_grad,
        w_out_grad,
        w_up_grad,
        w_down_grad,
    )


def solution(mesh):
    lead = P(AXES)
    table = P(None, AXES)
    return jax.shard_map(
        functools.partial(on_device, Wires(mesh)),
        mesh=mesh,
        in_specs=(lead,) * 5 + (table,) + (lead,) * 11,
        out_specs=(lead,) * 3 + (table,) + (lead,) * 11,
        check_vma=False,
    )
```

time: 1870 us -> 733 us (0.39)
  waiting for transfers between devices: 1470 us -> 330 us
  blocking collectives: 149 us -> 0 us
  local copies, waits for them, and re-layouts: 42.4 us -> 152 us
  matrix products: 167 us -> 84.4 us
  starting transfers between devices: 0.44 us -> 82.1 us
  other arithmetic: 21.7 us -> 70.1 us
    reduce_scatter x5 -> x0, waiting for transfers between devices: 1170 us -> none  [the longest x1 356 us: on_device(): lax.psum_scatter(down_grad, ('dp', 'fsdp'), scatter_dimension=0, tiled=True)]
    ppermute x0 -> x98, waiting for transfers between devices: none -> 325 us  [send(): return lax.ppermute(block, AXES, moves)]
    all_gather x5 -> x0, waiting for transfers between devices: 293 us -> none  [the longest x1 121 us: on_device(): lax.all_gather(w_up, ('dp', 'fsdp'), axis=0, tiled=True)]
    dot_general x17 -> x18, matrix products: 157 us -> 70.5 us  [the longest x15 69.4 us: dot(): lax.dot_general(left, right, (contract, ((), ())), preferred_element_type...]
    unnamed x2 -> x0, blocking collectives: 82.3 us -> none
    ppermute x0 -> x98, starting transfers between devices: none -> 72.4 us  [send(): return lax.ppermute(block, AXES, moves)]
    all_gather x1 -> x0, blocking collectives: 66.8 us -> none  [on_device(): lax.all_gather(time_table, ('dp', 'fsdp'), axis=1, tiled=True)]
    dynamic_update_slice x0 -> x30, local copies, waits for them, and re-layouts: none -> 22.9 us  [put(): return lax.dynamic_update_slice(array, block, start)]
  transfers between devices with their start and end apart: 11 -> 100, of which waited for: 9 -> 56; matrix products, arithmetic and copies ran while one was open for 8% -> 27% of each run, Pallas kernels for 0% -> 0%
where the time goes in v1:
time: 733 us; the launch traced here: 723 us
  waiting for transfers between devices  330 us (45%)
  local copies, waits for them, and re-layouts  152 us (21%)
  matrix products  84.4 us (12%)
  starting transfers between devices  82.1 us (11%)
  other arithmetic  70.1 us (10%)
    ppermute x98, waiting for transfers between devices, send(): return lax.ppermute(block, AXES, moves)  325 us
    ppermute x98, starting transfers between devices, send(): return lax.ppermute(block, AXES, moves)  72.4 us
    dot_general x15, matrix products, dot(): lax.dot_general(left, right, (contract, ((), ())), preferred_element_type...  69.4 us
    dynamic_update_slice x30, local copies, waits for them, and re-layouts, put(): return lax.dynamic_update_slice(array, block, start)  22.9 us
  transfers between devices with their start and end apart: 100, of which 56 were waited for; matrix products, arithmetic and copies ran while one was open for 27% of the time, Pallas kernels for 0%

profile of v1, /device:TPU:0, one launch (start us, length us, event | category | flops | bytes accessed | tf_op | source)
XLA Modules:
  0.0 722.6 jit_solution(15282517896423499529)
XLA Ops:
  8.5 7.1 all-to-all-start
  79.0 5.6 collective-permute-done.23
  89.9 4.4 collective-permute-done.36
  107.0 6.1 collective-permute-done.26
  117.3 4.1 collective-permute-done.5
  123.9 5.7 collective-permute-done.9
  138.1 3.9 collective-permute-done.12
  143.4 6.9 collective-permute-done.14
  154.0 8.3 %collective-permute-done.25 = bf16[2,4,48,768]{3,2,1,0:T(8,128)(2,1)S(1)} collective-permute-done((bf16[2,4,48,768]{3,2,1,0:T(8,128)(2,1)S(1)}, bf16[2,4,48,768]{3,2,1,0:T(8,128)(2,1)S(1)}, u32[]{:S(2)}, u32[]{:S(2)}) %collective-permute-start.25) | collective-permute-done | bytes 589856 | tf_op jit(solution)/shard_map/ppermute | solution.py:72
  164.1 11.1 %collective-permute-done.10 = bf16[2,48,2304]{2,1,0:T(8,128)(2,1)S(1)} collective-permute-done((bf16[2,48,2304]{2,1,0:T(8,128)(2,1)S(1)}, bf16[2,48,2304]{2,1,0:T(8,128)(2,1)S(1)}, u32[]{:S(2)}, u32[]{:S(2)}) %collective-permute-start.10) | collective-permute-done | bytes 442400 | tf_op jit(solution)/shard_map/ppermute | solution.py:72
  176.8 8.3 %collective-permute-done.27 = bf16[2,4,48,768]{3,2,1,0:T(8,128)(2,1)S(1)} collective-permute-done((bf16[2,4,48,768]{3,2,1,0:T(8,128)(2,1)S(1)}, bf16[2,4,48,768]{3,2,1,0:T(8,128)(2,1)S(1)}, u32[]{:S(2)}, u32[]{:S(2)}) %collective-permute-start.27) | collective-permute-done | bytes 589856 | tf_op jit(solution)/shard_map/ppermute | solution.py:72
  188.7 6.3 reshape.1195
  197.8 8.3 %collective-permute-done.13 = bf16[2,48,2304]{2,1,0:T(8,128)(2,1)S(1)} collective-permute-done((bf16[2,48,2304]{2,1,0:T(8,128)(2,1)}, bf16[2,48,2304]{2,1,0:T(8,128)(2,1)S(1)}, u32[]{:S(2)}, u32[]{:S(2)}) %collective-permute-start.13) | collective-permute-done | bytes 442400 | tf_op jit(solution)/shard_map/ppermute | solution.py:72
  207.5 6.9 collective-permute-done.17
  215.5 6.5 collective-permute-done.19
  223.2 9.8 %collective-permute-done.15 = bf16[2,48,2304]{2,1,0:T(8,128)(2,1)S(1)} collective-permute-done((bf16[2,48,2304]{2,1,0:T(8,128)(2,1)S(1)}, bf16[2,48,2304]{2,1,0:T(8,128)(2,1)S(1)}, u32[]{:S(2)}, u32[]{:S(2)}) %collective-permute-start.15) | collective-permute-done | bytes 442400 | tf_op jit(solution)/shard_map/ppermute | solution.py:72
  243.0 6.6 collective-permute-done.20
  254.2 9.4 %convolution_convert_fusion = bf16[4,320,1536]{2,1,0:T(8,128)(2,1)S(1)} fusion(bf16[1536,2304]{1,0:T(8,128)(2,1)} %bitcast.52, bf16[2,320,1536]{2,1,0:T(8,128)(2,1)} %collective-permute-done, bf16[2,64,1536]{2,1,0:T(8,128)(2,1)S(1)} %fusion.44, bf16[2,256,1536]{2,1,0:T(8,128)(2,1)S(1)} %add_convert_fusion.1), kind=kOutput, calls=%fused_computation.11 | convolution fusion | flops 6053560320 | bytes 12582912 | tf_op jit(solution)/shard_map/dot_general | solution.py:29
  271.8 4.1 copy.209
  298.0 5.3 collective-permute-done.29
  312.5 8.9 %collective-permute-done.39 = bf16[384,768]{1,0:T(8,128)(2,1)S(1)} collective-permute-done((bf16[384,768]{1,0:T(8,128)(2,1)}, bf16[384,768]{1,0:T(8,128)(2,1)S(1)}, u32[]{:S(2)}, u32[]{:S(2)}) %collective-permute-start.39) | collective-permute-done | bytes 589856 | tf_op jit(solution)/shard_map/ppermute | solution.py:72
  321.7 12.4 %collective-permute-done.43 = bf16[192,1536]{1,0:T(8,128)(2,1)S(1)} collective-permute-done((bf16[192,1536]{1,0:T(8,128)(2,1)S(1)}, bf16[192,1536]{1,0:T(8,128)(2,1)S(1)}, u32[]{:S(2)}, u32[]{:S(2)}) %collective-permute-start.43) | collective-permute-done | bytes 589856 | tf_op jit(solution)/shard_map/ppermute | solution.py:72
  335.5 10.6 %collective-permute-done.40 = bf16[384,768]{1,0:T(8,128)(2,1)S(1)} collective-permute-done((bf16[384,768]{1,0:T(8,128)(2,1)S(1)}, bf16[384,768]{1,0:T(8,128)(2,1)S(1)}, u32[]{:S(2)}, u32[]{:S(2)}) %collective-permute-start.40) | collective-permute-done | bytes 589856 | tf_op jit(solution)/shard_map/ppermute | solution.py:72
  349.4 10.7 %add_convert_fusion = (bf16[1024,768]{1,0:T(8,128)(2,1)S(1)}, f32[1024,768]{1,0:T(8,128)S(1)}) fusion(f32[1024,768]{1,0:T(8,128)S(1)} %fusion.165, bf16[1024,1536]{1,0:T(8,128)(2,1)S(1)} %bitcast.623, bf16[768,1536]{1,0:T(8,128)(2,1)} %bitcast.110), kind=kOutput, calls=%fused_computation.38 | convolution fusion | flops 2472542208 | bytes 13369344 | tf_op jit(solution)/shard_map/dot_general | solution.py:29
  367.2 4.3 fusion.166
  371.9 9.7 %collective-permute-done.95 = bf16[192,1536]{1,0:T(8,128)(2,1)S(1)} collective-permute-done((bf16[192,1536]{1,0:T(8,128)(2,1)S(1)}, bf16[192,1536]{1,0:T(8,128)(2,1)S(1)}, u32[]{:S(2)}, u32[]{:S(2)}) %collective-permute-start.95) | collective-permute-done | bytes 589856 | tf_op jit(solution)/shard_map/ppermute | solution.py:72
  381.9 12.4 %collective-permute-done.88 = bf16[2,4,48,768]{3,2,0,1:T(8,128)(2,1)S(1)} collective-permute-done((bf16[2,4,48,768]{3,2,0,1:T(8,128)(2,1)S(1)}, bf16[2,4,48,768]{3,2,0,1:T(8,128)(2,1)S(1)}, u32[]{:S(2)}, u32[]{:S(2)}) %collective-permute-start.88) | collective-permute-done | bytes 589856 | tf_op jit(solution)/shard_map/ppermute | solution.py:72
  400.4 6.5 collective-permute-done.96
  407.9 11.7 %collective-permute-done.89 = bf16[2,4,48,768]{3,2,0,1:T(8,128)(2,1)S(1)} collective-permute-done((bf16[2,4,48,768]{3,2,0,1:T(8,128)(2,1)S(1)}, bf16[2,4,48,768]{3,2,0,1:T(8,128)(2,1)S(1)}, u32[]{:S(2)}, u32[]{:S(2)}) %collective-permute-start.89) | collective-permute-done | bytes 589856 | tf_op jit(solution)/shard_map/ppermute | solution.py:72
  429.5 13.9 %collective-permute-done.90 = bf16[2,4,48,768]{3,2,0,1:T(8,128)(2,1)S(1)} collective-permute-done((bf16[2,4,48,768]{3,2,0,1:T(8,128)(2,1)S(1)}, bf16[2,4,48,768]{3,2,0,1:T(8,128)(2,1)S(1)}, u32[]{:S(2)}, u32[]{:S(2)}) %collective-permute-start.90) | collective-permute-done | bytes 589856 | tf_op jit(solution)/shard_map/ppermute | solution.py:72
  459.6 7.7 %collective-permute-done.93 = bf16[2,48,4,192]{3,2,1,0:T(4,128)(2,1)S(1)} collective-permute-done((bf16[2,48,4,192]{3,2,1,0:T(4,128)(2,1)}, bf16[2,48,4,192]{3,2,1,0:T(4,128)(2,1)S(1)}, u32[]{:S(2)}, u32[]{:S(2)}) %collective-permute-start.93) | collective-permute-done | bytes 147488 | tf_op jit(solution)/shard_map/ppermute | solution.py:72
  473.2 4.5 collective-permute-done.57
  523.3 4.3 copy.240
  532.5 10.4 %fusion.3 = f32[4,320,1536]{2,1,0:T(8,128)} fusion(bf16[1536,2304]{1,0:T(8,128)(2,1)} %bitcast.52, bf16[4,320,768]{2,1,0:T(8,128)(2,1)S(1)} %copy-done.34, bf16[4,320,768]{2,1,0:T(8,128)(2,1)S(1)} %copy-done.33), kind=kOutput, calls=%fused_computation.17 | convolution fusion | flops 6047662080 | bytes 16515072 | tf_op jit(solution)/shard_map/dot_general | solution.py:29
  542.9 8.2 %bitcast_convert_fusion = bf16[1536,1536]{0,1:T(8,128)(2,1)S(1)} fusion(bf16[4,320,768]{2,1,0:T(8,128)(2,1)S(1)} %copy-done.34, bf16[4,320,768]{2,1,0:T(8,128)(2,1)S(1)} %copy-done.33, bf16[2,320,1536]{2,1,0:T(8,128)(2,1)} %collective-permute-done, bf16[2,64,1536]{2,1,0:T(8,128)(2,1)S(1)} %copy-done.29, bf16[2,256,1536]{2,1,0:T(8,128)(2,1)S(1)} %copy-done.7), kind=kOutput, calls=%fused_computation.1 | convolution fusion | flops 6061817856 | bytes 12582912 | tf_op jit(solution)/shard_map/dot_general | solution.py:29
  554.4 10.1 %copy.243 = bf16[1536,2304]{1,0:T(8,128)(2,1)} copy(bf16[1536,2304]{0,1:T(8,128)(2,1)} %pad_maximum_fusion) | data formatting | bytes 14155776 | tf_op jit(solution)/shard_map/concatenate | solution.py:388
  575.4 5.1 fusion.23
  582.3 7.8 %collective-permute-done.67 = bf16[2,48,2304]{2,1,0:T(8,128)(2,1)S(1)} collective-permute-done((bf16[2,48,2304]{2,1,0:T(8,128)(2,1)S(1)}, bf16[2,48,2304]{2,1,0:T(8,128)(2,1)S(1)}, u32[]{:S(2)}, u32[]{:S(2)}) %collective-permute-start.67) | collective-permute-done | bytes 442400 | tf_op jit(solution)/shard_map/ppermute | solution.py:72
  590.4 9.2 %collective-permute-done.71 = bf16[2,48,2304]{2,1,0:T(8,128)(2,1)S(1)} collective-permute-done((bf16[2,48,2304]{2,1,0:T(8,128)(2,1)S(1)}, bf16[2,48,2304]{2,1,0:T(8,128)(2,1)S(1)}, u32[]{:S(2)}, u32[]{:S(2)}) %collective-permute-start.71) | collective-permute-done | bytes 442400 | tf_op jit(solution)/shard_map/ppermute | solution.py:72
  602.2 6.4 collective-permute-done.75
  615.5 9.4 %collective-permute-done.83 = bf16[2,4,48,768]{3,2,1,0:T(8,128)(2,1)S(1)} collective-permute-done((bf16[2,4,48,768]{3,2,1,0:T(8,128)(2,1)S(1)}, bf16[2,4,48,768]{3,2,1,0:T(8,128)(2,1)S(1)}, u32[]{:S(2)}, u32[]{:S(2)}) %collective-permute-start.83) | collective-permute-done | bytes 589856 | tf_op jit(solution)/shard_map/ppermute | solution.py:72
  626.8 6.2 collective-permute-done.70
  634.7 4.5 collective-permute-done.66
  651.9 9.9 %collective-permute-done.77 = bf16[2,48,2304]{2,1,0:T(8,128)(2,1)S(1)} collective-permute-done((bf16[2,48,2304]{2,1,0:T(8,128)(2,1)S(1)}, bf16[2,48,2304]{2,1,0:T(8,128)(2,1)S(1)}, u32[]{:S(2)}, u32[]{:S(2)}) %collective-permute-start.77) | collective-permute-done | bytes 442400 | tf_op jit(solution)/shard_map/ppermute | solution.py:72
  665.1 9.3 %collective-permute-done.78 = bf16[2,48,2304]{2,1,0:T(8,128)(2,1)S(1)} collective-permute-done((bf16[2,48,2304]{2,1,0:T(8,128)(2,1)S(1)}, bf16[2,48,2304]{2,1,0:T(8,128)(2,1)S(1)}, u32[]{:S(2)}, u32[]{:S(2)}) %collective-permute-start.78) | collective-permute-done | bytes 442400 | tf_op jit(solution)/shard_map/ppermute | solution.py:72
  677.9 6.8 collective-permute-done.79
  695.7 4.0 fusion.2
  714.0 5.5 all-to-all-done.1
  (634 shorter events, 353.2 us)
Async XLA Ops:
  7.2 48.1 %collective-permute-start.1 = (bf16[48,2304]{1,0:T(8,128)(2,1)}, bf16[48,2304]{1,0:T(8,128)(2,1)}, u32[]{:S(2)}, u32[]{:S(2)}) collective-permute-start(bf16[48,2304]{1,0:T(8,128)(2,1)} %reshape.1123), channel_id=1, source_target_pairs={{0,4},{1,5},{2,6},{3,7},{4,0},{5,1},{6,2},{7,3},{8,12},{9,13},{10,... | collective-permute-start | bytes 663560 | tf_op jit(solution)/shard_map/ppermute | solution.py:72
  8.5 23.1 %all-to-all-start = ((bf16[32,2,336]{2,1,0:T(2,128)(2,1)}), bf16[32,2,336]{2,1,0:T(2,128)(2,1)}, u32[]{:S(2)}, u32[]{:S(2)}) async-start(bf16[32,2,336]{2,1,0:T(2,128)(2,1)} %reshape.1236), calls=%async_computation | async-start | bytes 98304 | tf_op jit(solution)/shard_map/all_to_all | solution.py:240
  15.6 28.1 %collective-permute-start.21 = (bf16[48,1536]{1,0:T(8,128)(2,1)}, bf16[48,1536]{1,0:T(8,128)(2,1)}, u32[]{:S(2)}, u32[]{:S(2)}) collective-permute-start(bf16[48,1536]{1,0:T(8,128)(2,1)} %param.31), channel_id=1, source_target_pairs={{0,8},{1,9},{2,10},{3,11},{4,12},{5,13},{6,14},{7,15},{8,16},{9,17... | collective-permute-start | bytes 442376 | tf_op jit(solution)/shard_map/ppermute | solution.py:72
  19.6 40.2 %collective-permute-start.34 = (bf16[48,4,4,192]{3,1,0,2:T(4,128)(2,1)}, bf16[48,4,4,192]{3,1,0,2:T(4,128)(2,1)}, u32[]{:S(2)}, u32[]{:S(2)}) collective-permute-start(bf16[48,4,4,192]{3,1,0,2:T(4,128)(2,1)} %bitcast.600), channel_id=1, source_target_pairs={{0,4},{1,5},{2,6},{3,7},{4,0},{5,1},{6,2},{7,3},{8,12},{9,13},{10,... | collective-permute-start | bytes 884744 | tf_op jit(solution)/shard_map/ppermute | solution.py:72
  19.6 268.8 %collective-permute-start.41 = (bf16[192,1536]{1,0:T(8,128)(2,1)}, bf16[192,1536]{1,0:T(8,128)(2,1)}, u32[]{:S(2)}, u32[]{:S(2)}) collective-permute-start(bf16[192,1536]{1,0:T(8,128)(2,1)} %param.33), channel_id=1, source_target_pairs={{0,8},{1,9},{2,10},{3,11},{4,12},{5,13},{6,14},{7,15},{8,16},{9,17... | collective-permute-start | bytes 1769480 | tf_op jit(solution)/shard_map/ppermute | solution.py:72
  22.7 28.7 %collective-permute-start.49 = (bf16[1,64,1536]{2,1,0:T(8,128)(2,1)}, bf16[1,64,1536]{2,1,0:T(8,128)(2,1)}, u32[]{:S(2)}, u32[]{:S(2)}) collective-permute-start(bf16[1,64,1536]{2,1,0:T(8,128)(2,1)} %get-tuple-element.121), channel_id=1, source_target_pairs={{0,1},{1,0},{2,3},{3,2},{4,5},{5,4},{6,7},{7,6},{8,9},{9,8},{10,11... | collective-permute-start | bytes 589832 | tf_op jit(solution)/shard_map/ppermute | solution.py:72
  50.5 185.7 %collective-permute-start = (bf16[2,320,1536]{2,1,0:T(8,128)(2,1)}, bf16[2,320,1536]{2,1,0:T(8,128)(2,1)}, u32[]{:S(2)}, u32[]{:S(2)}) collective-permute-start(bf16[2,320,1536]{2,1,0:T(8,128)(2,1)} %pad_maximum_fusion.8), channel_id=1, source_target_pairs={{0,4},{1,5},{2,6},{3,7},{4,0},{5,1},{6,2},{7,3},{8,12},{9,13},{10,... | collective-permute-start | bytes 5898248 | tf_op jit(solution)/shard_map/ppermute | solution.py:72
  51.5 18.3 %collective-permute-start.22 = (bf16[48,1536]{1,0:T(8,128)(2,1)}, bf16[48,1536]{1,0:T(8,128)(2,1)}, u32[]{:S(2)}, u32[]{:S(2)}) collective-permute-start(bf16[48,1536]{1,0:T(8,128)(2,1)} %collective-permute-done.21), channel_id=1, source_target_pairs={{0,8},{1,9},{2,10},{3,11},{4,12},{5,13},{6,14},{7,15},{8,16},{9,17... | collective-permute-start | bytes 442376 | tf_op jit(solution)/shard_map/ppermute | solution.py:72
  59.3 44.4 %collective-permute-start.6 = (bf16[2,48,2304]{2,1,0:T(8,128)(2,1)}, bf16[2,48,2304]{2,1,0:T(8,128)(2,1)}, u32[]{:S(2)}, u32[]{:S(2)}) collective-permute-start(bf16[2,48,2304]{2,1,0:T(8,128)(2,1)} %maximum_select_fusion.7), channel_id=1, source_target_pairs={{0,8},{1,9},{2,10},{3,11},{4,12},{5,13},{6,14},{7,15},{8,16},{9,17... | collective-permute-start | bytes 1327112 | tf_op jit(solution)/shard_map/ppermute | solution.py:72
  59.8 14.8 %collective-permute-start.2 = (bf16[48,2304]{1,0:T(8,128)(2,1)}, bf16[48,2304]{1,0:T(8,128)(2,1)}, u32[]{:S(2)}, u32[]{:S(2)}) collective-permute-start(bf16[48,2304]{1,0:T(8,128)(2,1)} %get-tuple-element.112), channel_id=1, source_target_pairs={{0,1},{1,0},{2,3},{3,2},{4,5},{5,4},{6,7},{7,6},{8,9},{9,8},{10,11... | collective-permute-start | bytes 663560 | tf_op jit(solution)/shard_map/ppermute | solution.py:72
  74.6 13.1 %collective-permute-start.35 = (bf16[2,48,768]{2,1,0:T(8,128)(2,1)}, bf16[2,48,768]{2,1,0:T(8,128)(2,1)S(1)}, u32[]{:S(2)}, u32[]{:S(2)}) collective-permute-start(bf16[2,48,768]{2,1,0:T(8,128)(2,1)} %reshape.1146), channel_id=1, source_target_pairs={{0,1},{1,0},{2,3},{3,2},{4,5},{5,4},{6,7},{7,6},{8,9},{9,8},{10,11... | collective-permute-start | bytes 442376 | tf_op jit(solution)/shard_map/ppermute | solution.py:72
  94.3 20.5 %collective-permute-start.3 = (bf16[2,48,2304]{2,1,0:T(8,128)(2,1)S(1)}, bf16[2,48,2304]{2,1,0:T(8,128)(2,1)S(1)}, u32[]{:S(2)}, u32[]{:S(2)}) collective-permute-start(bf16[2,48,2304]{2,1,0:T(8,128)(2,1)S(1)} %maximum_select_fusion.9), channel_id=1, source_target_pairs={{0,2},{1,3},{2,0},{3,1},{4,6},{5,7},{6,4},{7,5},{8,10},{9,11},{10,... | collective-permute-start | bytes 1327112 | tf_op jit(solution)/shard_map/ppermute | solution.py:72
  104.8 181.5 %collective-permute-start.50 = (bf16[2,64,1536]{2,1,0:T(8,128)(2,1)}, bf16[2,64,1536]{2,1,0:T(8,128)(2,1)}, u32[]{:S(2)}, u32[]{:S(2)}) collective-permute-start(bf16[2,64,1536]{2,1,0:T(8,128)(2,1)} %pad_maximum_fusion.22), channel_id=1, source_target_pairs={{0,2},{1,3},{2,0},{3,1},{4,6},{5,7},{6,4},{7,5},{8,10},{9,11},{10,... | collective-permute-start | bytes 1179656 | tf_op jit(solution)/shard_map/ppermute | solution.py:72
  129.5 22.9 %collective-permute-start.8 = (bf16[2,48,2304]{2,1,0:T(8,128)(2,1)S(1)}, bf16[2,48,2304]{2,1,0:T(8,128)(2,1)S(1)}, u32[]{:S(2)}, u32[]{:S(2)}) collective-permute-start(bf16[2,48,2304]{2,1,0:T(8,128)(2,1)S(1)} %maximum_select_fusion.13), channel_id=1, source_target_pairs={{0,2},{1,3},{2,0},{3,1},{4,6},{5,7},{6,4},{7,5},{8,10},{9,11},{10,... | collective-permute-start | bytes 1327112 | tf_op jit(solution)/shard_map/ppermute | solution.py:72
  150.3 134.9 %collective-permute-start.52 = (bf16[2,64,1536]{2,1,0:T(8,128)(2,1)}, bf16[2,64,1536]{2,1,0:T(8,128)(2,1)}, u32[]{:S(2)}, u32[]{:S(2)}) collective-permute-start(bf16[2,64,1536]{2,1,0:T(8,128)(2,1)} %get-tuple-element.125), channel_id=1, source_target_pairs={{0,1},{1,0},{2,3},{3,2},{4,5},{5,4},{6,7},{7,6},{8,9},{9,8},{10,11... | collective-permute-start | bytes 1179656 | tf_op jit(solution)/shard_map/ppermute | solution.py:72
  236.3 57.3 %collective-permute-start.38 = (bf16[384,768]{1,0:T(8,128)(2,1)}, bf16[384,768]{1,0:T(8,128)(2,1)}, u32[]{:S(2)}, u32[]{:S(2)}) collective-permute-start(bf16[384,768]{1,0:T(8,128)(2,1)} %bitcast.101), channel_id=1, source_target_pairs={{0,8},{1,9},{2,10},{3,11},{4,12},{5,13},{6,14},{7,15},{8,16},{9,17... | collective-permute-start | bytes 1769480 | tf_op jit(solution)/shard_map/ppermute | solution.py:72
  287.8 47.1 %collective-permute-start.53 = (bf16[4,2,64,1536]{3,2,0,1:T(8,128)(2,1)S(1)}, bf16[4,2,64,1536]{3,2,0,1:T(8,128)(2,1)S(1)}, u32[]{:S(2)}, u32[]{:S(2)}) collective-permute-start(bf16[4,2,64,1536]{3,2,0,1:T(8,128)(2,1)S(1)} %get-tuple-element.66), channel_id=1, source_target_pairs={{0,4},{1,5},{2,6},{3,7},{4,0},{5,1},{6,2},{7,3},{8,12},{9,13},{10,... | collective-permute-start | bytes 4718600 | tf_op jit(solution)/shard_map/ppermute | solution.py:72
  288.4 20.4 %collective-permute-start.42 = (bf16[192,1536]{1,0:T(8,128)(2,1)}, bf16[192,1536]{1,0:T(8,128)(2,1)S(1)}, u32[]{:S(2)}, u32[]{:S(2)}) collective-permute-start(bf16[192,1536]{1,0:T(8,128)(2,1)} %collective-permute-done.41), channel_id=1, source_target_pairs={{0,8},{1,9},{2,10},{3,11},{4,12},{5,13},{6,14},{7,15},{8,16},{9,17... | collective-permute-start | bytes 1769480 | tf_op jit(solution)/shard_map/ppermute | solution.py:72
  293.6 27.9 %collective-permute-start.39 = (bf16[384,768]{1,0:T(8,128)(2,1)}, bf16[384,768]{1,0:T(8,128)(2,1)S(1)}, u32[]{:S(2)}, u32[]{:S(2)}) collective-permute-start(bf16[384,768]{1,0:T(8,128)(2,1)} %collective-permute-done.38), channel_id=1, source_target_pairs={{0,8},{1,9},{2,10},{3,11},{4,12},{5,13},{6,14},{7,15},{8,16},{9,17... | collective-permute-start | bytes 1769480 | tf_op jit(solution)/shard_map/ppermute | solution.py:72
  308.8 25.3 %collective-permute-start.43 = (bf16[192,1536]{1,0:T(8,128)(2,1)S(1)}, bf16[192,1536]{1,0:T(8,128)(2,1)S(1)}, u32[]{:S(2)}, u32[]{:S(2)}) collective-permute-start(bf16[192,1536]{1,0:T(8,128)(2,1)S(1)} %collective-permute-done.42), channel_id=1, source_target_pairs={{0,8},{1,9},{2,10},{3,11},{4,12},{5,13},{6,14},{7,15},{8,16},{9,17... | collective-permute-start | bytes 1769480 | tf_op jit(solution)/shard_map/ppermute | solution.py:72
  311.6 34.6 %collective-permute-start.33 = (bf16[4,2,64,1536]{3,2,0,1:T(8,128)(2,1)S(1)}, bf16[4,2,64,1536]{3,2,0,1:T(8,128)(2,1)S(1)}, u32[]{:S(2)}, u32[]{:S(2)}) collective-permute-start(bf16[4,2,64,1536]{3,2,0,1:T(8,128)(2,1)S(1)} %get-tuple-element.64), channel_id=1, source_target_pairs={{0,4},{1,5},{2,6},{3,7},{4,0},{5,1},{6,2},{7,3},{8,12},{9,13},{10,... | collective-permute-start | bytes 4718600 | tf_op jit(solution)/shard_map/ppermute | solution.py:72
  321.4 24.7 %collective-permute-start.40 = (bf16[384,768]{1,0:T(8,128)(2,1)S(1)}, bf16[384,768]{1,0:T(8,128)(2,1)S(1)}, u32[]{:S(2)}, u32[]{:S(2)}) collective-permute-start(bf16[384,768]{1,0:T(8,128)(2,1)S(1)} %collective-permute-done.39), channel_id=1, source_target_pairs={{0,8},{1,9},{2,10},{3,11},{4,12},{5,13},{6,14},{7,15},{8,16},{9,17... | collective-permute-start | bytes 1769480 | tf_op jit(solution)/shard_map/ppermute | solution.py:72
  363.5 18.1 %collective-permute-start.95 = (bf16[192,1536]{1,0:T(8,128)(2,1)S(1)}, bf16[192,1536]{1,0:T(8,128)(2,1)S(1)}, u32[]{:S(2)}, u32[]{:S(2)}) collective-permute-start(bf16[192,1536]{1,0:T(8,128)(2,1)S(1)} %dynamic-slice_bitcast_fusion), channel_id=1, source_target_pairs={{0,8},{1,9},{2,10},{3,11},{4,12},{5,13},{6,14},{7,15},{8,16},{9,17... | collective-permute-start | bytes 1769480 | tf_op jit(solution)/shard_map/ppermute | solution.py:72
  366.8 27.5 %collective-permute-start.88 = (bf16[2,4,48,768]{3,2,0,1:T(8,128)(2,1)S(1)}, bf16[2,4,48,768]{3,2,0,1:T(8,128)(2,1)S(1)}, u32[]{:S(2)}, u32[]{:S(2)}) collective-permute-start(bf16[2,4,48,768]{3,2,0,1:T(8,128)(2,1)S(1)} %bitcast.661), channel_id=1, source_target_pairs={{0,8},{1,9},{2,10},{3,11},{4,12},{5,13},{6,14},{7,15},{8,16},{9,17... | collective-permute-start | bytes 1769480 | tf_op jit(solution)/shard_map/ppermute | solution.py:72
  371.8 47.9 %collective-permute-start.44 = (bf16[4,2,64,1536]{3,2,0,1:T(8,128)(2,1)S(1)}, bf16[4,2,64,1536]{3,2,0,1:T(8,128)(2,1)S(1)}, u32[]{:S(2)}, u32[]{:S(2)}) collective-permute-start(bf16[4,2,64,1536]{3,2,0,1:T(8,128)(2,1)S(1)} %copy.226), channel_id=1, source_target_pairs={{0,4},{1,5},{2,6},{3,7},{4,0},{5,1},{6,2},{7,3},{8,12},{9,13},{10,... | collective-permute-start | bytes 4718600 | tf_op jit(solution)/shard_map/ppermute | solution.py:72
  381.8 25.1 %collective-permute-start.96 = (bf16[192,1536]{1,0:T(8,128)(2,1)S(1)}, bf16[192,1536]{1,0:T(8,128)(2,1)S(1)}, u32[]{:S(2)}, u32[]{:S(2)}) collective-permute-start(bf16[192,1536]{1,0:T(8,128)(2,1)S(1)} %fusion.33), channel_id=1, source_target_pairs={{0,8},{1,9},{2,10},{3,11},{4,12},{5,13},{6,14},{7,15},{8,16},{9,17... | collective-permute-start | bytes 1769480 | tf_op jit(solution)/shard_map/ppermute | solution.py:72
  394.4 25.1 %collective-permute-start.89 = (bf16[2,4,48,768]{3,2,0,1:T(8,128)(2,1)S(1)}, bf16[2,4,48,768]{3,2,0,1:T(8,128)(2,1)S(1)}, u32[]{:S(2)}, u32[]{:S(2)}) collective-permute-start(bf16[2,4,48,768]{3,2,0,1:T(8,128)(2,1)S(1)} %fusion.35), channel_id=1, source_target_pairs={{0,8},{1,9},{2,10},{3,11},{4,12},{5,13},{6,14},{7,15},{8,16},{9,17... | collective-permute-start | bytes 1769480 | tf_op jit(solution)/shard_map/ppermute | solution.py:72
  400.3 21.0 %collective-permute-start.54 = (bf16[4,2,64,1536]{3,2,0,1:T(8,128)(2,1)S(1)}, bf16[4,2,64,1536]{3,2,0,1:T(8,128)(2,1)S(1)}, u32[]{:S(2)}, u32[]{:S(2)}) collective-permute-start(bf16[4,2,64,1536]{3,2,0,1:T(8,128)(2,1)S(1)} %copy.232), channel_id=1, source_target_pairs={{0,4},{1,5},{2,6},{3,7},{4,0},{5,1},{6,2},{7,3},{8,12},{9,13},{10,... | collective-permute-start | bytes 4718600 | tf_op jit(solution)/shard_map/ppermute | solution.py:72
  407.9 84.0 %collective-permute-start.97 = (bf16[192,1536]{1,0:T(8,128)(2,1)}, bf16[192,1536]{1,0:T(8,128)(2,1)}, u32[]{:S(2)}, u32[]{:S(2)}) collective-permute-start(bf16[192,1536]{1,0:T(8,128)(2,1)} %fusion.34), channel_id=1, source_target_pairs={{0,8},{1,9},{2,10},{3,11},{4,12},{5,13},{6,14},{7,15},{8,16},{9,17... | collective-permute-start | bytes 1769480 | tf_op jit(solution)/shard_map/ppermute | solution.py:72
  419.7 23.7 %collective-permute-start.90 = (bf16[2,4,48,768]{3,2,0,1:T(8,128)(2,1)S(1)}, bf16[2,4,48,768]{3,2,0,1:T(8,128)(2,1)S(1)}, u32[]{:S(2)}, u32[]{:S(2)}) collective-permute-start(bf16[2,4,48,768]{3,2,0,1:T(8,128)(2,1)S(1)} %fusion.36), channel_id=1, source_target_pairs={{0,8},{1,9},{2,10},{3,11},{4,12},{5,13},{6,14},{7,15},{8,16},{9,17... | collective-permute-start | bytes 1769480 | tf_op jit(solution)/shard_map/ppermute | solution.py:72
  425.6 42.8 %collective-permute-start.45 = (bf16[2,64,1536]{2,1,0:T(8,128)(2,1)}, bf16[2,64,1536]{2,1,0:T(8,128)(2,1)}, u32[]{:S(2)}, u32[]{:S(2)}) collective-permute-start(bf16[2,64,1536]{2,1,0:T(8,128)(2,1)} %fusion.85), channel_id=1, source_target_pairs={{0,2},{1,3},{2,0},{3,1},{4,6},{5,7},{6,4},{7,5},{8,10},{9,11},{10,... | collective-permute-start | bytes 1179656 | tf_op jit(solution)/shard_map/ppermute | solution.py:72
  427.5 50.2 %collective-permute-start.47 = (bf16[2,64,1536]{2,1,0:T(8,128)(2,1)}, bf16[2,64,1536]{2,1,0:T(8,128)(2,1)}, u32[]{:S(2)}, u32[]{:S(2)}) collective-permute-start(bf16[2,64,1536]{2,1,0:T(8,128)(2,1)} %fusion.87), channel_id=1, source_target_pairs={{0,1},{1,0},{2,3},{3,2},{4,5},{5,4},{6,7},{7,6},{8,9},{9,8},{10,11... | collective-permute-start | bytes 1179656 | tf_op jit(solution)/shard_map/ppermute | solution.py:72
  427.5 42.3 %collective-permute-start.55 = (bf16[2,64,1536]{2,1,0:T(8,128)(2,1)}, bf16[2,64,1536]{2,1,0:T(8,128)(2,1)}, u32[]{:S(2)}, u32[]{:S(2)}) collective-permute-start(bf16[2,64,1536]{2,1,0:T(8,128)(2,1)} %fusion.86), channel_id=1, source_target_pairs={{0,2},{1,3},{2,0},{3,1},{4,6},{5,7},{6,4},{7,5},{8,10},{9,11},{10,... | collective-permute-start | bytes 1179656 | tf_op jit(solution)/shard_map/ppermute | solution.py:72
  468.4 26.8 %collective-permute-start.94 = (bf16[48,4,4,192]{3,0,2,1:T(8,128)(2,1)}, bf16[48,4,4,192]{3,0,2,1:T(8,128)(2,1)}, u32[]{:S(2)}, u32[]{:S(2)}) collective-permute-start(bf16[48,4,4,192]{3,0,2,1:T(8,128)(2,1)} %get-tuple-element.74), channel_id=1, source_target_pairs={{0,4},{1,5},{2,6},{3,7},{4,0},{5,1},{6,2},{7,3},{8,12},{9,13},{10,... | collective-permute-start | bytes 884744 | tf_op jit(solution)/shard_map/ppermute | solution.py:72
  469.8 16.2 %collective-permute-start.46 = (bf16[64,1536]{1,0:T(8,128)(2,1)S(1)}, bf16[64,1536]{1,0:T(8,128)(2,1)S(1)}, u32[]{:S(2)}, u32[]{:S(2)}) collective-permute-start(bf16[64,1536]{1,0:T(8,128)(2,1)S(1)} %fusion.129), channel_id=1, source_target_pairs={{0,1},{1,0},{2,3},{3,2},{4,5},{5,4},{6,7},{7,6},{8,9},{9,8},{10,11... | collective-permute-start | bytes 589832 | tf_op jit(solution)/shard_map/ppermute | solution.py:72
  568.9 21.2 %collective-permute-start.67 = (bf16[2,48,2304]{2,1,0:T(8,128)(2,1)S(1)}, bf16[2,48,2304]{2,1,0:T(8,128)(2,1)S(1)}, u32[]{:S(2)}, u32[]{:S(2)}) collective-permute-start(bf16[2,48,2304]{2,1,0:T(8,128)(2,1)S(1)} %get-tuple-element.53), channel_id=1, source_target_pairs={{0,2},{1,3},{2,0},{3,1},{4,6},{5,7},{6,4},{7,5},{8,10},{9,11},{10,... | collective-permute-start | bytes 1327112 | tf_op jit(solution)/shard_map/ppermute | solution.py:72
  569.7 29.9 %collective-permute-start.71 = (bf16[2,48,2304]{2,1,0:T(8,128)(2,1)S(1)}, bf16[2,48,2304]{2,1,0:T(8,128)(2,1)S(1)}, u32[]{:S(2)}, u32[]{:S(2)}) collective-permute-start(bf16[2,48,2304]{2,1,0:T(8,128)(2,1)S(1)} %get-tuple-element.52), channel_id=1, source_target_pairs={{0,2},{1,3},{2,0},{3,1},{4,6},{5,7},{6,4},{7,5},{8,10},{9,11},{10,... | collective-permute-start | bytes 1327112 | tf_op jit(solution)/shard_map/ppermute | solution.py:72
  570.9 37.7 %collective-permute-start.75 = (bf16[2,48,2304]{2,1,0:T(8,128)(2,1)S(1)}, bf16[2,48,2304]{2,1,0:T(8,128)(2,1)S(1)}, u32[]{:S(2)}, u32[]{:S(2)}) collective-permute-start(bf16[2,48,2304]{2,1,0:T(8,128)(2,1)S(1)} %get-tuple-element.51), channel_id=1, source_target_pairs={{0,2},{1,3},{2,0},{3,1},{4,6},{5,7},{6,4},{7,5},{8,10},{9,11},{10,... | collective-permute-start | bytes 1327112 | tf_op jit(solution)/shard_map/ppermute | solution.py:72
  571.7 38.1 %collective-permute-start.61 = (bf16[2,48,2304]{2,1,0:T(8,128)(2,1)S(1)}, bf16[2,48,2304]{2,1,0:T(8,128)(2,1)S(1)}, u32[]{:S(2)}, u32[]{:S(2)}) collective-permute-start(bf16[2,48,2304]{2,1,0:T(8,128)(2,1)S(1)} %get-tuple-element.50), channel_id=1, source_target_pairs={{0,1},{1,0},{2,3},{3,2},{4,5},{5,4},{6,7},{7,6},{8,9},{9,8},{10,11... | collective-permute-start | bytes 1327112 | tf_op jit(solution)/shard_map/ppermute | solution.py:72
  580.7 29.5 %collective-permute-start.65 = (bf16[2,48,2304]{2,1,0:T(8,128)(2,1)S(1)}, bf16[2,48,2304]{2,1,0:T(8,128)(2,1)S(1)}, u32[]{:S(2)}, u32[]{:S(2)}) collective-permute-start(bf16[2,48,2304]{2,1,0:T(8,128)(2,1)S(1)} %get-tuple-element.49), channel_id=1, source_target_pairs={{0,1},{1,0},{2,3},{3,2},{4,5},{5,4},{6,7},{7,6},{8,9},{9,8},{10,11... | collective-permute-start | bytes 1327112 | tf_op jit(solution)/shard_map/ppermute | solution.py:72
  590.1 20.0 %collective-permute-start.69 = (bf16[2,48,2304]{2,1,0:T(8,128)(2,1)S(1)}, bf16[2,48,2304]{2,1,0:T(8,128)(2,1)S(1)}, u32[]{:S(2)}, u32[]{:S(2)}) collective-permute-start(bf16[2,48,2304]{2,1,0:T(8,128)(2,1)S(1)} %get-tuple-element.48), channel_id=1, source_target_pairs={{0,1},{1,0},{2,3},{3,2},{4,5},{5,4},{6,7},{7,6},{8,9},{9,8},{10,11... | collective-permute-start | bytes 1327112 | tf_op jit(solution)/shard_map/ppermute | solution.py:72
  608.6 16.2 %collective-permute-start.83 = (bf16[2,4,48,768]{3,2,1,0:T(8,128)(2,1)S(1)}, bf16[2,4,48,768]{3,2,1,0:T(8,128)(2,1)S(1)}, u32[]{:S(2)}, u32[]{:S(2)}) collective-permute-start(bf16[2,4,48,768]{3,2,1,0:T(8,128)(2,1)S(1)} %dynamic-slice_bitcast_fusion.1), channel_id=1, source_target_pairs={{0,2},{1,3},{2,0},{3,1},{4,6},{5,7},{6,4},{7,5},{8,10},{9,11},{10,... | collective-permute-start | bytes 1769480 | tf_op jit(solution)/shard_map/ppermute | solution.py:72
  609.9 16.4 %collective-permute-start.81 = (bf16[2,4,48,768]{3,2,1,0:T(8,128)(2,1)S(1)}, bf16[2,4,48,768]{3,2,1,0:T(8,128)(2,1)S(1)}, u32[]{:S(2)}, u32[]{:S(2)}) collective-permute-start(bf16[2,4,48,768]{3,2,1,0:T(8,128)(2,1)S(1)} %dynamic-slice_bitcast_fusion.2), channel_id=1, source_target_pairs={{0,1},{1,0},{2,3},{3,2},{4,5},{5,4},{6,7},{7,6},{8,9},{9,8},{10,11... | collective-permute-start | bytes 1769480 | tf_op jit(solution)/shard_map/ppermute | solution.py:72
  610.1 85.5 %collective-permute-start.60 = (f32[2,320,1536]{2,1,0:T(8,128)}, f32[2,320,1536]{2,1,0:T(8,128)}, u32[]{:S(2)}, u32[]{:S(2)}) collective-permute-start(f32[2,320,1536]{2,1,0:T(8,128)} %pad_maximum_fusion.1), channel_id=1, source_target_pairs={{0,4},{1,5},{2,6},{3,7},{4,0},{5,1},{6,2},{7,3},{8,12},{9,13},{10,... | collective-permute-start | bytes 11796488 | tf_op jit(solution)/shard_map/ppermute | solution.py:72
  612.4 27.9 %collective-permute-start.74 = (bf16[48,2304]{1,0:T(8,128)(2,1)S(1)}, bf16[48,2304]{1,0:T(8,128)(2,1)S(1)}, u32[]{:S(2)}, u32[]{:S(2)}) collective-permute-start(bf16[48,2304]{1,0:T(8,128)(2,1)S(1)} %fusion.125), channel_id=1, source_target_pairs={{0,2},{1,3},{2,0},{3,1},{4,6},{5,7},{6,4},{7,5},{8,10},{9,11},{10,... | collective-permute-start | bytes 663560 | tf_op jit(solution)/shard_map/ppermute | solution.py:72
  613.8 27.0 %collective-permute-start.76 = (bf16[48,2304]{1,0:T(8,128)(2,1)S(1)}, bf16[48,2304]{1,0:T(8,128)(2,1)S(1)}, u32[]{:S(2)}, u32[]{:S(2)}) collective-permute-start(bf16[48,2304]{1,0:T(8,128)(2,1)S(1)} %fusion.126), channel_id=1, source_target_pairs={{0,1},{1,0},{2,3},{3,2},{4,5},{5,4},{6,7},{7,6},{8,9},{9,8},{10,11... | collective-permute-start | bytes 663560 | tf_op jit(solution)/shard_map/ppermute | solution.py:72
  647.3 14.5 %collective-permute-start.77 = (bf16[2,48,2304]{2,1,0:T(8,128)(2,1)S(1)}, bf16[2,48,2304]{2,1,0:T(8,128)(2,1)S(1)}, u32[]{:S(2)}, u32[]{:S(2)}) collective-permute-start(bf16[2,48,2304]{2,1,0:T(8,128)(2,1)S(1)} %pad_maximum_fusion.19), channel_id=1, source_target_pairs={{0,8},{1,9},{2,10},{3,11},{4,12},{5,13},{6,14},{7,15},{8,16},{9,17... | collective-permute-start | bytes 1327112 | tf_op jit(solution)/shard_map/ppermute | solution.py:72
  651.8 13.1 %collective-permute-start.85 = (bf16[48,1536]{1,0:T(8,128)(2,1)S(1)}, bf16[48,1536]{1,0:T(8,128)(2,1)S(1)}, u32[]{:S(2)}, u32[]{:S(2)}) collective-permute-start(bf16[48,1536]{1,0:T(8,128)(2,1)S(1)} %fusion.133), channel_id=1, source_target_pairs={{0,8},{1,9},{2,10},{3,11},{4,12},{5,13},{6,14},{7,15},{8,16},{9,17... | collective-permute-start | bytes 442376 | tf_op jit(solution)/shard_map/ppermute | solution.py:72
  (146 other events, 1629.6 us)

commit v2 on v0

v2 whole, which is shorter than its diff:
```python
import functools
import math

import jax
import jax.numpy as jnp
from jax import lax
from jax.experimental import pallas as pl
from jax.experimental.pallas import tpu as pltpu
from jax.sharding import PartitionSpec as P

HEAD = 96
PACK = 4
AXES = ("dp", "fsdp")
LOW = jnp.bfloat16
WIDE = jnp.float32
HIGHEST = lax.Precision.HIGHEST
NORM_EPS = 1e-05


def norm_rows(inputs, gain, shift):
    row_mean = jnp.mean(inputs, axis=-1, keepdims=True)
    centered = inputs - row_mean
    variance = jnp.mean(centered * centered, axis=-1, keepdims=True)
    return centered * lax.rsqrt(variance + NORM_EPS) * gain + shift


def exact_gelu(inputs):
    return jax.nn.gelu(inputs, approximate=False)


def dot(left, right, contract):
    return lax.dot_general(left, right, (contract, ((), ())), preferred_element_type=WIDE)


def rows_by(left, right):
    return dot(left, right, ((left.ndim - 1,), (0,)))


def rows_back(left, right):
    return dot(left, right, ((left.ndim - 1,), (1,)))


def outer(left, right):
    return dot(left, right, ((0,), (0,)))


class Wires:
    def __init__(self, mesh):
        self.deep = mesh.shape["dp"] // 2
        self.flat = mesh.shape["fsdp"]
        self.count = 2 * self.deep * self.flat
        places = [
            (z, c, f) for z in range(self.deep) for c in range(2) for f in range(self.flat)
        ]

        def number(z, c, f):
            return (z * 2 + c) * self.flat + f

        def moves(target):
            return [(number(*place), number(*target(*place))) for place in places]

        self.bits = [1 << k for k in range(self.flat.bit_length() - 1)]
        self.masks = list(range(1, self.flat))
        self.moves = {
            "core": moves(lambda z, c, f: (z, 1 - c, f)),
        }
        self.moves["rise"] = moves(lambda z, c, f: ((z + 1) % self.deep, c, f))
        self.columns = [
            [number(z, c, f) for z in range(self.deep)] for c in range(2) for f in range(self.flat)
        ]
        self.planes = [
            [number(z, c, f) for c in range(2) for f in range(self.flat)] for z in range(self.deep)
        ]
        for mask in self.masks:
            self.moves[mask] = moves(lambda z, c, f, mask=mask: (z, c, f ^ mask))

    def place(self):
        outer_at = lax.axis_index("dp")
        self.z, self.c = outer_at // 2, outer_at % 2
        self.f = lax.axis_index("fsdp")
        self.queues = {}

    def send(self, block, kind, *ahead):
        if ahead:
            block = after(block, *ahead)
        return lax.ppermute(block, AXES, self.moves[kind])

    def swap_blocks(self, blocks, groups):
        return lax.all_to_all(blocks, AXES, 0, 0, tiled=True, axis_index_groups=groups)

    def plane(self, step):
        return lax.rem(self.z + 2 * self.deep - step, self.deep)


def after(block, *others):
    return lax.optimization_barrier((block, *others))[0]


def at(array, index, axis):
    return lax.dynamic_index_in_dim(array, index, axis, keepdims=False)


def pair(mine, other, side, axis):
    return jnp.where(
        side == 0, jnp.stack([mine, other], axis=axis), jnp.stack([other, mine], axis=axis)
    )


def pick(array, side, axis):
    return jnp.where(
        side == 0,
        lax.index_in_dim(array, 0, axis, keepdims=False),
        lax.index_in_dim(array, 1, axis, keepdims=False),
    )


def corner(mask):
    return mask & -mask, 1 << (mask.bit_length() - 1)


def gather_rows(wires, block, take, guest, hooks):
    rings, gathered, before, guests = [block], [], (), {0: guest}
    single = [mask for mask in wires.masks if not mask & (mask - 1)]
    multiple = sorted((m for m in wires.masks if m & (m - 1)), key=lambda m: bin(m).count("1"))
    steps = []
    for step in range(wires.deep + 1):
        now = []
        before = (*before, *(hooks[step](guests) if step in hooks else ()))
        if step < wires.deep:
            if step + 1 < wires.deep:
                rings.append(wires.send(rings[step], "rise", *before))
                now.append(rings[-1])
            mine = take(rings[step])
            got = {0: mine}
            for mask in single:
                got[mask] = wires.send(mine, mask, *before)
                now.append(got[mask])
            gathered.append(got)
        for mask in single if step == 0 else multiple if step == wires.deep - 1 else ():
            guests[mask] = wires.send(guest, mask, *before)
            if step == 0:
                now.append(guests[mask])
        if step:
            got = gathered[step - 1]
            for mask in multiple:
                low, high = corner(mask)
                got[mask] = (
                    wires.send(got[mask ^ high][0], high, *before),
                    wires.send(got[mask ^ low][1], low, *before),
                )
                now += got[mask]
        before = now
        steps.append(now)
    return rings, gathered, guests, steps


def scatter_rows(wires, part, pulls):
    single = [mask for mask in wires.masks if not mask & (mask - 1)]
    multiple = sorted((m for m in wires.masks if m & (m - 1)), key=lambda m: -bin(m).count("1"))
    extra = [{} for _ in range(wires.deep)]
    before, total = [None], None
    for step in range(wires.deep + 2):
        now = []
        ahead = (*(before if step else ()), *(pulls[step](before[-1]) if step in pulls else ()))

        def term(block, mask, half=None):
            mine = part(block, mask)
            if half is not None:
                mine = mine[half]
            more = extra[block].get((mask, half), [])
            return sum([m.astype(WIDE) for m in more], mine).astype(LOW)

        block = step - 2
        if 0 <= block:
            total = (
                sum([m.astype(WIDE) for m in extra[block][0, None]], part(block, 0).astype(WIDE))
                + (0.0 if total is None else total)
            )
            if block == wires.deep - 1:
                return total
            arrived = wires.send(total.astype(LOW), "rise", *ahead)
            now.append(arrived)
            total = arrived.astype(WIDE)
        block = step - 1
        if 0 <= block < wires.deep:
            for mask in single:
                halves = [term(block, mask, half) for half in range(2)]
                arrived = wires.send(jnp.stack(halves), mask, *ahead)
                extra[block].setdefault((0, None), []).append(arrived)
                now.append(arrived)
        if step < wires.deep:
            for mask in multiple:
                low, high = corner(mask)
                for half, bit in ((0, high), (1, low)):
                    arrived = wires.send(term(step, mask, half), bit, *ahead)
                    extra[step].setdefault((mask ^ bit, half), []).append(arrived)
                    now.append(arrived)
        before = now


def spread_plane(wires, block, *ahead):
    got = {0: block}
    for mask in reversed(wires.masks):
        got[mask] = wires.send(block, mask, *ahead)
    return got


def sum_plane(wires, part, *ahead):
    arrived = [wires.send(part(mask).astype(LOW), mask, *ahead) for mask in reversed(wires.masks)]
    return sum([block.astype(WIDE) for block in arrived], part(0).astype(WIDE)), arrived


def lay(places, pieces, count):
    entry = pieces[0].shape[1:]
    views = [(k, i) for k, piece in enumerate(pieces) for i in range(piece.shape[0])]
    number = len(views)

    def kernel(places_ref, *refs):
        out_ref, held, sems = refs[-3:]
        loads = [
            pltpu.make_async_copy(refs[k].at[i], held.at[n], sems.at[0, n])
            for n, (k, i) in enumerate(views)
        ]
        stores = [
            pltpu.make_async_copy(held.at[n], out_ref.at[places_ref[n]], sems.at[1, n])
            for n in range(number)
        ]
        for load in loads:
            load.start()
        for load, store in zip(loads, stores, strict=True):
            load.wait()
            store.start()
        for store in stores:
            store.wait()

    anywhere = pl.BlockSpec(memory_space=pl.ANY)
    return pl.pallas_call(
        kernel,
        out_shape=jax.ShapeDtypeStruct((count,) + entry, pieces[0].dtype),
        in_specs=[pl.BlockSpec(memory_space=pltpu.SMEM)] + [anywhere] * len(pieces),
        out_specs=anywhere,
        scratch_shapes=[
            pltpu.VMEM((number,) + entry, pieces[0].dtype),
            pltpu.SemaphoreType.DMA((2, number)),
        ],
        compiler_params=pltpu.CompilerParams(vmem_limit_bytes=16 * 2**20),
    )(jnp.stack(places).astype(jnp.int32), *pieces)


def whole_tiles(rows):
    return rows % 16 == 0


def joined(places, pieces):
    shard = pieces[0].shape[-2]
    if whole_tiles(shard):
        return places, pieces
    rows = [row for piece in pieces for row in (piece if piece.ndim == 3 else (piece,))]
    full = jnp.zeros((len(rows), *rows[0].shape), rows[0].dtype)
    for place, row in zip(places, rows, strict=True):
        full = lax.dynamic_update_index_in_dim(full, row, place, 0)
    return [jnp.zeros((), jnp.int32)], [full.reshape(1, len(rows) * shard, -1)]


def on_chip(kernel, out_shape, side, *operands):
    whole = pl.BlockSpec(memory_space=pltpu.VMEM)
    return pl.pallas_call(
        kernel,
        out_shape=out_shape,
        in_specs=[pl.BlockSpec(memory_space=pltpu.SMEM)] + [whole] * len(operands),
        out_specs=jax.tree.map(lambda _: whole, out_shape),
    )(side.reshape(1).astype(jnp.int32), *operands)


def deal_columns(side, arrays, group):
    shard = arrays[0].shape[0]
    width = sum(array.shape[1] for array in arrays) // 2
    if not whole_tiles(shard):
        both = jnp.concatenate(arrays, axis=1).reshape(shard, -1, 2, group)
        return tuple(pick(both, s, 2).reshape(shard, width) for s in (side, 1 - side))

    def kernel(side_ref, *refs):
        *in_refs, own_ref, other_ref = refs
        first = side_ref[0] == 0
        base = 0
        for ref in in_refs:
            block = ref[...]
            count = block.shape[1] // (2 * group)
            hands = [
                jnp.concatenate(
                    [block[:, (2 * j + s) * group : (2 * j + s + 1) * group] for j in range(count)],
                    axis=1,
                )
                for s in range(2)
            ]
            own_ref[:, base : base + count * group] = jnp.where(first, hands[0], hands[1])
            other_ref[:, base : base + count * group] = jnp.where(first, hands[1], hands[0])
            base += count * group

    shape = jax.ShapeDtypeStruct((shard, width), arrays[0].dtype)
    return on_chip(kernel, (shape, shape), side, *arrays)


def join_columns(side, own, other, widths, group):
    shard = own.shape[0]
    if not whole_tiles(shard):
        halves = [part.reshape(shard, -1, group) for part in (own, other)]
        both = pair(halves[0], halves[1], side, 2).reshape(shard, -1)
        return tuple(jnp.split(both, [widths[0]], axis=1))

    def kernel(side_ref, own_ref, other_ref, *out_refs):
        first = side_ref[0] == 0
        hands = (
            jnp.where(first, own_ref[...], other_ref[...]),
            jnp.where(first, other_ref[...], own_ref[...]),
        )
        base = 0
        for ref in out_refs:
            parts = []
            for j in range(ref.shape[1] // (2 * group)):
                columns = slice(base + j * group, base + (j + 1) * group)
                parts += [hand[:, columns] for hand in hands]
            ref[...] = jnp.concatenate(parts, axis=1)
            base += ref.shape[1] // 2

    shapes = tuple(jax.ShapeDtypeStruct((own.shape[0], width), own.dtype) for width in widths)
    return on_chip(kernel, shapes, side, own, other)


def split_units(array, ways, unit):
    shard, width = array.shape
    deep = width // (ways * unit)
    if not whole_tiles(shard):
        blocks = array.reshape(shard, deep, ways, unit).transpose(2, 0, 1, 3)
        return blocks.reshape(ways, shard, deep * unit)

    def kernel(_, in_ref, out_ref):
        block = in_ref[...]
        for way in range(ways):
            parts = [
                block[:, (z * ways + way) * unit : (z * ways + way + 1) * unit] for z in range(deep)
            ]
            out_ref[way] = jnp.concatenate(parts, axis=1)

    shape = jax.ShapeDtypeStruct((ways, shard, deep * unit), array.dtype)
    return on_chip(kernel, shape, jnp.zeros((), jnp.int32), array)


def merge_units(blocks, unit):
    ways, shard, part = blocks.shape
    deep = part // unit
    if not whole_tiles(shard):
        blocks = blocks.reshape(ways, shard, deep, unit).transpose(1, 2, 0, 3)
        return blocks.reshape(shard, -1).astype(WIDE)

    def kernel(_, in_ref, out_ref):
        parts = []
        for z in range(deep):
            for way in range(ways):
                parts.append(in_ref[way][:, z * unit : (z + 1) * unit].astype(WIDE))
        out_ref[...] = jnp.concatenate(parts, axis=1)

    shape = jax.ShapeDtypeStruct((shard, deep * ways * unit), WIDE)
    return on_chip(kernel, shape, jnp.zeros((), jnp.int32), blocks)


def tile_heads(rows, mask):
    return jnp.concatenate([rows] * PACK, axis=0) * mask


def untile_heads(rows, mask):
    kept = rows * mask
    size = rows.shape[0] // PACK
    return sum(kept[k * size : (k + 1) * size] for k in range(PACK))


def head_mask(rows, dtype):
    row = lax.broadcasted_iota(jnp.int32, (PACK * rows, PACK * HEAD), 0) // rows
    column = lax.broadcasted_iota(jnp.int32, (PACK * rows, PACK * HEAD), 1) // HEAD
    return (row == column).astype(WIDE).astype(dtype)


def attend(places, pieces, own, far, patches, half_width):
    images, key_rows, model_width = own.shape
    slots = 2 * images
    lat_rows = key_rows - patches
    width = 3 * half_width
    places, pieces = joined(places, pieces)
    chunk = PACK * HEAD
    groups = half_width // chunk
    scale = 1.0 / math.sqrt(HEAD)
    shard = pieces[0].shape[-2]
    views = []
    for k, piece in enumerate(pieces):
        views += [(k, None)] if piece.ndim == 2 else [(k, core) for core in range(piece.shape[0])]

    def kernel(places_ref, *refs):
        piece_refs = refs[: len(pieces)]
        (
            own_ref,
            far_ref,
            full_ref,
            query_ref,
            keyval_ref,
            probs_ref,
            mixed_ref,
            w_ref,
            sems,
        ) = refs[len(pieces) :]
        slot = pl.program_id(0)

        def save():
            return pltpu.make_async_copy(w_ref, full_ref, sems.at[len(views)])

        @pl.when(slot == 0)
        def _():
            loads = []
            for i, (k, core) in enumerate(views):
                source = piece_refs[k] if core is None else piece_refs[k].at[core]
                start = pl.multiple_of(places_ref[i] * shard, shard)
                loads.append(
                    pltpu.make_async_copy(source, w_ref.at[pl.ds(start, shard)], sems.at[i])
                )
            for load in loads:
                load.start()
            for load in loads:
                load.wait()
            save().start()

        x = jnp.where(slot < images, own_ref[0], far_ref[0])
        mask_low, mask_wide = head_mask(lat_rows, LOW), head_mask(lat_rows, WIDE)

        def project(rows, part):
            w = w_ref[:, part * chunk : (part + 1) * chunk]
            return jnp.dot(rows, w, preferred_element_type=WIDE).astype(LOW)

        for part in range(groups):
            columns = slice(part * chunk, (part + 1) * chunk)
            query = project(x[patches:], part)
            query_ref[0, :, columns] = query
            k = project(x, groups + part)
            keyval_ref[0, :, columns] = k
            v = project(x, 2 * groups + part)
            keyval_ref[0, :, half_width + part * chunk : half_width + (part + 1) * chunk] = v
            s = dot(tile_heads(query, mask_low), k, ((1,), (1,)))
            e = jnp.exp((s - jnp.max(s, axis=1, keepdims=True)) * scale)
            p = e * (1.0 / jnp.sum(e, axis=1, keepdims=True))
            probs_ref[0, part] = p
            m = jnp.dot(p.astype(LOW), v, preferred_element_type=WIDE)
            mixed_ref[0, :, columns] = untile_heads(m, mask_wide).astype(LOW)

        @pl.when(slot == slots - 1)
        def _():
            save().wait()

    anywhere = pl.BlockSpec(memory_space=pl.ANY)

    def slotted(*block):
        return pl.BlockSpec((1, *block), lambda i: (i,) + (0,) * len(block))

    return pl.pallas_call(
        kernel,
        grid=(slots,),
        out_shape=(
            jax.ShapeDtypeStruct((model_width, width), LOW),
            jax.ShapeDtypeStruct((slots, lat_rows, half_width), LOW),
            jax.ShapeDtypeStruct((slots, key_rows, 2 * half_width), LOW),
            jax.ShapeDtypeStruct((slots, groups, PACK * lat_rows, key_rows), WIDE),
            jax.ShapeDtypeStruct((slots, lat_rows, half_width), LOW),
        ),
        in_specs=[pl.BlockSpec(memory_space=pltpu.SMEM)]
        + [anywhere] * len(pieces)
        + [
            pl.BlockSpec((1, key_rows, model_width), lambda i: (jnp.minimum(i, images - 1), 0, 0)),
            pl.BlockSpec((1, key_rows, model_width), lambda i: (jnp.maximum(i - images, 0), 0, 0)),
        ],
        out_specs=(
            anywhere,
            slotted(lat_rows, half_width),
            slotted(key_rows, 2 * half_width),
            slotted(groups, PACK * lat_rows, key_rows),
            slotted(lat_rows, half_width),
        ),
        scratch_shapes=[
            pltpu.VMEM((model_width, width), LOW),
            pltpu.SemaphoreType.DMA((len(views) + 1,)),
        ],
        compiler_params=pltpu.CompilerParams(vmem_limit_bytes=40 * 2**20),
        cost_estimate=pl.CostEstimate(
            flops=2 * slots * key_rows * model_width * width,
            bytes_accessed=4 * model_width * width,
            transcendentals=0,
        ),
    )(jnp.stack(places).astype(jnp.int32), *pieces, own, far)


def project_out(places, pieces, mixed, model_width):
    slots, lat_rows, half_width = mixed.shape
    places, pieces = joined(places, pieces)
    shard = pieces[0].shape[-2]
    views = [(k, i) for k, piece in enumerate(pieces) for i in range(piece.shape[0])]
    chunk = PACK * HEAD

    def kernel(places_ref, *refs):
        piece_refs = refs[: len(pieces)]
        mixed_ref, full_ref, branch_ref, w_ref, sems = refs[len(pieces) :]
        loads = []
        for i, (k, entry) in enumerate(views):
            start = pl.multiple_of(places_ref[i] * shard, shard)
            loads.append(
                pltpu.make_async_copy(
                    piece_refs[k].at[entry], w_ref.at[pl.ds(start, shard)], sems.at[i]
                )
            )
        for load in loads:
            load.start()
        for load in loads:
            load.wait()
        save = pltpu.make_async_copy(w_ref, full_ref, sems.at[len(views)])
        save.start()
        rows = mixed_ref[...].reshape(slots * lat_rows, half_width)
        for part in range(model_width // chunk):
            columns = slice(part * chunk, (part + 1) * chunk)
            branch_ref[:, columns] = jnp.dot(
                rows, w_ref[:, columns], preferred_element_type=WIDE
            )
        save.wait()

    anywhere = pl.BlockSpec(memory_space=pl.ANY)
    whole = pl.BlockSpec(memory_space=pltpu.VMEM)
    full, branch = pl.pallas_call(
        kernel,
        out_shape=(
            jax.ShapeDtypeStruct((half_width, model_width), LOW),
            jax.ShapeDtypeStruct((slots * lat_rows, model_width), WIDE),
        ),
        in_specs=[pl.BlockSpec(memory_space=pltpu.SMEM)] + [anywhere] * len(pieces) + [whole],
        out_specs=(anywhere, whole),
        scratch_shapes=[
            pltpu.VMEM((half_width, model_width), LOW),
            pltpu.SemaphoreType.DMA((len(views) + 1,)),
        ],
        compiler_params=pltpu.CompilerParams(vmem_limit_bytes=16 * 2**20),
    )(jnp.stack(places).astype(jnp.int32), *pieces, mixed)
    return full, branch.reshape(slots, lat_rows, model_width)


def normal_parts(x):
    density = jnp.exp(-0.5 * x * x)
    t = 1.0 / (1.0 + (0.3275911 * math.sqrt(0.5)) * jnp.abs(x))
    series = t * (
        0.254829592
        + t * (-0.284496736 + t * (1.421413741 + t * (-1.453152027 + t * 1.061405429)))
    )
    upper = 0.5 * series * density
    return jnp.where(x < 0, upper, 1.0 - upper), density * (1.0 / math.sqrt(2 * math.pi))


def fold_up(block, folds):
    return jnp.concatenate(jnp.split(block, folds, axis=-2), axis=-1)


def unfold_up(block, folds):
    return jnp.concatenate(jnp.split(block, folds, axis=-1), axis=-2)


def ffn_rows_back(ffn_blocks, xs, d_outs, unit):
    deep = ffn_blocks.shape[0]
    hidden_units = deep * unit
    rows, model_width = xs[0].shape
    folds = model_width // hidden_units
    block = 128
    direct = whole_tiles(unit) and hidden_units % 128 == 0
    if direct:
        weights = (ffn_blocks,)
    else:
        weights = (
            unfold_up(ffn_blocks[:, unit:], folds).reshape(model_width, hidden_units),
            ffn_blocks[:, :unit].reshape(hidden_units, model_width),
        )

    def copies(weight_refs, up_ref, down_ref, sems):
        if not direct:
            moves = list(zip(weight_refs, (up_ref, down_ref), strict=True))
        else:
            (ffn_ref,) = weight_refs
            moves = []
            for z in range(deep):
                moves.append((ffn_ref.at[z, pl.ds(0, unit)], down_ref.at[pl.ds(z * unit, unit)]))
                for fold in range(folds):
                    moves.append(
                        (
                            ffn_ref.at[z, pl.ds(unit, unit), pl.ds(fold * hidden_units, hidden_units)],
                            up_ref.at[pl.ds((folds * z + fold) * unit, unit)],
                        )
                    )
        return [pltpu.make_async_copy(*move, sems.at[i]) for i, move in enumerate(moves)]

    def kernel(x0, x1, d0, d1, *refs):
        weight_refs, (hidden0, hidden1, pre0, pre1, in0, in1, up_ref, down_ref, sems) = (
            refs[: len(weights)],
            refs[len(weights) :],
        )

        @pl.when(pl.program_id(0) == 0)
        def _():
            loads = copies(weight_refs, up_ref, down_ref, sems)
            for load in loads:
                load.start()
            for load in loads:
                load.wait()

        x = jnp.concatenate([x0[...], x1[...]])
        d_out = jnp.concatenate([d0[...], d1[...]])
        pre = jnp.dot(x, up_ref[...], preferred_element_type=WIDE)
        d_hidden = dot(d_out, down_ref[...], ((1,), (1,)))
        below, density = normal_parts(pre)
        hidden = (pre * below).astype(LOW)
        d_pre = (d_hidden * (below + pre * density)).astype(LOW)
        d_input = dot(d_pre, up_ref[...], ((1,), (1,)))
        for side, (hidden_ref, pre_ref, in_ref) in enumerate(
            ((hidden0, pre0, in0), (hidden1, pre1, in1))
        ):
            mine = slice(side * block, (side + 1) * block)
            hidden_ref[...] = hidden[mine]
            pre_ref[...] = d_pre[mine]
            in_ref[...] = d_input[mine].astype(in_ref.dtype)

    wide = pl.BlockSpec((block, model_width), lambda i: (i, 0))
    narrow = pl.BlockSpec((block, hidden_units), lambda i: (i, 0))
    low = jax.ShapeDtypeStruct((rows, hidden_units), LOW)
    return pl.pallas_call(
        kernel,
        grid=(rows // block,),
        out_shape=(
            low,
            low,
            low,
            low,
            jax.ShapeDtypeStruct((rows, model_width), WIDE),
            jax.ShapeDtypeStruct((rows, model_width), LOW),
        ),
        in_specs=[wide] * 4 + [pl.BlockSpec(memory_space=pl.ANY)] * len(weights),
        out_specs=(narrow,) * 4 + (wide,) * 2,
        scratch_shapes=[
            pltpu.VMEM((model_width, hidden_units), LOW),
            pltpu.VMEM((hidden_units, model_width), LOW),
            pltpu.SemaphoreType.DMA(((folds + 1) * deep,)),
        ],
        compiler_params=pltpu.CompilerParams(vmem_limit_bytes=32 * 2**20),
        cost_estimate=pl.CostEstimate(
            flops=12 * rows * hidden_units * model_width,
            bytes_accessed=8 * rows * model_width,
            transcendentals=0,
        ),
    )(*xs, *d_outs, *weights)


def attend_back(d_mixed, query, keyval, probs):
    slots, lat_rows, half_width = query.shape
    key_rows = keyval.shape[1]
    patches = key_rows - lat_rows
    chunk = PACK * HEAD
    groups = half_width // chunk
    scale = 1.0 / math.sqrt(HEAD)

    def kernel(d_ref, query_ref, keyval_ref, probs_ref, out_ref):
        mask_low, mask_wide = head_mask(lat_rows, LOW), head_mask(lat_rows, WIDE)
        out_ref[0, :patches, :half_width] = jnp.zeros((patches, half_width), LOW)
        for part in range(groups):
            columns = slice(part * chunk, (part + 1) * chunk)
            q = tile_heads(query_ref[0, :, columns], mask_low)
            d = tile_heads(d_ref[0, :, columns], mask_low)
            k = keyval_ref[0, :, columns]
            v = keyval_ref[0, :, half_width + part * chunk : half_width + (part + 1) * chunk]
            p = probs_ref[0, part]
            d_probs = dot(d, v, ((1,), (1,)))
            d_value = dot(p.astype(LOW), d, ((0,), (0,)))
            delta = jnp.sum(p * d_probs, axis=1, keepdims=True)
            d_scores = (p * (d_probs - delta)).astype(LOW)
            d_query = untile_heads(jnp.dot(d_scores, k, preferred_element_type=WIDE), mask_wide)
            d_key = dot(d_scores, q, ((0,), (0,)))
            out_ref[0, patches:, columns] = (d_query * scale).astype(LOW)
            out_ref[0, :, half_width + part * chunk : half_width + (part + 1) * chunk] = (
                d_key * scale
            ).astype(LOW)
            out_ref[0, :, 2 * half_width + part * chunk : 2 * half_width + (part + 1) * chunk] = (
                d_value.astype(LOW)
            )

    def slotted(*block):
        return pl.BlockSpec((1, *block), lambda i: (i,) + (0,) * len(block))

    return pl.pallas_call(
        kernel,
        grid=(slots,),
        out_shape=jax.ShapeDtypeStruct((slots, key_rows, 3 * half_width), LOW),
        in_specs=[
            slotted(lat_rows, half_width),
            slotted(lat_rows, half_width),
            slotted(key_rows, 2 * half_width),
            slotted(groups, PACK * lat_rows, key_rows),
        ],
        out_specs=slotted(key_rows, 3 * half_width),
        compiler_params=pltpu.CompilerParams(vmem_limit_bytes=32 * 2**20),
        cost_estimate=pl.CostEstimate(
            flops=16 * slots * groups * PACK * lat_rows * key_rows * chunk,
            bytes_accessed=10 * slots * key_rows * half_width,
            transcendentals=0,
        ),
    )(d_mixed, query, keyval, probs)


def on_device(
    wires,
    media,
    latents,
    upstream,
    time_index,
    live_count,
    time_table,
    media_gain,
    media_bias,
    latent_gain,
    latent_bias,
    ff_gain,
    ff_bias,
    w_query,
    w_keyval,
    w_out,
    w_up,
    w_down,
):
    wires.place()
    deep, flat, count = wires.deep, wires.flat, wires.count
    images, patches, model_width = media.shape
    lat_rows = latents.shape[1]
    key_rows = patches + lat_rows
    table_rows, shard = time_table.shape
    group = model_width // (2 * deep)
    half_width = model_width // 2
    slots = 2 * images

    qkv_mine, qkv_other = deal_columns(wires.c, (w_query, w_keyval), group)
    qkv_arrived = wires.send(qkv_other, "core")
    qkv_block = pair(qkv_mine, qkv_arrived, wires.c, 0)

    unit = w_down.shape[0]
    hidden_units = deep * unit
    tall, wide = 2 * shard, 3 * half_width
    ring_block = jnp.concatenate(
        [qkv_block.reshape(tall, wide), jnp.pad(w_out, ((0, 0), (0, wide - model_width)))]
    )
    made = {}

    def norms(guests):
        smalls = jnp.concatenate(
            [time_table]
            + [
                v[None]
                for v in (media_gain, media_bias, latent_gain, latent_bias, ff_gain, ff_bias)
            ],
            axis=0,
        )
        smalls = jnp.broadcast_to(smalls[None], (count,) + smalls.shape)
        smalls = lax.all_to_all(after(smalls, guests[wires.bits[0]]), AXES, 0, 0, tiled=True)
        smalls = smalls.transpose(1, 0, 2).reshape(-1, model_width).astype(WIDE)
        table_full = smalls[:table_rows]
        (
            media_gain_full,
            media_bias_full,
            latent_gain_full,
            latent_bias_full,
            ff_gain_full,
            ff_bias_full,
        ) = [smalls[table_rows + k] for k in range(6)]

        alive = (jnp.arange(images) < live_count[0]).astype(WIDE)
        live_mask = alive[:, None, None]
        one_hot = (time_index[:, None] == jnp.arange(table_rows)[None, :]).astype(WIDE)
        time_rows = jnp.dot(one_hot, table_full, precision=HIGHEST)
        media_in = media.astype(WIDE) + time_rows[:, None, :]
        media_normed, media_norm_back = jax.vjp(norm_rows, media_in, media_gain_full, media_bias_full)
        latents_wide = after(latents, smalls).astype(WIDE)
        latent_normed, latent_norm_back = jax.vjp(
            norm_rows, latents_wide, latent_gain_full, latent_bias_full
        )
        own_sources = jnp.concatenate([media_normed.astype(LOW), latent_normed.astype(LOW)], axis=1)
        made.update(
            ff_gain_full=ff_gain_full,
            ff_bias_full=ff_bias_full,
            live_mask=live_mask,
            one_hot=one_hot,
            media_norm_back=media_norm_back,
            latent_norm_back=latent_norm_back,
            latents_wide=latents_wide,
            own_sources=own_sources,
        )
        return (own_sources,)

    d_out_low = after(upstream, qkv_other) * (jnp.arange(images) < live_count[0]).astype(LOW)[:, None, None]
    rings, gathered, d_out_got, steps = gather_rows(
        wires, ring_block, lambda block: block[:tall].reshape(2, shard, wide), d_out_low, {1: norms}
    )
    own_sources, latents_wide, live_mask, one_hot = (
        made[name] for name in ("own_sources", "latents_wide", "live_mask", "one_hot")
    )
    places, pieces = [], []
    for step, got in enumerate(gathered):
        for mask, part in got.items():
            pieces += part if isinstance(part, tuple) else [part]
            for core in range(2):
                places.append((wires.plane(step) * 2 + core) * flat + (wires.f ^ mask))
    out_column = [ring[tall:, :model_width] for ring in rings]

    up_block = wires.swap_blocks(
        split_units(after(w_up, gathered[0][wires.bits[0]]), 2 * flat, unit), wires.planes
    )
    folds = model_width // hidden_units
    ffn_block = jnp.concatenate([w_down, fold_up(up_block.reshape(-1, hidden_units), folds)])

    ffn_blocks = jnp.broadcast_to(ffn_block[None], (deep, *ffn_block.shape))
    ffn_blocks = after(ffn_blocks, rings[-1])
    ffn_blocks = wires.swap_blocks(ffn_blocks, wires.columns)

    out_places, out_pieces = [], []
    for mask, part in spread_plane(wires, jnp.stack(out_column), *steps[-2]).items():
        out_pieces.append(part)
        for step in range(deep):
            out_places.append(wires.plane(step) * flat + (wires.f ^ mask))

    far_sources = wires.send(own_sources, "core", rings[-1])

    qkv_full, query, keyval, probs, mixed = attend(
        places,
        pieces,
        own_sources,
        far_sources,
        patches,
        half_width,
    )
    out_full, branch = project_out(
        out_places, out_pieces, after(mixed, *d_out_got.values()), model_width
    )
    branch = branch[:images] + wires.send(branch[images:], "core")
    middle = latents_wide + branch

    ffn_normed, ffn_norm_back = jax.vjp(norm_rows, middle, made["ff_gain_full"], made["ff_bias_full"])
    d_out = upstream.astype(WIDE) * live_mask

    def swapped(blocks, *ahead):
        mine = jnp.stack(blocks)
        far = wires.send(mine, "core", *ahead)
        return mine.reshape(-1, model_width), far.reshape(-1, model_width)

    ffn_low = ffn_normed.astype(LOW)
    ffn_got = spread_plane(wires, ffn_low)
    d_out_got = {mask: after(part, ffn_low) for mask, part in d_out_got.items()}
    d_out_chunks = [swapped([d_out_got[0]]), swapped([d_out_got[mask] for mask in wires.masks])]
    ffn_chunks = [swapped([ffn_low])]
    near = ffn_rows_back(ffn_blocks, ffn_chunks[0], d_out_chunks[0], unit)
    ffn_chunks.append(swapped([ffn_got[mask] for mask in wires.masks], near[0]))
    far = ffn_rows_back(ffn_blocks, ffn_chunks[1], d_out_chunks[1], unit)
    block_shape = (images, lat_rows, model_width)

    def collect_core(near, far, *ahead):
        far_whole = far[0] + wires.send(far[1].astype(LOW), "core", *ahead).astype(WIDE)
        far_whole = far_whole.reshape(len(wires.masks), *block_shape)
        near_whole = near[0] + wires.send(near[1].astype(LOW), "core", *ahead).astype(WIDE)
        return {0: near_whole.reshape(block_shape)} | dict(zip(wires.masks, far_whole, strict=True))

    d_sums = collect_core(near[4:], far[4:])
    d_ffn_input, d_arrived = sum_plane(wires, d_sums.get)

    hidden = jnp.concatenate([after(near[0], d_arrived[0]), near[1], *far[:2]])
    d_pre_low = jnp.concatenate([after(near[2], d_arrived[0]), near[3], *far[2:4]])
    d_out_rows = jnp.concatenate([rows for pair_of in d_out_chunks for rows in pair_of])
    ffn_rows = jnp.concatenate([rows for pair_of in ffn_chunks for rows in pair_of])
    down_partial = outer(hidden, d_out_rows).astype(LOW).reshape(deep, unit, model_width)
    up_partial = outer(ffn_rows, d_pre_low).astype(LOW)
    up_partial = up_partial.reshape(deep, 2 * flat * shard, hidden_units)
    ffn_partial = jnp.concatenate([down_partial, fold_up(up_partial, folds)], axis=1)
    ffn_terms = wires.swap_blocks(ffn_partial, wires.columns)

    d_ffn_input = after(d_ffn_input, ffn_partial)
    d_middle_norm, ff_gain_grad, ff_bias_grad = ffn_norm_back(d_ffn_input)
    d_middle = d_out + d_middle_norm

    down_full = after(ffn_blocks, d_middle)[:, :unit].reshape(hidden_units, model_width)
    results = rows_by(hidden, down_full)
    counts = [near[0].shape[0], far[0].shape[0]]
    cuts = [counts[0], 2 * counts[0], 2 * counts[0] + counts[1]]
    results = jnp.split(results, cuts)
    result_sums = collect_core(results[:2], results[2:])
    result_low = [result_sums[mask].astype(LOW) for mask in wires.masks]

    own_branch = d_middle.astype(LOW)
    d_branch = jnp.concatenate([own_branch, wires.send(own_branch, "core")], axis=0)
    out_partial = outer(mixed.reshape(-1, half_width), d_branch.reshape(-1, model_width))
    out_partial = out_partial.astype(LOW).reshape(deep, flat, shard, model_width)
    out_partial = jnp.stack([out_partial[..., :half_width], out_partial[..., half_width:]], axis=2)
    d_mixed = rows_back(after(d_branch, out_partial), out_full).astype(LOW)
    d_projected = attend_back(d_mixed, query, keyval, probs)

    source_rows = jnp.concatenate([after(own_sources, d_branch), far_sources]).reshape(-1, model_width)
    d_projected_rows = d_projected.reshape(-1, wide)
    plane_rows = 2 * flat * shard

    kept = {}

    def results_home(arrived):
        own_result, got = sum_plane(wires, result_sums.get, d_projected)
        kept["out"] = ((middle + own_result) * live_mask).astype(LOW)
        return got

    def sources_back(arrived):
        d_projected_now = after(d_projected, arrived)
        far_d = rows_back(d_projected_now[images:], qkv_full).astype(LOW)
        far_d = wires.send(far_d, "core").astype(WIDE)
        kept["rows"] = rows_back(d_projected_now[:images], qkv_full) + far_d
        return (kept["rows"],)

    def norms_back(arrived):
        d_rows = after(kept["rows"], arrived)
        d_latent_in, latent_gain_grad, latent_bias_grad = made["latent_norm_back"](d_rows[:, patches:, :])
        media_grad, media_gain_grad, media_bias_grad = made["media_norm_back"](d_rows[:, :patches, :])
        latent_grad = d_middle + d_latent_in
        table_part = jnp.dot(one_hot.T, jnp.sum(media_grad, axis=1), precision=HIGHEST)

        small_grads = jnp.concatenate(
            [table_part]
            + [
                v[None]
                for v in (
                    media_gain_grad,
                    media_bias_grad,
                    latent_gain_grad,
                    latent_bias_grad,
                    ff_gain_grad,
                    ff_bias_grad,
                )
            ],
            axis=0,
        )
        small_grads = small_grads.reshape(-1, count, shard).transpose(1, 0, 2)
        kept["media"], kept["latent"], kept["small"] = media_grad, latent_grad, small_grads
        return media_grad, latent_grad, small_grads

    def ffn_home(arrived):
        ffn_sum = jnp.sum(after(ffn_terms, arrived).astype(WIDE), axis=0)
        kept["down"] = ffn_sum[:unit]
        up_sum = unfold_up(ffn_sum[unit:].astype(LOW), folds)
        kept["up"] = up_sum.reshape(2 * flat, shard, hidden_units)
        small_grads = lax.all_to_all(after(kept["small"], ffn_terms), AXES, 0, 0, tiled=True)
        kept["small"] = jnp.sum(small_grads, axis=0)
        return kept["down"], kept["up"], small_grads

    def partial_rows(step, d_rows):
        at_plane = wires.plane(1 + step)
        rows = lax.dynamic_slice_in_dim(source_rows, at_plane * plane_rows, plane_rows, 1)
        block = outer(rows, d_rows).astype(LOW).reshape(2, flat, shard, wide)
        return block, at(out_partial, at_plane, 0)

    partials = {0: partial_rows(0, d_projected_rows)}

    def more_partials(arrived):
        d_rows = after(d_projected_rows, arrived)
        for step in range(1, deep):
            partials[step] = partial_rows(step, d_rows)
        return (partials[1][0], *results_home(arrived))

    def part(step, mask):
        block, out_block = partials[step]
        target = wires.f ^ mask
        return jnp.concatenate([at(block, target, 1), at(out_block, target, 0)], axis=-1)

    total = scatter_rows(
        wires,
        part,
        {
            0: lambda _: result_low,
            1: more_partials,
            2: sources_back,
            3: norms_back,
            4: ffn_home,
        },
    )
    qkv_sum = total[..., :wide]
    w_out_grad = jnp.concatenate([total[0, :, wide:], total[1, :, wide:]], axis=-1)
    media_grad, latent_grad = kept["media"], kept["latent"]
    w_down_grad = kept["down"]
    small_grads = kept["small"]
    latents_out = kept["out"]
    up_blocks = wires.swap_blocks(after(kept["up"], small_grads), wires.planes)
    w_up_grad = merge_units(up_blocks, unit)
    qkv_own = pick(qkv_sum, wires.c, 0)
    qkv_far = wires.send(pick(qkv_sum, 1 - wires.c, 0), "core", up_blocks)
    w_query_grad, w_keyval_grad = join_columns(
        wires.c, qkv_own, qkv_far, (model_width, 2 * model_width), group
    )
    return (
        latents_out,
        media_grad,
        latent_grad,
        small_grads[:table_rows],
        *[small_grads[table_rows + k] for k in range(6)],
        w_query_grad,
        w_keyval_grad,
        w_out_grad,
        w_up_grad,
        w_down_grad,
    )


def solution(mesh):
    lead = P(AXES)
    table = P(None, AXES)
    return jax.shard_map(
        functools.partial(on_device, Wires(mesh)),
        mesh=mesh,
        in_specs=(lead,) * 5 + (table,) + (lead,) * 11,
        out_specs=(lead,) * 3 + (table,) + (lead,) * 11,
        check_vma=False,
    )
```

time: 1870 us -> 472 us (0.25)
  waiting for transfers between devices: 1470 us -> 136 us
  blocking collectives: 149 us -> 0 us
  matrix products: 167 us -> 40.8 us
  starting transfers between devices: 0.44 us -> 92.9 us
  Pallas kernels: 0 us -> 60.2 us
  other arithmetic: 21.7 us -> 66.3 us
  local copies, waits for them, and re-layouts: 42.4 us -> 65.2 us
    reduce_scatter x5 -> x0, waiting for transfers between devices: 1170 us -> none  [the longest x1 356 us: on_device(): lax.psum_scatter(down_grad, ('dp', 'fsdp'), scatter_dimension=0, tiled=True)]
    all_gather x5 -> x0, waiting for transfers between devices: 293 us -> none  [the longest x1 121 us: on_device(): lax.all_gather(w_up, ('dp', 'fsdp'), axis=0, tiled=True)]
    dot_general x22 -> x13, matrix products: 166 us -> 40.8 us  [the longest x11 39.7 us: dot(): lax.dot_general(left, right, (contract, ((), ())), preferred_element_type...]
    ppermute x0 -> x67, waiting for transfers between devices: none -> 123 us  [send(): return lax.ppermute(block, AXES, self.moves[kind])]
    unnamed x2 -> x0, blocking collectives: 82.3 us -> none
    all_gather x1 -> x0, blocking collectives: 66.8 us -> none  [on_device(): lax.all_gather(time_table, ('dp', 'fsdp'), axis=1, tiled=True)]
    ppermute x0 -> x67, starting transfers between devices: none -> 64 us  [send(): return lax.ppermute(block, AXES, self.moves[kind])]
    pallas_call x0 -> x9, Pallas kernels: none -> 60.2 us  [the longest x1 25.2 us: attend(): pl.pallas_call(kernel, grid=(slots,), out_shape=(jax.ShapeDtypeStruct((mo...]
  transfers between devices with their start and end apart: 11 -> 73, of which waited for: 9 -> 32; matrix products, arithmetic and copies ran while one was open for 8% -> 31% of each run, Pallas kernels for 0% -> 10%
where the time goes in v2:
time: 472 us; the launch traced here: 465 us
  waiting for transfers between devices  136 us (29%)
  starting transfers between devices  92.9 us (20%)
  other arithmetic  66.3 us (14%)
  local copies, waits for them, and re-layouts  65.2 us (14%)
  Pallas kernels  60.2 us (13%)
  matrix products  40.8 us (9%)
    ppermute x67, waiting for transfers between devices, send(): return lax.ppermute(block, AXES, self.moves[kind])  123 us
    ppermute x67, starting transfers between devices, send(): return lax.ppermute(block, AXES, self.moves[kind])  64 us
    dot_general x11, matrix products, dot(): lax.dot_general(left, right, (contract, ((), ())), preferred_element_type...  39.7 us
    pallas_call x1, Pallas kernels, attend(): pl.pallas_call(kernel, grid=(slots,), out_shape=(jax.ShapeDtypeStruct((mo...  25.2 us
    unnamed x255, local copies, waits for them, and re-layouts  24.8 us
    all_to_all x4, starting transfers between devices, swap_blocks(): lax.all_to_all(blocks, AXES, 0, 0, tiled=True, axis_index_groups=groups)  18.3 us
    pallas_call x2, Pallas kernels, ffn_rows_back(): pl.pallas_call(kernel, grid=(rows // block,), out_shape=(low, low, low, l...  15.3 us
  transfers between devices with their start and end apart: 73, of which 32 were waited for; matrix products, arithmetic and copies ran while one was open for 31% of the time, Pallas kernels for 10%

profile of v2, /device:TPU:0, one launch (start us, length us, event | category | flops | bytes accessed | tf_op | source)
XLA Modules:
  0.0 465.0 jit_solution(6717820509077018160)
XLA Ops:
  4.9 2.6 collective-permute-start.5
  15.4 4.2 collective-permute-done.4
  20.4 4.9 %all-to-all-start = ((bf16[32,2,336]{2,1,0:T(2,128)(2,1)}), bf16[32,2,336]{2,1,0:T(2,128)(2,1)S(1)}, u32[]{:S(2)}, u32[]{:S(2)}) async-start(bf16[32,2,336]{2,1,0:T(2,128)(2,1)} %reshape.396), calls=%async_computation | async-start | bytes 98304 | tf_op jit(solution)/shard_map/all_to_all | solution.py:766
  27.9 4.7 %all-to-all-done = bf16[32,2,336]{2,1,0:T(2,128)(2,1)S(1)} async-done(((bf16[32,2,336]{2,1,0:T(2,128)(2,1)}), bf16[32,2,336]{2,1,0:T(2,128)(2,1)S(1)}, u32[]{:S(2)}, u32[]{:S(2)}) %all-to-all-start) | async-done | bytes 43040 | tf_op jit(solution)/shard_map/all_to_all | solution.py:766
  41.6 4.2 all-to-all-start.1
  58.1 7.3 %collective-permute-done.8.refs_7_ = bf16[2,48,2304]{2,1,0:T(8,128)(2,1)S(1)} collective-permute-done((bf16[2,48,2304]{2,1,0:T(8,128)(2,1)S(1)}, bf16[2,48,2304]{2,1,0:T(8,128)(2,1)S(1)}, u32[]{:S(2)}, u32[]{:S(2)}) %collective-permute-start.8) | collective-permute-done | bytes 442400 | tf_op jit(solution)/shard_map/ppermute | solution.py:86
  67.7 3.9 collective-permute-done.6
  78.5 7.1 %collective-permute-done.13.refs_12_ = bf16[2,48,2304]{2,1,0:T(8,128)(2,1)S(1)} collective-permute-done((bf16[2,48,2304]{2,1,0:T(8,128)(2,1)S(1)}, bf16[2,48,2304]{2,1,0:T(8,128)(2,1)S(1)}, u32[]{:S(2)}, u32[]{:S(2)}) %collective-permute-start.13) | collective-permute-done | bytes 442400 | tf_op jit(solution)/shard_map/ppermute | solution.py:86
  87.1 6.0 %collective-permute-done.11 = bf16[144,2304]{1,0:T(8,128)(2,1)} collective-permute-done((bf16[144,2304]{1,0:T(8,128)(2,1)}, bf16[144,2304]{1,0:T(8,128)(2,1)}, u32[]{:S(2)}, u32[]{:S(2)}) %collective-permute-start.11) | collective-permute-done | bytes 663584 | tf_op jit(solution)/shard_map/ppermute | solution.py:86
  93.0 2.5 broadcast_in_dim.35
  95.5 5.5 %all-to-all-start.2 = ((bf16[4,384,1536]{2,1,0:T(8,128)(2,1)}), bf16[4,384,1536]{2,1,0:T(8,128)(2,1)}, u32[]{:S(2)}, u32[]{:S(2)}) async-start(bf16[4,384,1536]{2,1,0:T(8,128)(2,1)} %broadcast_in_dim.35), calls=%async_computation.2 | async-start | bytes 9437184 | tf_op jit(solution)/shard_map/all_to_all | solution.py:89
  108.3 7.7 %collective-permute-done.17.refs_17_ = bf16[2,48,2304]{2,1,0:T(8,128)(2,1)S(1)} collective-permute-done((bf16[2,48,2304]{2,1,0:T(8,128)(2,1)S(1)}, bf16[2,48,2304]{2,1,0:T(8,128)(2,1)S(1)}, u32[]{:S(2)}, u32[]{:S(2)}) %collective-permute-start.17) | collective-permute-done | bytes 442400 | tf_op jit(solution)/shard_map/ppermute | solution.py:86
  118.0 5.4 %collective-permute-done.18.refs_13_ = bf16[48,2304]{1,0:T(8,128)(2,1)S(1)} collective-permute-done((bf16[48,2304]{1,0:T(8,128)(2,1)S(1)}, bf16[48,2304]{1,0:T(8,128)(2,1)S(1)}, u32[]{:S(2)}, u32[]{:S(2)}) %collective-permute-start.18) | collective-permute-done | bytes 221216 | tf_op jit(solution)/shard_map/ppermute | solution.py:86
  127.1 6.8 %collective-permute-done.23.refs_18_ = bf16[48,2304]{1,0:T(8,128)(2,1)S(1)} collective-permute-done((bf16[48,2304]{1,0:T(8,128)(2,1)S(1)}, bf16[48,2304]{1,0:T(8,128)(2,1)S(1)}, u32[]{:S(2)}, u32[]{:S(2)}) %collective-permute-start.23) | collective-permute-done | bytes 221216 | tf_op jit(solution)/shard_map/ppermute | solution.py:86
  136.6 25.2 %shard_map.281 = (bf16[1536,2304]{1,0:T(8,128)(2,1)}, bf16[4,64,768]{2,1,0:T(8,128)(2,1)S(1)}, bf16[4,320,1536]{2,1,0:T(8,128)(2,1)}, f32[4,2,256,320]{3,2,1,0:T(8,128)}, bf16[4,64,768]{2,1,0:T(8,128)(2,1)S(1)}) custom-call(s32[32]{0:T(128)S(1)} %stack.324.places_ref, bf16[2,48,2304]{2,1,0:T(8,128)(2,1)S(1)} %maximum_select_fusion.refs_0_, ...), custom_call_target="tpu_custom_call" | custom-call | flops 9059696640 | bytes 14155776 | tf_op jit(solution)/shard_map/pallas_call | solution.py:461
  163.5 5.4 %shard_map.282 = (bf16[768,1536]{1,0:T(8,128)(2,1)S(1)}, f32[256,1536]{1,0:T(8,128)S(1)}) custom-call(s32[16]{0:T(128)S(1)} %stack.282.places_ref, bf16[4,48,1536]{2,1,0:T(8,128)(2,1)S(1)} %pad_maximum_fusion.6.refs_0_, bf16[4,48,1536]{2,1,0:T(8,128)(2,1)S(1)} %collective-permute-done.20.refs_1_, bf16[4,48,1536]{2,1,0:T(8,128)(2,1)S(1)} %collective-permute-done.21.refs_2_, ...), custom_call_target="tpu_custom_call" | custom-call | tf_op jit(solution)/shard_map/pallas_call | solution.py:531
  181.9 7.4 %collective-permute-done.32 = bf16[2,64,1536]{2,1,0:T(8,128)(2,1)S(1)} collective-permute-done((bf16[2,64,1536]{2,1,0:T(8,128)(2,1)S(1)}, bf16[2,64,1536]{2,1,0:T(8,128)(2,1)S(1)}, u32[]{:S(2)}, u32[]{:S(2)}) %collective-permute-start.32) | collective-permute-done | bytes 393248 | tf_op jit(solution)/shard_map/ppermute | solution.py:86
  189.2 7.6 %collective-permute-done.31 = bf16[2,64,1536]{2,1,0:T(8,128)(2,1)S(1)} collective-permute-done((bf16[2,64,1536]{2,1,0:T(8,128)(2,1)S(1)}, bf16[2,64,1536]{2,1,0:T(8,128)(2,1)S(1)}, u32[]{:S(2)}, u32[]{:S(2)}) %collective-permute-start.31) | collective-permute-done | bytes 393248 | tf_op jit(solution)/shard_map/ppermute | solution.py:86
  199.5 2.7 all-to-all-done.2.refs_0_
  205.2 4.5 shard_map.284
  212.1 2.8 collective-permute-done.33
  214.9 10.7 %shard_map.285 = (bf16[384,768]{1,0:T(8,128)(2,1)S(1)}, bf16[384,768]{1,0:T(8,128)(2,1)S(1)}, bf16[384,768]{1,0:T(8,128)(2,1)S(1)}, bf16[384,768]{1,0:T(8,128)(2...) custom-call(bf16[384,1536]{1,0:T(8,128)(2,1)S(1)} %bitcast.361, bf16[384,1536]{1,0:T(8,128)(2,1)S(1)} %bitcast.377, ...), custom_call_target="tpu_custom_call" | custom-call | flops 5435817984 | bytes 4718592 | tf_op jit(solution)/shard_map/pallas_call | solution.py:632
  233.6 2.4 add_convert_fusion.1
  241.6 8.4 %collective-permute-done.36 = bf16[2,64,1536]{2,1,0:T(8,128)(2,1)S(1)} collective-permute-done((bf16[2,64,1536]{2,1,0:T(8,128)(2,1)S(1)}, bf16[2,64,1536]{2,1,0:T(8,128)(2,1)S(1)}, u32[]{:S(2)}, u32[]{:S(2)}) %collective-permute-start.36) | collective-permute-done | bytes 393248 | tf_op jit(solution)/shard_map/ppermute | solution.py:86
  250.8 2.8 convolution_convert_fusion.4
  255.6 4.5 convolution_convert_fusion.5
  262.4 5.1 %all-to-all-start.3 = ((bf16[4,384,1536]{2,1,0:T(8,128)(2,1)}), bf16[4,384,1536]{2,1,0:T(8,128)(2,1)}, u32[]{:S(2)}, u32[]{:S(2)}) async-start(bf16[4,384,1536]{2,1,0:T(8,128)(2,1)} %maximum_maximum_fusion), calls=%async_computation.3 | async-start | bytes 9437184 | tf_op jit(solution)/shard_map/all_to_all | solution.py:89
  274.4 4.5 fusion.176
  290.1 5.7 %shard_map.286 = bf16[4,320,2304]{2,1,0:T(8,128)(2,1)S(1)} custom-call(bf16[4,64,768]{2,1,0:T(8,128)(2,1)S(1)} %fusion.37.d_ref, bf16[4,64,768]{2,1,0:T(8,128)(2,1)S(1)} %copy-done.46, bf16[4,320,1536]{2,1,0:T(8,128)(2,1)S(1)} %copy-done.39, f32[4,2,256,320]{3,2,1,0:T(8,128)S(1)} %copy-done.40), custom_call_target="tpu_custom_call" | custom-call | flops 4026531840 | bytes 9830400 | tf_op jit(solution)/shard_map/pallas_call | solution.py:694
  296.2 2.6 convolution_convert_fusion.3
  311.2 3.7 collective-permute-done.46
  314.8 9.5 %collective-permute-done.47 = bf16[48,3072]{1,0:T(8,128)(2,1)S(1)} collective-permute-done((bf16[48,3072]{1,0:T(8,128)(2,1)S(1)}, bf16[48,3072]{1,0:T(8,128)(2,1)S(1)}, u32[]{:S(2)}, u32[]{:S(2)}) %collective-permute-start.47) | collective-permute-done | bytes 294944 | tf_op jit(solution)/shard_map/ppermute | solution.py:86
  324.5 2.6 convolution_convert_fusion
  328.0 2.6 convolution_convert_fusion.1
  330.6 2.6 convolution_convert_fusion.2
  342.4 4.3 collective-permute-done.48
  346.7 7.8 %fusion.6 = bf16[2,320,1536]{2,1,0:T(8,128)(2,1)S(1)} fusion(bf16[4,320,2304]{2,1,0:T(8,128)(2,1)S(1)} %shard_map.286, bf16[1536,2304]{1,0:T(8,128)(2,1)} %get-tuple-element.159), kind=kOutput, calls=%fused_computation.49 | convolution fusion | flops 4530831360 | bytes 14942208 | tf_op jit(solution)/shard_map/dot_general | solution.py:32
  358.5 7.0 %convert_add_fusion = f32[2,320,1536]{2,1,0:T(8,128)S(1)} fusion(bf16[2,320,1536]{2,1,0:T(8,128)(2,1)S(1)} %collective-permute-done.49, bf16[4,320,2304]{2,1,0:T(8,128)(2,1)S(1)} %shard_map.286, bf16[1536,2304]{1,0:T(8,128)(2,1)} %get-tuple-element.159), kind=kOutput, calls=%fused_computation.46 | convolution fusion | flops 4531814400 | bytes 18874368 | tf_op jit(solution)/shard_map/dot_general | solution.py:32
  372.8 2.7 collective-permute-done.53
  378.1 2.4 fusion.167
  389.1 2.7 add_add_fusion.3
  402.1 2.5 collective-permute-done.58
  406.4 5.8 %collective-permute-done.60 = bf16[2,48,3072]{2,1,0:T(8,128)(2,1)S(1)} collective-permute-done((bf16[2,48,3072]{2,1,0:T(8,128)(2,1)S(1)}, bf16[2,48,3072]{2,1,0:T(8,128)(2,1)S(1)}, u32[]{:S(2)}, u32[]{:S(2)}) %collective-permute-start.60) | collective-permute-done | bytes 589856 | tf_op jit(solution)/shard_map/ppermute | solution.py:86
  416.5 5.7 %all-to-all-start.4 = ((f32[32,1,672]{2,1,0:T(1,128)}), f32[32,1,672]{2,1,0:T(1,128)S(1)}, u32[]{:S(2)}, u32[]{:S(2)}) async-start(f32[32,1,672]{2,1,0:T(1,128)} %reshape.398), calls=%async_computation.4 | async-start | bytes 196608 | tf_op jit(solution)/shard_map/all_to_all | solution.py:954
  422.2 3.4 convert_reduce_fusion
  431.7 3.5 all-to-all-start.5
  442.5 2.8 all-to-all-done.5.in_ref
  448.5 9.0 %collective-permute-done.63 = bf16[2,48,3072]{2,1,0:T(8,128)(2,1)} collective-permute-done((bf16[2,48,3072]{2,1,0:T(8,128)(2,1)}, bf16[2,48,3072]{2,1,0:T(8,128)(2,1)}, u32[]{:S(2)}, u32[]{:S(2)}) %collective-permute-start.63) | collective-permute-done | bytes 589856 | tf_op jit(solution)/shard_map/ppermute | solution.py:86
  (520 shorter events, 206.1 us)
Async XLA Ops:
  4.9 44.4 %collective-permute-start.5 = (bf16[2,64,1536]{2,1,0:T(8,128)(2,1)S(1)}, bf16[2,64,1536]{2,1,0:T(8,128)(2,1)}, u32[]{:S(2)}, u32[]{:S(2)}) collective-permute-start(bf16[2,64,1536]{2,1,0:T(8,128)(2,1)S(1)} %broadcast_multiply_fusion), channel_id=1, source_target_pairs={{0,2},{1,3},{2,0},{3,1},{4,6},{5,7},{6,4},{7,5},{8,10},{9,11},{10,... | collective-permute-start | bytes 1179656 | tf_op jit(solution)/shard_map/ppermute | solution.py:86
  14.7 32.7 %collective-permute-start.3 = (bf16[2,48,2304]{2,1,0:T(8,128)(2,1)S(1)}, bf16[2,48,2304]{2,1,0:T(8,128)(2,1)S(1)}, u32[]{:S(2)}, u32[]{:S(2)}) collective-permute-start(bf16[2,48,2304]{2,1,0:T(8,128)(2,1)S(1)} %maximum_select_fusion.refs_0_), channel_id=1, source_target_pairs={{0,2},{1,3},{2,0},{3,1},{4,6},{5,7},{6,4},{7,5},{8,10},{9,11},{10,... | collective-permute-start | bytes 1327112 | tf_op jit(solution)/shard_map/ppermute | solution.py:86
  15.3 24.2 %collective-permute-start.2 = (bf16[2,48,2304]{2,1,0:T(8,128)(2,1)S(1)}, bf16[2,48,2304]{2,1,0:T(8,128)(2,1)}, u32[]{:S(2)}, u32[]{:S(2)}) collective-permute-start(bf16[2,48,2304]{2,1,0:T(8,128)(2,1)S(1)} %maximum_select_fusion.refs_0_), channel_id=1, source_target_pairs={{0,1},{1,0},{2,3},{3,2},{4,5},{5,4},{6,7},{7,6},{8,9},{9,8},{10,11... | collective-permute-start | bytes 1327112 | tf_op jit(solution)/shard_map/ppermute | solution.py:86
  26.2 22.1 %collective-permute-start.1 = (bf16[144,2304]{1,0:T(8,128)(2,1)}, bf16[144,2304]{1,0:T(8,128)(2,1)}, u32[]{:S(2)}, u32[]{:S(2)}) collective-permute-start(bf16[144,2304]{1,0:T(8,128)(2,1)} %fusion.64), channel_id=1, source_target_pairs={{0,8},{1,9},{2,10},{3,11},{4,12},{5,13},{6,14},{7,15},{8,16},{9,17... | collective-permute-start | bytes 1990664 | tf_op jit(solution)/shard_map/ppermute | solution.py:86
  49.3 16.0 %collective-permute-start.8 = (bf16[2,48,2304]{2,1,0:T(8,128)(2,1)S(1)}, bf16[2,48,2304]{2,1,0:T(8,128)(2,1)S(1)}, u32[]{:S(2)}, u32[]{:S(2)}) collective-permute-start(bf16[2,48,2304]{2,1,0:T(8,128)(2,1)S(1)} %bitcast.363), channel_id=1, source_target_pairs={{0,2},{1,3},{2,0},{3,1},{4,6},{5,7},{6,4},{7,5},{8,10},{9,11},{10,... | collective-permute-start | bytes 1327112 | tf_op jit(solution)/shard_map/ppermute | solution.py:86
  51.3 14.8 %collective-permute-start.7 = (bf16[2,48,2304]{2,1,0:T(8,128)(2,1)S(1)}, bf16[2,48,2304]{2,1,0:T(8,128)(2,1)}, u32[]{:S(2)}, u32[]{:S(2)}) collective-permute-start(bf16[2,48,2304]{2,1,0:T(8,128)(2,1)S(1)} %bitcast.364), channel_id=1, source_target_pairs={{0,1},{1,0},{2,3},{3,2},{4,5},{5,4},{6,7},{7,6},{8,9},{9,8},{10,11... | collective-permute-start | bytes 1327112 | tf_op jit(solution)/shard_map/ppermute | solution.py:86
  52.7 20.0 %collective-permute-start.9 = (bf16[48,2304]{1,0:T(8,128)(2,1)}, bf16[48,2304]{1,0:T(8,128)(2,1)S(1)}, u32[]{:S(2)}, u32[]{:S(2)}) collective-permute-start(bf16[48,2304]{1,0:T(8,128)(2,1)} %slice_bitcast_fusion.9), channel_id=1, source_target_pairs={{0,2},{1,3},{2,0},{3,1},{4,6},{5,7},{6,4},{7,5},{8,10},{9,11},{10,... | collective-permute-start | bytes 663560 | tf_op jit(solution)/shard_map/ppermute | solution.py:86
  53.3 19.4 %collective-permute-start.10 = (bf16[48,2304]{1,0:T(8,128)(2,1)}, bf16[48,2304]{1,0:T(8,128)(2,1)}, u32[]{:S(2)}, u32[]{:S(2)}) collective-permute-start(bf16[48,2304]{1,0:T(8,128)(2,1)} %slice_bitcast_fusion.8), channel_id=1, source_target_pairs={{0,1},{1,0},{2,3},{3,2},{4,5},{5,4},{6,7},{7,6},{8,9},{9,8},{10,11... | collective-permute-start | bytes 663560 | tf_op jit(solution)/shard_map/ppermute | solution.py:86
  53.4 18.2 %collective-permute-start.6 = (bf16[144,2304]{1,0:T(8,128)(2,1)}, bf16[144,2304]{1,0:T(8,128)(2,1)}, u32[]{:S(2)}, u32[]{:S(2)}) collective-permute-start(bf16[144,2304]{1,0:T(8,128)(2,1)} %collective-permute-done.1), channel_id=1, source_target_pairs={{0,8},{1,9},{2,10},{3,11},{4,12},{5,13},{6,14},{7,15},{8,16},{9,17... | collective-permute-start | bytes 1990664 | tf_op jit(solution)/shard_map/ppermute | solution.py:86
  74.4 26.7 %collective-permute-start.12 = (bf16[2,48,2304]{2,1,0:T(8,128)(2,1)S(1)}, bf16[2,48,2304]{2,1,0:T(8,128)(2,1)}, u32[]{:S(2)}, u32[]{:S(2)}) collective-permute-start(bf16[2,48,2304]{2,1,0:T(8,128)(2,1)S(1)} %bitcast.367), channel_id=1, source_target_pairs={{0,1},{1,0},{2,3},{3,2},{4,5},{5,4},{6,7},{7,6},{8,9},{9,8},{10,11... | collective-permute-start | bytes 1327112 | tf_op jit(solution)/shard_map/ppermute | solution.py:86
  75.9 27.3 %collective-permute-start.14 = (bf16[48,2304]{1,0:T(8,128)(2,1)}, bf16[48,2304]{1,0:T(8,128)(2,1)}, u32[]{:S(2)}, u32[]{:S(2)}) collective-permute-start(bf16[48,2304]{1,0:T(8,128)(2,1)} %slice_bitcast_fusion.7), channel_id=1, source_target_pairs={{0,2},{1,3},{2,0},{3,1},{4,6},{5,7},{6,4},{7,5},{8,10},{9,11},{10,... | collective-permute-start | bytes 663560 | tf_op jit(solution)/shard_map/ppermute | solution.py:86
  76.4 26.8 %collective-permute-start.15 = (bf16[48,2304]{1,0:T(8,128)(2,1)}, bf16[48,2304]{1,0:T(8,128)(2,1)}, u32[]{:S(2)}, u32[]{:S(2)}) collective-permute-start(bf16[48,2304]{1,0:T(8,128)(2,1)} %slice_bitcast_fusion.6), channel_id=1, source_target_pairs={{0,1},{1,0},{2,3},{3,2},{4,5},{5,4},{6,7},{7,6},{8,9},{9,8},{10,11... | collective-permute-start | bytes 663560 | tf_op jit(solution)/shard_map/ppermute | solution.py:86
  76.9 16.2 %collective-permute-start.11 = (bf16[144,2304]{1,0:T(8,128)(2,1)}, bf16[144,2304]{1,0:T(8,128)(2,1)}, u32[]{:S(2)}, u32[]{:S(2)}) collective-permute-start(bf16[144,2304]{1,0:T(8,128)(2,1)} %collective-permute-done.6), channel_id=1, source_target_pairs={{0,8},{1,9},{2,10},{3,11},{4,12},{5,13},{6,14},{7,15},{8,16},{9,17... | collective-permute-start | bytes 1990664 | tf_op jit(solution)/shard_map/ppermute | solution.py:86
  95.5 106.7 %all-to-all-start.2 = ((bf16[4,384,1536]{2,1,0:T(8,128)(2,1)}), bf16[4,384,1536]{2,1,0:T(8,128)(2,1)}, u32[]{:S(2)}, u32[]{:S(2)}) async-start(bf16[4,384,1536]{2,1,0:T(8,128)(2,1)} %broadcast_in_dim.35), calls=%async_computation.2 | async-start | bytes 9437184 | tf_op jit(solution)/shard_map/all_to_all | solution.py:89
  104.7 18.8 %collective-permute-start.16 = (bf16[2,48,2304]{2,1,0:T(8,128)(2,1)S(1)}, bf16[2,48,2304]{2,1,0:T(8,128)(2,1)S(1)}, u32[]{:S(2)}, u32[]{:S(2)}) collective-permute-start(bf16[2,48,2304]{2,1,0:T(8,128)(2,1)S(1)} %bitcast.370), channel_id=1, source_target_pairs={{0,1},{1,0},{2,3},{3,2},{4,5},{5,4},{6,7},{7,6},{8,9},{9,8},{10,11... | collective-permute-start | bytes 1327112 | tf_op jit(solution)/shard_map/ppermute | solution.py:86
  106.1 17.3 %collective-permute-start.18 = (bf16[48,2304]{1,0:T(8,128)(2,1)S(1)}, bf16[48,2304]{1,0:T(8,128)(2,1)S(1)}, u32[]{:S(2)}, u32[]{:S(2)}) collective-permute-start(bf16[48,2304]{1,0:T(8,128)(2,1)S(1)} %slice_bitcast_fusion.5), channel_id=1, source_target_pairs={{0,2},{1,3},{2,0},{3,1},{4,6},{5,7},{6,4},{7,5},{8,10},{9,11},{10,... | collective-permute-start | bytes 663560 | tf_op jit(solution)/shard_map/ppermute | solution.py:86
  106.7 16.8 %collective-permute-start.19 = (bf16[48,2304]{1,0:T(8,128)(2,1)}, bf16[48,2304]{1,0:T(8,128)(2,1)S(1)}, u32[]{:S(2)}, u32[]{:S(2)}) collective-permute-start(bf16[48,2304]{1,0:T(8,128)(2,1)} %slice_bitcast_fusion.4), channel_id=1, source_target_pairs={{0,1},{1,0},{2,3},{3,2},{4,5},{5,4},{6,7},{7,6},{8,9},{9,8},{10,11... | collective-permute-start | bytes 663560 | tf_op jit(solution)/shard_map/ppermute | solution.py:86
  107.4 29.3 %collective-permute-start.25 = (bf16[2,320,1536]{2,1,0:T(8,128)(2,1)S(1)}, bf16[2,320,1536]{2,1,0:T(8,128)(2,1)S(1)}, u32[]{:S(2)}, u32[]{:S(2)}) collective-permute-start(bf16[2,320,1536]{2,1,0:T(8,128)(2,1)S(1)} %pad_maximum_fusion.2.refs_20_), channel_id=1, source_target_pairs={{0,4},{1,5},{2,6},{3,7},{4,0},{5,1},{6,2},{7,3},{8,12},{9,13},{10,... | collective-permute-start | bytes 5898248 | tf_op jit(solution)/shard_map/ppermute | solution.py:86
  115.9 46.7 %collective-permute-start.26 = (bf16[2,64,1536]{2,1,0:T(8,128)(2,1)}, bf16[2,64,1536]{2,1,0:T(8,128)(2,1)S(1)}, u32[]{:S(2)}, u32[]{:S(2)}) collective-permute-start(bf16[2,64,1536]{2,1,0:T(8,128)(2,1)} %copy-done.11), channel_id=1, source_target_pairs={{0,3},{1,2},{2,1},{3,0},{4,7},{5,6},{6,5},{7,4},{8,11},{9,10},{10,... | collective-permute-start | bytes 1179656 | tf_op jit(solution)/shard_map/ppermute | solution.py:86
  126.4 36.3 %collective-permute-start.22 = (bf16[4,48,1536]{2,1,0:T(8,128)(2,1)S(1)}, bf16[4,48,1536]{2,1,0:T(8,128)(2,1)S(1)}, u32[]{:S(2)}, u32[]{:S(2)}) collective-permute-start(bf16[4,48,1536]{2,1,0:T(8,128)(2,1)S(1)} %pad_maximum_fusion.6.refs_0_), channel_id=1, source_target_pairs={{0,1},{1,0},{2,3},{3,2},{4,5},{5,4},{6,7},{7,6},{8,9},{9,8},{10,11... | collective-permute-start | bytes 1769480 | tf_op jit(solution)/shard_map/ppermute | solution.py:86
  133.8 28.9 %collective-permute-start.21 = (bf16[4,48,1536]{2,1,0:T(8,128)(2,1)S(1)}, bf16[4,48,1536]{2,1,0:T(8,128)(2,1)S(1)}, u32[]{:S(2)}, u32[]{:S(2)}) collective-permute-start(bf16[4,48,1536]{2,1,0:T(8,128)(2,1)S(1)} %pad_maximum_fusion.6.refs_0_), channel_id=1, source_target_pairs={{0,2},{1,3},{2,0},{3,1},{4,6},{5,7},{6,4},{7,5},{8,10},{9,11},{10,... | collective-permute-start | bytes 1769480 | tf_op jit(solution)/shard_map/ppermute | solution.py:86
  135.2 28.3 %collective-permute-start.20 = (bf16[4,48,1536]{2,1,0:T(8,128)(2,1)S(1)}, bf16[4,48,1536]{2,1,0:T(8,128)(2,1)S(1)}, u32[]{:S(2)}, u32[]{:S(2)}) collective-permute-start(bf16[4,48,1536]{2,1,0:T(8,128)(2,1)S(1)} %pad_maximum_fusion.6.refs_0_), channel_id=1, source_target_pairs={{0,3},{1,2},{2,1},{3,0},{4,7},{5,6},{6,5},{7,4},{8,11},{9,10},{10,... | collective-permute-start | bytes 1769480 | tf_op jit(solution)/shard_map/ppermute | solution.py:86
  177.8 19.0 %collective-permute-start.31 = (bf16[2,64,1536]{2,1,0:T(8,128)(2,1)S(1)}, bf16[2,64,1536]{2,1,0:T(8,128)(2,1)S(1)}, u32[]{:S(2)}, u32[]{:S(2)}) collective-permute-start(bf16[2,64,1536]{2,1,0:T(8,128)(2,1)S(1)} %add_convert_fusion.5), channel_id=1, source_target_pairs={{0,2},{1,3},{2,0},{3,1},{4,6},{5,7},{6,4},{7,5},{8,10},{9,11},{10,... | collective-permute-start | bytes 1179656 | tf_op jit(solution)/shard_map/ppermute | solution.py:86
  179.0 17.9 %collective-permute-start.30 = (bf16[2,64,1536]{2,1,0:T(8,128)(2,1)S(1)}, bf16[2,64,1536]{2,1,0:T(8,128)(2,1)S(1)}, u32[]{:S(2)}, u32[]{:S(2)}) collective-permute-start(bf16[2,64,1536]{2,1,0:T(8,128)(2,1)S(1)} %add_convert_fusion.5), channel_id=1, source_target_pairs={{0,1},{1,0},{2,3},{3,2},{4,5},{5,4},{6,7},{7,6},{8,9},{9,8},{10,11... | collective-permute-start | bytes 1179656 | tf_op jit(solution)/shard_map/ppermute | solution.py:86
  180.0 18.0 %collective-permute-start.28 = (bf16[1,2,64,1536]{3,2,1,0:T(8,128)(2,1)S(1)}, bf16[1,2,64,1536]{3,2,1,0:T(8,128)(2,1)S(1)}, u32[]{:S(2)}, u32[]{:S(2)}) collective-permute-start(bf16[1,2,64,1536]{3,2,1,0:T(8,128)(2,1)S(1)} %fusion.189), channel_id=1, source_target_pairs={{0,4},{1,5},{2,6},{3,7},{4,0},{5,1},{6,2},{7,3},{8,12},{9,13},{10,... | collective-permute-start | bytes 1179656 | tf_op jit(solution)/shard_map/ppermute | solution.py:86
  180.1 18.7 %collective-permute-start.29 = (bf16[1,2,64,1536]{3,2,1,0:T(8,128)(2,1)S(1)}, bf16[1,2,64,1536]{3,2,1,0:T(8,128)(2,1)S(1)}, u32[]{:S(2)}, u32[]{:S(2)}) collective-permute-start(bf16[1,2,64,1536]{3,2,1,0:T(8,128)(2,1)S(1)} %bitcast.372), channel_id=1, source_target_pairs={{0,4},{1,5},{2,6},{3,7},{4,0},{5,1},{6,2},{7,3},{8,12},{9,13},{10,... | collective-permute-start | bytes 1179656 | tf_op jit(solution)/shard_map/ppermute | solution.py:86
  189.2 22.8 %collective-permute-start.34 = (bf16[3,2,64,1536]{3,2,1,0:T(8,128)(2,1)S(1)}, bf16[3,2,64,1536]{3,2,1,0:T(8,128)(2,1)}, u32[]{:S(2)}, u32[]{:S(2)}) collective-permute-start(bf16[3,2,64,1536]{3,2,1,0:T(8,128)(2,1)S(1)} %pad_maximum_fusion.4), channel_id=1, source_target_pairs={{0,4},{1,5},{2,6},{3,7},{4,0},{5,1},{6,2},{7,3},{8,12},{9,13},{10,... | collective-permute-start | bytes 3538952 | tf_op jit(solution)/shard_map/ppermute | solution.py:86
  240.1 27.5 %collective-permute-start.39 = (bf16[2,64,1536]{2,1,0:T(8,128)(2,1)}, bf16[2,64,1536]{2,1,0:T(8,128)(2,1)}, u32[]{:S(2)}, u32[]{:S(2)}) collective-permute-start(bf16[2,64,1536]{2,1,0:T(8,128)(2,1)} %bitcast.98), channel_id=1, source_target_pairs={{0,1},{1,0},{2,3},{3,2},{4,5},{5,4},{6,7},{7,6},{8,9},{9,8},{10,11... | collective-permute-start | bytes 1179656 | tf_op jit(solution)/shard_map/ppermute | solution.py:86
  240.6 27.0 %collective-permute-start.38 = (bf16[2,64,1536]{2,1,0:T(8,128)(2,1)}, bf16[2,64,1536]{2,1,0:T(8,128)(2,1)}, u32[]{:S(2)}, u32[]{:S(2)}) collective-permute-start(bf16[2,64,1536]{2,1,0:T(8,128)(2,1)} %bitcast.97), channel_id=1, source_target_pairs={{0,2},{1,3},{2,0},{3,1},{4,6},{5,7},{6,4},{7,5},{8,10},{9,11},{10,... | collective-permute-start | bytes 1179656 | tf_op jit(solution)/shard_map/ppermute | solution.py:86
  262.4 153.2 %all-to-all-start.3 = ((bf16[4,384,1536]{2,1,0:T(8,128)(2,1)}), bf16[4,384,1536]{2,1,0:T(8,128)(2,1)}, u32[]{:S(2)}, u32[]{:S(2)}) async-start(bf16[4,384,1536]{2,1,0:T(8,128)(2,1)} %maximum_maximum_fusion), calls=%async_computation.3 | async-start | bytes 9437184 | tf_op jit(solution)/shard_map/all_to_all | solution.py:89
  283.5 17.1 %collective-permute-start.40 = (bf16[128,1536]{1,0:T(8,128)(2,1)}, bf16[128,1536]{1,0:T(8,128)(2,1)S(1)}, u32[]{:S(2)}, u32[]{:S(2)}) collective-permute-start(bf16[128,1536]{1,0:T(8,128)(2,1)} %split.53), channel_id=1, source_target_pairs={{0,4},{1,5},{2,6},{3,7},{4,0},{5,1},{6,2},{7,3},{8,12},{9,13},{10,... | collective-permute-start | bytes 1179656 | tf_op jit(solution)/shard_map/ppermute | solution.py:86
  284.0 18.9 %collective-permute-start.41 = (bf16[384,1536]{1,0:T(8,128)(2,1)}, bf16[384,1536]{1,0:T(8,128)(2,1)S(1)}, u32[]{:S(2)}, u32[]{:S(2)}) collective-permute-start(bf16[384,1536]{1,0:T(8,128)(2,1)} %split.55), channel_id=1, source_target_pairs={{0,4},{1,5},{2,6},{3,7},{4,0},{5,1},{6,2},{7,3},{8,12},{9,13},{10,... | collective-permute-start | bytes 3538952 | tf_op jit(solution)/shard_map/ppermute | solution.py:86
  306.1 18.3 %collective-permute-start.47 = (bf16[48,3072]{1,0:T(8,128)(2,1)S(1)}, bf16[48,3072]{1,0:T(8,128)(2,1)S(1)}, u32[]{:S(2)}, u32[]{:S(2)}) collective-permute-start(bf16[48,3072]{1,0:T(8,128)(2,1)S(1)} %get-tuple-element.156), channel_id=1, source_target_pairs={{0,2},{1,3},{2,0},{3,1},{4,6},{5,7},{6,4},{7,5},{8,10},{9,11},{10,... | collective-permute-start | bytes 884744 | tf_op jit(solution)/shard_map/ppermute | solution.py:86
  307.6 30.1 %collective-permute-start.44 = (bf16[2,64,1536]{2,1,0:T(8,128)(2,1)S(1)}, bf16[2,64,1536]{2,1,0:T(8,128)(2,1)S(1)}, u32[]{:S(2)}, u32[]{:S(2)}) collective-permute-start(bf16[2,64,1536]{2,1,0:T(8,128)(2,1)S(1)} %bitcast.410), channel_id=1, source_target_pairs={{0,2},{1,3},{2,0},{3,1},{4,6},{5,7},{6,4},{7,5},{8,10},{9,11},{10,... | collective-permute-start | bytes 1179656 | tf_op jit(solution)/shard_map/ppermute | solution.py:86
  308.2 29.5 %collective-permute-start.43 = (bf16[2,64,1536]{2,1,0:T(8,128)(2,1)S(1)}, bf16[2,64,1536]{2,1,0:T(8,128)(2,1)S(1)}, u32[]{:S(2)}, u32[]{:S(2)}) collective-permute-start(bf16[2,64,1536]{2,1,0:T(8,128)(2,1)S(1)} %bitcast.409), channel_id=1, source_target_pairs={{0,3},{1,2},{2,1},{3,0},{4,7},{5,6},{6,5},{7,4},{8,11},{9,10},{10,... | collective-permute-start | bytes 1179656 | tf_op jit(solution)/shard_map/ppermute | solution.py:86
  309.7 28.0 %collective-permute-start.45 = (bf16[2,64,1536]{2,1,0:T(8,128)(2,1)S(1)}, bf16[2,64,1536]{2,1,0:T(8,128)(2,1)S(1)}, u32[]{:S(2)}, u32[]{:S(2)}) collective-permute-start(bf16[2,64,1536]{2,1,0:T(8,128)(2,1)S(1)} %bitcast.408), channel_id=1, source_target_pairs={{0,1},{1,0},{2,3},{3,2},{4,5},{5,4},{6,7},{7,6},{8,9},{9,8},{10,11... | collective-permute-start | bytes 1179656 | tf_op jit(solution)/shard_map/ppermute | solution.py:86
  338.8 26.8 %collective-permute-start.50 = (bf16[2,48,3072]{2,1,0:T(8,128)(2,1)S(1)}, bf16[2,48,3072]{2,1,0:T(8,128)(2,1)S(1)}, u32[]{:S(2)}, u32[]{:S(2)}) collective-permute-start(bf16[2,48,3072]{2,1,0:T(8,128)(2,1)S(1)} %fusion.66), channel_id=1, source_target_pairs={{0,1},{1,0},{2,3},{3,2},{4,5},{5,4},{6,7},{7,6},{8,9},{9,8},{10,11... | collective-permute-start | bytes 1769480 | tf_op jit(solution)/shard_map/ppermute | solution.py:86
  339.9 25.6 %collective-permute-start.51 = (bf16[2,48,3072]{2,1,0:T(8,128)(2,1)S(1)}, bf16[2,48,3072]{2,1,0:T(8,128)(2,1)S(1)}, u32[]{:S(2)}, u32[]{:S(2)}) collective-permute-start(bf16[2,48,3072]{2,1,0:T(8,128)(2,1)S(1)} %pad_maximum_fusion.7), channel_id=1, source_target_pairs={{0,2},{1,3},{2,0},{3,1},{4,6},{5,7},{6,4},{7,5},{8,10},{9,11},{10,... | collective-permute-start | bytes 1769480 | tf_op jit(solution)/shard_map/ppermute | solution.py:86
  367.6 14.7 %collective-permute-start.57 = (bf16[48,3072]{1,0:T(8,128)(2,1)}, bf16[48,3072]{1,0:T(8,128)(2,1)}, u32[]{:S(2)}, u32[]{:S(2)}) collective-permute-start(bf16[48,3072]{1,0:T(8,128)(2,1)} %get-tuple-element.169), channel_id=1, source_target_pairs={{0,2},{1,3},{2,0},{3,1},{4,6},{5,7},{6,4},{7,5},{8,10},{9,11},{10,... | collective-permute-start | bytes 884744 | tf_op jit(solution)/shard_map/ppermute | solution.py:86
  368.7 23.0 %collective-permute-start.54 = (bf16[2,48,3072]{2,1,0:T(8,128)(2,1)}, bf16[2,48,3072]{2,1,0:T(8,128)(2,1)}, u32[]{:S(2)}, u32[]{:S(2)}) collective-permute-start(bf16[2,48,3072]{2,1,0:T(8,128)(2,1)} %add_convert_fusion.4), channel_id=1, source_target_pairs={{0,8},{1,9},{2,10},{3,11},{4,12},{5,13},{6,14},{7,15},{8,16},{9,17... | collective-permute-start | bytes 1769480 | tf_op jit(solution)/shard_map/ppermute | solution.py:86
  370.8 21.0 %collective-permute-start.55 = (bf16[2,48,3072]{2,1,0:T(8,128)(2,1)}, bf16[2,48,3072]{2,1,0:T(8,128)(2,1)}, u32[]{:S(2)}, u32[]{:S(2)}) collective-permute-start(bf16[2,48,3072]{2,1,0:T(8,128)(2,1)} %fusion.68), channel_id=1, source_target_pairs={{0,1},{1,0},{2,3},{3,2},{4,5},{5,4},{6,7},{7,6},{8,9},{9,8},{10,11... | collective-permute-start | bytes 1769480 | tf_op jit(solution)/shard_map/ppermute | solution.py:86
  372.2 19.5 %collective-permute-start.56 = (bf16[2,48,3072]{2,1,0:T(8,128)(2,1)}, bf16[2,48,3072]{2,1,0:T(8,128)(2,1)}, u32[]{:S(2)}, u32[]{:S(2)}) collective-permute-start(bf16[2,48,3072]{2,1,0:T(8,128)(2,1)} %pad_maximum_fusion.8), channel_id=1, source_target_pairs={{0,2},{1,3},{2,0},{3,1},{4,6},{5,7},{6,4},{7,5},{8,10},{9,11},{10,... | collective-permute-start | bytes 1769480 | tf_op jit(solution)/shard_map/ppermute | solution.py:86
  395.7 16.5 %collective-permute-start.60 = (bf16[2,48,3072]{2,1,0:T(8,128)(2,1)S(1)}, bf16[2,48,3072]{2,1,0:T(8,128)(2,1)S(1)}, u32[]{:S(2)}, u32[]{:S(2)}) collective-permute-start(bf16[2,48,3072]{2,1,0:T(8,128)(2,1)S(1)} %copy-done.78), channel_id=1, source_target_pairs={{0,1},{1,0},{2,3},{3,2},{4,5},{5,4},{6,7},{7,6},{8,9},{9,8},{10,11... | collective-permute-start | bytes 1769480 | tf_op jit(solution)/shard_map/ppermute | solution.py:86
  397.2 17.3 %collective-permute-start.61 = (bf16[2,48,3072]{2,1,0:T(8,128)(2,1)S(1)}, bf16[2,48,3072]{2,1,0:T(8,128)(2,1)S(1)}, u32[]{:S(2)}, u32[]{:S(2)}) collective-permute-start(bf16[2,48,3072]{2,1,0:T(8,128)(2,1)S(1)} %copy-done.77), channel_id=1, source_target_pairs={{0,2},{1,3},{2,0},{3,1},{4,6},{5,7},{6,4},{7,5},{8,10},{9,11},{10,... | collective-permute-start | bytes 1769480 | tf_op jit(solution)/shard_map/ppermute | solution.py:86
  397.7 16.8 %collective-permute-start.59 = (bf16[2,48,3072]{2,1,0:T(8,128)(2,1)S(1)}, bf16[2,48,3072]{2,1,0:T(8,128)(2,1)S(1)}, u32[]{:S(2)}, u32[]{:S(2)}) collective-permute-start(bf16[2,48,3072]{2,1,0:T(8,128)(2,1)S(1)} %add_convert_fusion.3), channel_id=1, source_target_pairs={{0,8},{1,9},{2,10},{3,11},{4,12},{5,13},{6,14},{7,15},{8,16},{9,17... | collective-permute-start | bytes 1769480 | tf_op jit(solution)/shard_map/ppermute | solution.py:86
  435.3 22.2 %collective-permute-start.63 = (bf16[2,48,3072]{2,1,0:T(8,128)(2,1)}, bf16[2,48,3072]{2,1,0:T(8,128)(2,1)}, u32[]{:S(2)}, u32[]{:S(2)}) collective-permute-start(bf16[2,48,3072]{2,1,0:T(8,128)(2,1)} %fusion.70), channel_id=1, source_target_pairs={{0,1},{1,0},{2,3},{3,2},{4,5},{5,4},{6,7},{7,6},{8,9},{9,8},{10,11... | collective-permute-start | bytes 1769480 | tf_op jit(solution)/shard_map/ppermute | solution.py:86
  437.2 20.3 %collective-permute-start.64 = (bf16[2,48,3072]{2,1,0:T(8,128)(2,1)}, bf16[2,48,3072]{2,1,0:T(8,128)(2,1)}, u32[]{:S(2)}, u32[]{:S(2)}) collective-permute-start(bf16[2,48,3072]{2,1,0:T(8,128)(2,1)} %pad_maximum_fusion.11), channel_id=1, source_target_pairs={{0,2},{1,3},{2,0},{3,1},{4,6},{5,7},{6,4},{7,5},{8,10},{9,11},{10,... | collective-permute-start | bytes 1769480 | tf_op jit(solution)/shard_map/ppermute | solution.py:86
  438.7 18.9 %collective-permute-start.65 = (bf16[2,48,3072]{2,1,0:T(8,128)(2,1)}, bf16[2,48,3072]{2,1,0:T(8,128)(2,1)}, u32[]{:S(2)}, u32[]{:S(2)}) collective-permute-start(bf16[2,48,3072]{2,1,0:T(8,128)(2,1)} %add_convert_fusion.2), channel_id=1, source_target_pairs={{0,8},{1,9},{2,10},{3,11},{4,12},{5,13},{6,14},{7,15},{8,16},{9,17... | collective-permute-start | bytes 1769480 | tf_op jit(solution)/shard_map/ppermute | solution.py:86
  (149 other events, 1330.3 us)

commit v3 on v2

--- a/solution.py
+++ b/solution.py
@@ -15,6 +15,7 @@
 WIDE = jnp.float32
 HIGHEST = lax.Precision.HIGHEST
 NORM_EPS = 1e-05
+BRIEF = pl.CostEstimate(flops=1, bytes_accessed=1, transcendentals=0)
 
 
 def norm_rows(inputs, gain, shift):
@@ -118,14 +119,14 @@
     return mask & -mask, 1 << (mask.bit_length() - 1)
 
 
-def gather_rows(wires, block, take, guest, hooks):
-    rings, gathered, before, guests = [block], [], (), {0: guest}
+def gather_rows(wires, block, take, guest, hooks, before):
+    rings, gathered, guests = [block], [], {0: guest}
     single = [mask for mask in wires.masks if not mask & (mask - 1)]
     multiple = sorted((m for m in wires.masks if m & (m - 1)), key=lambda m: bin(m).count("1"))
     steps = []
     for step in range(wires.deep + 1):
         now = []
-        before = (*before, *(hooks[step](guests) if step in hooks else ()))
+        before = (*before, *(hooks[step](gathered[0]) if step in hooks else ()))
         if step < wires.deep:
             if step + 1 < wires.deep:
                 rings.append(wires.send(rings[step], "rise", *before))
@@ -136,9 +137,9 @@
                 got[mask] = wires.send(mine, mask, *before)
                 now.append(got[mask])
             gathered.append(got)
-        for mask in single if step == 0 else multiple if step == wires.deep - 1 else ():
-            guests[mask] = wires.send(guest, mask, *before)
-            if step == 0:
+        if step == 0:
+            for mask in single:
+                guests[mask] = wires.send(guest, mask, *before)
                 now.append(guests[mask])
         if step:
             got = gathered[step - 1]
@@ -154,14 +155,14 @@
     return rings, gathered, guests, steps
 
 
-def scatter_rows(wires, part, pulls):
+def scatter_rows(wires, part, pulls, riders, clocks):
     single = [mask for mask in wires.masks if not mask & (mask - 1)]
     multiple = sorted((m for m in wires.masks if m & (m - 1)), key=lambda m: -bin(m).count("1"))
     extra = [{} for _ in range(wires.deep)]
-    before, total = [None], None
+    before, total, clock = (), None, None
     for step in range(wires.deep + 2):
-        now = []
-        ahead = (*(before if step else ()), *(pulls[step](before[-1]) if step in pulls else ()))
+        now, ready = [], []
+        ahead = (*(before if step else ()), *(pulls[step](clock) if step in pulls else ()))
 
         def term(block, mask, half=None):
             mine = part(block, mask)
@@ -184,17 +185,23 @@
         block = step - 1
         if 0 <= block < wires.deep:
             for mask in single:
-                halves = [term(block, mask, half) for half in range(2)]
-                arrived = wires.send(jnp.stack(halves), mask, *ahead)
+                leaving = jnp.stack([term(block, mask, half) for half in range(2)])
+                ready.append(leaving)
+                arrived = wires.send(leaving, mask, *ahead)
                 extra[block].setdefault((0, None), []).append(arrived)
                 now.append(arrived)
         if step < wires.deep:
             for mask in multiple:
                 low, high = corner(mask)
                 for half, bit in ((0, high), (1, low)):
-                    arrived = wires.send(term(step, mask, half), bit, *ahead)
+                    leaving = term(step, mask, half)
+                    ready.append(leaving)
+                    arrived = wires.send(leaving, bit, *ahead)
                     extra[step].setdefault((mask ^ bit, half), []).append(arrived)
                     now.append(arrived)
+        clock = clocks[step](*ahead, *ready) if step in clocks else now[-1]
+        for rider in riders.get(step, ()):
+            now.append(rider(ahead))
         before = now
 
 
@@ -243,7 +250,7 @@
             pltpu.VMEM((number,) + entry, pieces[0].dtype),
             pltpu.SemaphoreType.DMA((2, number)),
         ],
-        compiler_params=pltpu.CompilerParams(vmem_limit_bytes=16 * 2**20),
+        compiler_params=pltpu.CompilerParams(vmem_limit_bytes=58 * 2**20),
     )(jnp.stack(places).astype(jnp.int32), *pieces)
 
 
@@ -380,10 +387,17 @@
     return (row == column).astype(WIDE).astype(dtype)
 
 
-def attend(places, pieces, own, far, patches, half_width):
+def normed(rows, gain, shift):
+    centered = rows - jnp.mean(rows, axis=-1, keepdims=True)
+    inverse = lax.rsqrt(jnp.mean(centered * centered, axis=-1, keepdims=True) + NORM_EPS)
+    unit = centered * inverse
+    return unit * gain + shift, unit, inverse
+
+
+def attend(places, pieces, own, far, time_rows, norm_rows_of, patches, half_width):
     images, key_rows, model_width = own.shape
+    lat_rows = key_rows - patches
     slots = 2 * images
-    lat_rows = key_rows - patches
     width = 3 * half_width
     places, pieces = joined(places, pieces)
     chunk = PACK * HEAD
@@ -399,7 +413,10 @@
         (
             own_ref,
             far_ref,
+            time_ref,
+            params_ref,
             full_ref,
+            sources_ref,
             query_ref,
             keyval_ref,
             probs_ref,
@@ -408,26 +425,33 @@
             sems,
         ) = refs[len(pieces) :]
         slot = pl.program_id(0)
+        loads = []
+        for i, (k, core) in enumerate(views):
+            source = piece_refs[k] if core is None else piece_refs[k].at[core]
+            start = pl.multiple_of(places_ref[i] * shard, shard)
+            loads.append(pltpu.make_async_copy(source, w_ref.at[pl.ds(start, shard)], sems.at[i]))
+
+        @pl.when(slot == 0)
+        def _():
+            for load in loads:
+                load.start()
 
         def save():
             return pltpu.make_async_copy(w_ref, full_ref, sems.at[len(views)])
 
+        raw = jnp.where(slot < images, own_ref[0], far_ref[0]).astype(WIDE)
+        media = raw[:patches] + time_ref[0]
+        sources_ref[0, :patches] = normed(media, params_ref[0:1], params_ref[1:2])[0].astype(LOW)
+        lat = normed(raw[patches:], params_ref[2:3], params_ref[3:4])[0]
+        sources_ref[0, patches:] = lat.astype(LOW)
+
         @pl.when(slot == 0)
         def _():
-            loads = []
-            for i, (k, core) in enumerate(views):
-                source = piece_refs[k] if core is None else piece_refs[k].at[core]
-                start = pl.multiple_of(places_ref[i] * shard, shard)
-                loads.append(
-                    pltpu.make_async_copy(source, w_ref.at[pl.ds(start, shard)], sems.at[i])
-                )
-            for load in loads:
-                load.start()
             for load in loads:
                 load.wait()
             save().start()
 
-        x = jnp.where(slot < images, own_ref[0], far_ref[0])
+        x = sources_ref[0]
         mask_low, mask_wide = head_mask(lat_rows, LOW), head_mask(lat_rows, WIDE)
 
         def project(rows, part):
@@ -454,15 +478,22 @@
             save().wait()
 
     anywhere = pl.BlockSpec(memory_space=pl.ANY)
+    whole = pl.BlockSpec(memory_space=pltpu.VMEM)
 
     def slotted(*block):
         return pl.BlockSpec((1, *block), lambda i: (i,) + (0,) * len(block))
+
+    def halved(first, *block):
+        if first:
+            return pl.BlockSpec((1, *block), lambda i: (jnp.minimum(i, images - 1), 0, 0))
+        return pl.BlockSpec((1, *block), lambda i: (jnp.maximum(i - images, 0), 0, 0))
 
     return pl.pallas_call(
         kernel,
         grid=(slots,),
         out_shape=(
             jax.ShapeDtypeStruct((model_width, width), LOW),
+            jax.ShapeDtypeStruct((slots, key_rows, model_width), LOW),
             jax.ShapeDtypeStruct((slots, lat_rows, half_width), LOW),
             jax.ShapeDtypeStruct((slots, key_rows, 2 * half_width), LOW),
             jax.ShapeDtypeStruct((slots, groups, PACK * lat_rows, key_rows), WIDE),
@@ -471,11 +502,14 @@
         in_specs=[pl.BlockSpec(memory_space=pltpu.SMEM)]
         + [anywhere] * len(pieces)
         + [
-            pl.BlockSpec((1, key_rows, model_width), lambda i: (jnp.minimum(i, images - 1), 0, 0)),
-            pl.BlockSpec((1, key_rows, model_width), lambda i: (jnp.maximum(i - images, 0), 0, 0)),
+            halved(True, key_rows, model_width),
+            halved(False, key_rows, model_width),
+            slotted(1, model_width),
+            whole,
         ],
         out_specs=(
             anywhere,
+            slotted(key_rows, model_width),
             slotted(lat_rows, half_width),
             slotted(key_rows, 2 * half_width),
             slotted(groups, PACK * lat_rows, key_rows),
@@ -485,13 +519,72 @@
             pltpu.VMEM((model_width, width), LOW),
             pltpu.SemaphoreType.DMA((len(views) + 1,)),
         ],
-        compiler_params=pltpu.CompilerParams(vmem_limit_bytes=40 * 2**20),
-        cost_estimate=pl.CostEstimate(
-            flops=2 * slots * key_rows * model_width * width,
-            bytes_accessed=4 * model_width * width,
-            transcendentals=0,
+        compiler_params=pltpu.CompilerParams(vmem_limit_bytes=58 * 2**20),
+        cost_estimate=BRIEF,
+    )(jnp.stack(places).astype(jnp.int32), *pieces, own, far, time_rows[:, None], norm_rows_of)
+
+
+def sources_back(d_projected, projections, far_part, own, time_rows, norm_rows_of, d_middle):
+    images, key_rows, model_width = own.shape
+    lat_rows = d_middle.shape[1]
+    patches = key_rows - lat_rows
+    width = d_projected.shape[-1]
+
+    def kernel(d_ref, w_ref, far_ref, raw_ref, time_ref, params_ref, mid_ref, m_out, l_out, s_out):
+        d = dot(d_ref[0], w_ref[...], ((1,), (1,))) + far_ref[0].astype(WIDE)
+
+        def back(rows, d_rows, gain, shift):
+            _, unit, inverse = normed(rows, gain, shift)
+            scaled = d_rows * gain
+            along = jnp.mean(scaled * unit, axis=-1, keepdims=True)
+            inner = scaled - jnp.mean(scaled, axis=-1, keepdims=True) - unit * along
+            sums = (
+                jnp.sum(d_rows * unit, axis=0, keepdims=True),
+                jnp.sum(d_rows, axis=0, keepdims=True),
+            )
+            return inverse * inner, sums
+
+        rows = raw_ref[0, :patches].astype(WIDE) + time_ref[0]
+        d_media, media_sums = back(rows, d[:patches], params_ref[0:1], params_ref[1:2])
+        m_out[0] = d_media
+        rows = raw_ref[0, patches:].astype(WIDE)
+        d_lat, lat_sums = back(rows, d[patches:], params_ref[2:3], params_ref[3:4])
+        l_out[0] = mid_ref[0] + d_lat
+        total = jnp.sum(d_media, axis=0, keepdims=True)
+        s_out[0] = jnp.concatenate(
+            [total, *media_sums, *lat_sums, jnp.zeros((3, model_width), WIDE)], axis=0
+        )
+
+    whole = pl.BlockSpec(memory_space=pltpu.VMEM)
+
+    def slotted(*block):
+        return pl.BlockSpec((1, *block), lambda i: (i,) + (0,) * len(block))
+
+    return pl.pallas_call(
+        kernel,
+        grid=(images,),
+        out_shape=(
+            jax.ShapeDtypeStruct((images, patches, model_width), WIDE),
+            jax.ShapeDtypeStruct((images, lat_rows, model_width), WIDE),
+            jax.ShapeDtypeStruct((images, 8, model_width), WIDE),
         ),
-    )(jnp.stack(places).astype(jnp.int32), *pieces, own, far)
+        in_specs=[
+            slotted(key_rows, width),
+            whole,
+            slotted(key_rows, model_width),
+            slotted(key_rows, model_width),
+            slotted(1, model_width),
+            whole,
+            slotted(lat_rows, model_width),
+        ],
+        out_specs=(
+            slotted(patches, model_width),
+            slotted(lat_rows, model_width),
+            slotted(8, model_width),
+        ),
+        compiler_params=pltpu.CompilerParams(vmem_limit_bytes=48 * 2**20),
+        cost_estimate=BRIEF,
+    )(d_projected, projections, far_part, own, time_rows[:, None], norm_rows_of, d_middle)
 
 
 def project_out(places, pieces, mixed, model_width):
@@ -541,6 +634,7 @@
             pltpu.SemaphoreType.DMA((len(views) + 1,)),
         ],
         compiler_params=pltpu.CompilerParams(vmem_limit_bytes=16 * 2**20),
+        cost_estimate=BRIEF,
     )(jnp.stack(places).astype(jnp.int32), *pieces, mixed)
     return full, branch.reshape(slots, lat_rows, model_width)
 
@@ -591,13 +685,13 @@
                     moves.append(
                         (
                             ffn_ref.at[z, pl.ds(unit, unit), pl.ds(fold * hidden_units, hidden_units)],
-                            up_ref.at[pl.ds((folds * z + fold) * unit, unit)],
+                            up_ref.at[pl.ds((z * folds + fold) * unit, unit)],
                         )
                     )
         return [pltpu.make_async_copy(*move, sems.at[i]) for i, move in enumerate(moves)]
 
     def kernel(x0, x1, d0, d1, *refs):
-        weight_refs, (hidden0, hidden1, pre0, pre1, in0, in1, up_ref, down_ref, sems) = (
+        weight_refs, (hidden0, hidden1, pre0, pre1, in0, in1, out0, out1, up_ref, down_ref, sems) = (
             refs[: len(weights)],
             refs[len(weights) :],
         )
@@ -618,18 +712,20 @@
         hidden = (pre * below).astype(LOW)
         d_pre = (d_hidden * (below + pre * density)).astype(LOW)
         d_input = dot(d_pre, up_ref[...], ((1,), (1,)))
-        for side, (hidden_ref, pre_ref, in_ref) in enumerate(
-            ((hidden0, pre0, in0), (hidden1, pre1, in1))
+        out = jnp.dot(hidden, down_ref[...], preferred_element_type=WIDE)
+        for side, (hidden_ref, pre_ref, in_ref, out_ref) in enumerate(
+            ((hidden0, pre0, in0, out0), (hidden1, pre1, in1, out1))
         ):
             mine = slice(side * block, (side + 1) * block)
             hidden_ref[...] = hidden[mine]
             pre_ref[...] = d_pre[mine]
             in_ref[...] = d_input[mine].astype(in_ref.dtype)
+            out_ref[...] = out[mine].astype(out_ref.dtype)
 
     wide = pl.BlockSpec((block, model_width), lambda i: (i, 0))
     narrow = pl.BlockSpec((block, hidden_units), lambda i: (i, 0))
     low = jax.ShapeDtypeStruct((rows, hidden_units), LOW)
-    return pl.pallas_call(
+    outs = pl.pallas_call(
         kernel,
         grid=(rows // block,),
         out_shape=(
@@ -639,21 +735,58 @@
             low,
             jax.ShapeDtypeStruct((rows, model_width), WIDE),
             jax.ShapeDtypeStruct((rows, model_width), LOW),
+            jax.ShapeDtypeStruct((rows, model_width), WIDE),
+            jax.ShapeDtypeStruct((rows, model_width), LOW),
         ),
         in_specs=[wide] * 4 + [pl.BlockSpec(memory_space=pl.ANY)] * len(weights),
-        out_specs=(narrow,) * 4 + (wide,) * 2,
+        out_specs=(narrow,) * 4 + (wide,) * 4,
         scratch_shapes=[
             pltpu.VMEM((model_width, hidden_units), LOW),
             pltpu.VMEM((hidden_units, model_width), LOW),
             pltpu.SemaphoreType.DMA(((folds + 1) * deep,)),
         ],
         compiler_params=pltpu.CompilerParams(vmem_limit_bytes=32 * 2**20),
-        cost_estimate=pl.CostEstimate(
-            flops=12 * rows * hidden_units * model_width,
-            bytes_accessed=8 * rows * model_width,
-            transcendentals=0,
-        ),
+        cost_estimate=BRIEF,
     )(*xs, *d_outs, *weights)
+    return outs[0:2], outs[2:4], outs[4:6], outs[6:8]
+
+
+def ffn_outer(xs, d_outs, hidden, d_pre, deep, unit):
+    model_width = xs[0].shape[1]
+    hidden_units = deep * unit
+    folds = model_width // hidden_units
+
+    def kernel(x0, x1, d0, d1, h0, h1, p0, p1, out_ref):
+        def both(left0, right0, left1, right1):
+            total = dot(left0[...], right0[...], ((0,), (0,)))
+            return (total + dot(left1[...], right1[...], ((0,), (0,)))).astype(LOW)
+
+        down = both(h0, d0, h1, d1)
+        for z in range(deep):
+            out_ref[z, :unit] = down[z * unit : (z + 1) * unit]
+        up = both(x0, p0, x1, p1)
+        for z in range(deep):
+            for fold in range(folds):
+                rows = up[(z * folds + fold) * unit : (z * folds + fold + 1) * unit]
+                out_ref[z, unit:, fold * hidden_units : (fold + 1) * hidden_units] = rows
+
+    if not (whole_tiles(unit) and hidden_units % 128 == 0):
+        pairs = ((hidden, d_outs), (xs, d_pre))
+        down, up = (
+            sum(outer(left, right) for left, right in zip(*pair_of, strict=True)).astype(LOW)
+            for pair_of in pairs
+        )
+        down = down.reshape(deep, unit, model_width)
+        return jnp.concatenate([down, fold_up(up.reshape(deep, -1, hidden_units), folds)], axis=1)
+    whole = pl.BlockSpec(memory_space=pltpu.VMEM)
+    return pl.pallas_call(
+        kernel,
+        out_shape=jax.ShapeDtypeStruct((deep, 2 * unit, model_width), LOW),
+        in_specs=[whole] * 8,
+        out_specs=whole,
+        compiler_params=pltpu.CompilerParams(vmem_limit_bytes=56 * 2**20),
+        cost_estimate=BRIEF,
+    )(*xs, *d_outs, *hidden, *d_pre)
 
 
 def attend_back(d_mixed, query, keyval, probs):
@@ -703,11 +836,7 @@
         ],
         out_specs=slotted(key_rows, 3 * half_width),
         compiler_params=pltpu.CompilerParams(vmem_limit_bytes=32 * 2**20),
-        cost_estimate=pl.CostEstimate(
-            flops=16 * slots * groups * PACK * lat_rows * key_rows * chunk,
-            bytes_accessed=10 * slots * key_rows * half_width,
-            transcendentals=0,
-        ),
+        cost_estimate=BRIEF,
     )(d_mixed, query, keyval, probs)
 
 
@@ -743,67 +872,42 @@
 
     qkv_mine, qkv_other = deal_columns(wires.c, (w_query, w_keyval), group)
     qkv_arrived = wires.send(qkv_other, "core")
+    raw = jnp.concatenate([after(media, qkv_other), latents], axis=1)
+    far_raw = wires.send(raw, "core")
     qkv_block = pair(qkv_mine, qkv_arrived, wires.c, 0)
 
     unit = w_down.shape[0]
     hidden_units = deep * unit
     tall, wide = 2 * shard, 3 * half_width
+    folds = model_width // hidden_units
     ring_block = jnp.concatenate(
         [qkv_block.reshape(tall, wide), jnp.pad(w_out, ((0, 0), (0, wide - model_width)))]
     )
+    smalls = jnp.concatenate(
+        [time_table]
+        + [v[None] for v in (media_gain, media_bias, latent_gain, latent_bias, ff_gain, ff_bias)],
+        axis=0,
+    )
+    smalls = jnp.broadcast_to(smalls[None], (count, *smalls.shape))
     made = {}
 
-    def norms(guests):
-        smalls = jnp.concatenate(
-            [time_table]
-            + [
-                v[None]
-                for v in (media_gain, media_bias, latent_gain, latent_bias, ff_gain, ff_bias)
-            ],
-            axis=0,
-        )
-        smalls = jnp.broadcast_to(smalls[None], (count,) + smalls.shape)
-        smalls = lax.all_to_all(after(smalls, guests[wires.bits[0]]), AXES, 0, 0, tiled=True)
-        smalls = smalls.transpose(1, 0, 2).reshape(-1, model_width).astype(WIDE)
-        table_full = smalls[:table_rows]
-        (
-            media_gain_full,
-            media_bias_full,
-            latent_gain_full,
-            latent_bias_full,
-            ff_gain_full,
-            ff_bias_full,
-        ) = [smalls[table_rows + k] for k in range(6)]
-
-        alive = (jnp.arange(images) < live_count[0]).astype(WIDE)
-        live_mask = alive[:, None, None]
-        one_hot = (time_index[:, None] == jnp.arange(table_rows)[None, :]).astype(WIDE)
-        time_rows = jnp.dot(one_hot, table_full, precision=HIGHEST)
-        media_in = media.astype(WIDE) + time_rows[:, None, :]
-        media_normed, media_norm_back = jax.vjp(norm_rows, media_in, media_gain_full, media_bias_full)
-        latents_wide = after(latents, smalls).astype(WIDE)
-        latent_normed, latent_norm_back = jax.vjp(
-            norm_rows, latents_wide, latent_gain_full, latent_bias_full
-        )
-        own_sources = jnp.concatenate([media_normed.astype(LOW), latent_normed.astype(LOW)], axis=1)
-        made.update(
-            ff_gain_full=ff_gain_full,
-            ff_bias_full=ff_bias_full,
-            live_mask=live_mask,
-            one_hot=one_hot,
-            media_norm_back=media_norm_back,
-            latent_norm_back=latent_norm_back,
-            latents_wide=latents_wide,
-            own_sources=own_sources,
-        )
-        return (own_sources,)
+    made["smalls"] = lax.all_to_all(smalls, AXES, 0, 0, tiled=True)
+
+    def swap_up(first):
+        shares = split_units(after(w_up, made["smalls"], first[wires.bits[-1]]), 2 * flat, unit)
+        up_block = wires.swap_blocks(shares, wires.planes).reshape(-1, hidden_units)
+        block = jnp.concatenate([w_down, fold_up(up_block, folds)])
+        made["ffn"] = jnp.broadcast_to(block[None], (deep, *block.shape))
+        return (made["ffn"],)
 
     d_out_low = after(upstream, qkv_other) * (jnp.arange(images) < live_count[0]).astype(LOW)[:, None, None]
     rings, gathered, d_out_got, steps = gather_rows(
-        wires, ring_block, lambda block: block[:tall].reshape(2, shard, wide), d_out_low, {1: norms}
-    )
-    own_sources, latents_wide, live_mask, one_hot = (
-        made[name] for name in ("own_sources", "latents_wide", "live_mask", "one_hot")
+        wires,
+        ring_block,
+        lambda block: block[:tall].reshape(2, shard, wide),
+        after(d_out_low, made["smalls"]),
+        {2: swap_up},
+        (far_raw,),
     )
     places, pieces = [], []
     for step, got in enumerate(gathered):
@@ -812,30 +916,36 @@
             for core in range(2):
                 places.append((wires.plane(step) * 2 + core) * flat + (wires.f ^ mask))
     out_column = [ring[tall:, :model_width] for ring in rings]
-
-    up_block = wires.swap_blocks(
-        split_units(after(w_up, gathered[0][wires.bits[0]]), 2 * flat, unit), wires.planes
-    )
-    folds = model_width // hidden_units
-    ffn_block = jnp.concatenate([w_down, fold_up(up_block.reshape(-1, hidden_units), folds)])
-
-    ffn_blocks = jnp.broadcast_to(ffn_block[None], (deep, *ffn_block.shape))
-    ffn_blocks = after(ffn_blocks, rings[-1])
-    ffn_blocks = wires.swap_blocks(ffn_blocks, wires.columns)
+    for mask in wires.masks:
+        if mask not in d_out_got:
+            d_out_got[mask] = wires.send(d_out_low, mask, *steps[-1])
+
+
+    ffn_blocks = wires.swap_blocks(after(made["ffn"], rings[-1]), wires.columns)
+
+    smalls = after(made["smalls"], *steps[-2][-1:])
+    smalls = smalls.transpose(1, 0, 2).reshape(-1, model_width).astype(WIDE)
+    norm_params = smalls[table_rows : table_rows + 4]
+    ff_params = smalls[table_rows + 4 :]
+    live_mask = (jnp.arange(images) < live_count[0]).astype(WIDE)[:, None, None]
+    one_hot = (time_index[:, None] == jnp.arange(table_rows)[None, :]).astype(WIDE)
+    time_rows = jnp.dot(one_hot, smalls[:table_rows], precision=HIGHEST)
+    both_rows = jnp.concatenate([time_rows, wires.send(time_rows, "core")])
 
     out_places, out_pieces = [], []
-    for mask, part in spread_plane(wires, jnp.stack(out_column), *steps[-2]).items():
+    for mask, part in spread_plane(wires, jnp.stack(out_column), *steps[-1]).items():
         out_pieces.append(part)
         for step in range(deep):
             out_places.append(wires.plane(step) * flat + (wires.f ^ mask))
 
-    far_sources = wires.send(own_sources, "core", rings[-1])
-
-    qkv_full, query, keyval, probs, mixed = attend(
+
+    qkv_full, sources, query, keyval, probs, mixed = attend(
         places,
         pieces,
-        own_sources,
-        far_sources,
+        raw,
+        far_raw,
+        both_rows,
+        norm_params,
         patches,
         half_width,
     )
@@ -843,9 +953,9 @@
         out_places, out_pieces, after(mixed, *d_out_got.values()), model_width
     )
     branch = branch[:images] + wires.send(branch[images:], "core")
-    middle = latents_wide + branch
-
-    ffn_normed, ffn_norm_back = jax.vjp(norm_rows, middle, made["ff_gain_full"], made["ff_bias_full"])
+    middle = latents.astype(WIDE) + branch
+
+    ffn_normed, ffn_norm_back = jax.vjp(norm_rows, middle, ff_params[0], ff_params[1])
     d_out = upstream.astype(WIDE) * live_mask
 
     def swapped(blocks, *ahead):
@@ -856,43 +966,28 @@
     ffn_low = ffn_normed.astype(LOW)
     ffn_got = spread_plane(wires, ffn_low)
     d_out_got = {mask: after(part, ffn_low) for mask, part in d_out_got.items()}
-    d_out_chunks = [swapped([d_out_got[0]]), swapped([d_out_got[mask] for mask in wires.masks])]
-    ffn_chunks = [swapped([ffn_low])]
-    near = ffn_rows_back(ffn_blocks, ffn_chunks[0], d_out_chunks[0], unit)
-    ffn_chunks.append(swapped([ffn_got[mask] for mask in wires.masks], near[0]))
-    far = ffn_rows_back(ffn_blocks, ffn_chunks[1], d_out_chunks[1], unit)
+    order = [0, *wires.masks]
+    d_out_rows = swapped([d_out_got[mask] for mask in order])
+    ffn_rows = swapped([ffn_got[mask] for mask in order])
+    hidden, d_pre, d_inputs, results = ffn_rows_back(
+        ffn_blocks, ffn_rows, d_out_rows, unit
+    )
     block_shape = (images, lat_rows, model_width)
 
-    def collect_core(near, far, *ahead):
-        far_whole = far[0] + wires.send(far[1].astype(LOW), "core", *ahead).astype(WIDE)
-        far_whole = far_whole.reshape(len(wires.masks), *block_shape)
-        near_whole = near[0] + wires.send(near[1].astype(LOW), "core", *ahead).astype(WIDE)
-        return {0: near_whole.reshape(block_shape)} | dict(zip(wires.masks, far_whole, strict=True))
-
-    d_sums = collect_core(near[4:], far[4:])
-    d_ffn_input, d_arrived = sum_plane(wires, d_sums.get)
-
-    hidden = jnp.concatenate([after(near[0], d_arrived[0]), near[1], *far[:2]])
-    d_pre_low = jnp.concatenate([after(near[2], d_arrived[0]), near[3], *far[2:4]])
-    d_out_rows = jnp.concatenate([rows for pair_of in d_out_chunks for rows in pair_of])
-    ffn_rows = jnp.concatenate([rows for pair_of in ffn_chunks for rows in pair_of])
-    down_partial = outer(hidden, d_out_rows).astype(LOW).reshape(deep, unit, model_width)
-    up_partial = outer(ffn_rows, d_pre_low).astype(LOW)
-    up_partial = up_partial.reshape(deep, 2 * flat * shard, hidden_units)
-    ffn_partial = jnp.concatenate([down_partial, fold_up(up_partial, folds)], axis=1)
+    def collect_core(parts, *ahead):
+        arrived = wires.send(parts[1], "core", *ahead)
+        rows = (parts[0] + arrived.astype(WIDE)).reshape(len(order), *block_shape)
+        return dict(zip(order, rows, strict=True)), arrived
+
+    d_sums, d_swapped = collect_core(d_inputs)
+    ffn_partial = ffn_outer(
+        ffn_rows, d_out_rows, hidden, (after(d_pre[0], d_swapped), d_pre[1]), deep, unit
+    )
     ffn_terms = wires.swap_blocks(ffn_partial, wires.columns)
-
+    d_ffn_input, _ = sum_plane(wires, d_sums.get)
     d_ffn_input = after(d_ffn_input, ffn_partial)
     d_middle_norm, ff_gain_grad, ff_bias_grad = ffn_norm_back(d_ffn_input)
     d_middle = d_out + d_middle_norm
-
-    down_full = after(ffn_blocks, d_middle)[:, :unit].reshape(hidden_units, model_width)
-    results = rows_by(hidden, down_full)
-    counts = [near[0].shape[0], far[0].shape[0]]
-    cuts = [counts[0], 2 * counts[0], 2 * counts[0] + counts[1]]
-    results = jnp.split(results, cuts)
-    result_sums = collect_core(results[:2], results[2:])
-    result_low = [result_sums[mask].astype(LOW) for mask in wires.masks]
 
     own_branch = d_middle.astype(LOW)
     d_branch = jnp.concatenate([own_branch, wires.send(own_branch, "core")], axis=0)
@@ -902,58 +997,63 @@
     d_mixed = rows_back(after(d_branch, out_partial), out_full).astype(LOW)
     d_projected = attend_back(d_mixed, query, keyval, probs)
 
-    source_rows = jnp.concatenate([after(own_sources, d_branch), far_sources]).reshape(-1, model_width)
+    source_rows = sources.reshape(-1, model_width)
     d_projected_rows = d_projected.reshape(-1, wide)
     plane_rows = 2 * flat * shard
 
     kept = {}
 
-    def results_home(arrived):
-        own_result, got = sum_plane(wires, result_sums.get, d_projected)
-        kept["out"] = ((middle + own_result) * live_mask).astype(LOW)
-        return got
-
-    def sources_back(arrived):
-        d_projected_now = after(d_projected, arrived)
-        far_d = rows_back(d_projected_now[images:], qkv_full).astype(LOW)
-        far_d = wires.send(far_d, "core").astype(WIDE)
-        kept["rows"] = rows_back(d_projected_now[:images], qkv_full) + far_d
-        return (kept["rows"],)
+    def results_clock(*ahead):
+        result_sums, arrived = collect_core(results, *ahead)
+        kept["own"] = result_sums[0]
+        kept["low"] = {mask: rows.astype(LOW) for mask, rows in result_sums.items()}
+        return arrived
+
+    def far_back(_):
+        kept["far"] = rows_back(d_projected[images:], qkv_full).astype(LOW)
+        return (kept["far"], *kept["low"].values())
+
+    def far_clock(*ahead):
+        kept["far"] = wires.send(kept["far"], "core", *ahead)
+        return kept["far"]
 
     def norms_back(arrived):
-        d_rows = after(kept["rows"], arrived)
-        d_latent_in, latent_gain_grad, latent_bias_grad = made["latent_norm_back"](d_rows[:, patches:, :])
-        media_grad, media_gain_grad, media_bias_grad = made["media_norm_back"](d_rows[:, :patches, :])
-        latent_grad = d_middle + d_latent_in
-        table_part = jnp.dot(one_hot.T, jnp.sum(media_grad, axis=1), precision=HIGHEST)
-
-        small_grads = jnp.concatenate(
-            [table_part]
-            + [
-                v[None]
-                for v in (
-                    media_gain_grad,
-                    media_bias_grad,
-                    latent_gain_grad,
-                    latent_bias_grad,
-                    ff_gain_grad,
-                    ff_bias_grad,
-                )
-            ],
-            axis=0,
+        media_grad, latent_grad, sums = sources_back(
+            after(d_projected[:images], arrived),
+            qkv_full,
+            kept["far"],
+            raw,
+            time_rows,
+            norm_params,
+            d_middle,
         )
-        small_grads = small_grads.reshape(-1, count, shard).transpose(1, 0, 2)
+        table_part = jnp.dot(one_hot.T, sums[:, 0], precision=HIGHEST)
+        small_grads = [table_part, jnp.sum(sums[:, 1:5], axis=0), ff_gain_grad[None], ff_bias_grad[None]]
+        small_grads = jnp.concatenate(small_grads).reshape(-1, count, shard).transpose(1, 0, 2)
         kept["media"], kept["latent"], kept["small"] = media_grad, latent_grad, small_grads
-        return media_grad, latent_grad, small_grads
-
-    def ffn_home(arrived):
-        ffn_sum = jnp.sum(after(ffn_terms, arrived).astype(WIDE), axis=0)
+        return media_grad, small_grads
+
+    def last_pull(_):
+        ffn_sum = jnp.sum(ffn_terms.astype(WIDE), axis=0)
         kept["down"] = ffn_sum[:unit]
         up_sum = unfold_up(ffn_sum[unit:].astype(LOW), folds)
         kept["up"] = up_sum.reshape(2 * flat, shard, hidden_units)
-        small_grads = lax.all_to_all(after(kept["small"], ffn_terms), AXES, 0, 0, tiled=True)
-        kept["small"] = jnp.sum(small_grads, axis=0)
-        return kept["down"], kept["up"], small_grads
+        return (kept["up"],)
+
+    result_got = []
+
+    def send_result(mask):
+        def ride(ahead):
+            result_got.append(wires.send(kept["low"][mask], mask, *ahead))
+            return result_got[-1]
+
+        return ride
+
+    turning = [mask for mask in wires.masks if mask & (mask - 1)]
+    riders = {
+        1: [send_result(mask) for mask in turning],
+        deep: [send_result(mask) for mask in wires.bits],
+    }
 
     def partial_rows(step, d_rows):
         at_plane = wires.plane(1 + step)
@@ -961,13 +1061,7 @@
         block = outer(rows, d_rows).astype(LOW).reshape(2, flat, shard, wide)
         return block, at(out_partial, at_plane, 0)
 
-    partials = {0: partial_rows(0, d_projected_rows)}
-
-    def more_partials(arrived):
-        d_rows = after(d_projected_rows, arrived)
-        for step in range(1, deep):
-            partials[step] = partial_rows(step, d_rows)
-        return (partials[1][0], *results_home(arrived))
+    partials = [partial_rows(step, d_projected_rows) for step in range(deep)]
 
     def part(step, mask):
         block, out_block = partials[step]
@@ -978,23 +1072,25 @@
         wires,
         part,
         {
-            0: lambda _: result_low,
-            1: more_partials,
-            2: sources_back,
+            1: far_back,
             3: norms_back,
-            4: ffn_home,
+            4: last_pull,
         },
+        riders,
+        {0: results_clock, 2: far_clock},
     )
     qkv_sum = total[..., :wide]
     w_out_grad = jnp.concatenate([total[0, :, wide:], total[1, :, wide:]], axis=-1)
     media_grad, latent_grad = kept["media"], kept["latent"]
     w_down_grad = kept["down"]
-    small_grads = kept["small"]
-    latents_out = kept["out"]
-    up_blocks = wires.swap_blocks(after(kept["up"], small_grads), wires.planes)
-    w_up_grad = merge_units(up_blocks, unit)
+    up_sum = wires.swap_blocks(kept["up"], wires.planes)
+    w_up_grad = merge_units(up_sum, unit)
+    small_grads = lax.all_to_all(after(kept["small"], up_sum), AXES, 0, 0, tiled=True)
+    small_grads = jnp.sum(small_grads, axis=0)
+    own_result = sum([rows.astype(WIDE) for rows in result_got], kept["own"])
+    latents_out = ((middle + own_result) * live_mask).astype(LOW)
     qkv_own = pick(qkv_sum, wires.c, 0)
-    qkv_far = wires.send(pick(qkv_sum, 1 - wires.c, 0), "core", up_blocks)
+    qkv_far = wires.send(pick(qkv_sum, 1 - wires.c, 0), "core", small_grads)
     w_query_grad, w_keyval_grad = join_columns(
         wires.c, qkv_own, qkv_far, (model_width, 2 * model_width), group
     )

time: 472 us -> 438 us (0.928)
  other arithmetic: 66.3 us -> 36.1 us
  local copies, waits for them, and re-layouts: 65.2 us -> 40.8 us
  matrix products: 40.8 us -> 18.3 us
  Pallas kernels: 60.2 us -> 79.9 us
  waiting for transfers between devices: 136 us -> 149 us
  starting transfers between devices: 92.9 us -> 105 us
    pallas_call x0 -> x2, Pallas kernels: none -> 22.5 us  [the longest x1 11.5 us: sources_back(): pl.pallas_call(kernel, grid=(images,), out_shape=(jax.ShapeDtypeStruct((i...]
    dot_general x11 -> x7, matrix products: 39.7 us -> 17.8 us  [dot(): lax.dot_general(left, right, (contract, ((), ())), preferred_element_type...]
    all_to_all x4, waiting for transfers between devices: 5.67 us -> 21.2 us  [swap_blocks(): lax.all_to_all(blocks, AXES, 0, 0, tiled=True, axis_index_groups=groups)]
    ppermute x67 -> x64, starting transfers between devices: 64 us -> 71.2 us  [send(): return lax.ppermute(block, AXES, self.moves[kind])]
    concatenate x9 -> x6, local copies, waits for them, and re-layouts: 6.97 us -> 0.39 us  [the longest x4 0.32 us: norms_back(): jnp.concatenate(small_grads).reshape(-1, count, shard).transpose(1, 0, 2)]
    add x3 -> x0, other arithmetic: 5.75 us -> none  [the longest x2 3.08 us: collect_core(): near[0] + wires.send(near[1].astype(LOW), 'core', *ahead).astype(WIDE)]
    unnamed x255 -> x149, local copies, waits for them, and re-layouts: 24.8 us -> 19.3 us
    another operation x19, other arithmetic: 12.5 us -> 7.16 us  [the longest x16 5.92 us: scatter_rows(): leaving = jnp.stack([term(block, mask, half) for half in range(2)])]
  transfers between devices with their start and end apart: 73 -> 70, of which waited for: 32 -> 31; matrix products, arithmetic and copies ran while one was open for 31% -> 17% of each run, Pallas kernels for 10% -> 14%
where the time goes in v3:
time: 438 us; the launch traced here: 432 us
  waiting for transfers between devices  149 us (34%)
  starting transfers between devices  105 us (24%)
  Pallas kernels  79.9 us (18%)
  local copies, waits for them, and re-layouts  40.8 us (9%)
  other arithmetic  36.1 us (8%)
  matrix products  18.3 us (4%)
    ppermute x64, waiting for transfers between devices, send(): return lax.ppermute(block, AXES, self.moves[kind])  124 us
    ppermute x64, starting transfers between devices, send(): return lax.ppermute(block, AXES, self.moves[kind])  71.2 us
    pallas_call x1, Pallas kernels, attend(): pl.pallas_call(kernel, grid=(slots,), out_shape=(jax.ShapeDtypeStruct((mo...  24.1 us
    all_to_all x4, waiting for transfers between devices, swap_blocks(): lax.all_to_all(blocks, AXES, 0, 0, tiled=True, axis_index_groups=groups)  21.2 us
    unnamed x149, local copies, waits for them, and re-layouts  19.3 us
    all_to_all x4, starting transfers between devices, swap_blocks(): lax.all_to_all(blocks, AXES, 0, 0, tiled=True, axis_index_groups=groups)  18.4 us
    dot_general x7, matrix products, dot(): lax.dot_general(left, right, (contract, ((), ())), preferred_element_type...  17.8 us
    pallas_call x1, Pallas kernels, ffn_rows_back(): pl.pallas_call(kernel, grid=(rows // block,), out_shape=(low, low, low, l...  13.3 us
  transfers between devices with their start and end apart: 70, of which 31 were waited for; matrix products, arithmetic and copies ran while one was open for 17% of the time, Pallas kernels for 14%

profile of v3, /device:TPU:0, one launch (start us, length us, event | category | flops | bytes accessed | tf_op | source)
XLA Modules:
  0.0 432.5 jit_solution(17465755761034871191)
XLA Ops:
  5.8 7.3 %all-to-all-start = ((bf16[32,2,336]{2,1,0:T(2,128)(2,1)}), bf16[32,2,336]{2,1,0:T(2,128)(2,1)S(1)}, u32[]{:S(2)}, u32[]{:S(2)}) async-start(bf16[32,2,336]{2,1,0:T(2,128)(2,1)} %reshape.269), calls=%async_computation | async-start | bytes 98304 | tf_op jit(solution)/shard_map/all_to_all | solution.py:894
  24.7 4.4 %collective-permute-done.4.refs_2_ = bf16[2,48,2304]{2,1,0:T(8,128)(2,1)} collective-permute-done((bf16[2,48,2304]{2,1,0:T(8,128)(2,1)S(1)}, bf16[2,48,2304]{2,1,0:T(8,128)(2,1)}, u32[]{:S(2)}, u32[]{:S(2)}) %collective-permute-start.4) | collective-permute-done | bytes 442400 | tf_op jit(solution)/shard_map/ppermute | solution.py:87
  31.2 3.9 all-to-all-start.1
  38.3 3.8 collective-permute-done.2
  50.7 7.3 %collective-permute-done.9.refs_7_ = bf16[2,48,2304]{2,1,0:T(8,128)(2,1)S(1)} collective-permute-done((bf16[2,48,2304]{2,1,0:T(8,128)(2,1)S(1)}, bf16[2,48,2304]{2,1,0:T(8,128)(2,1)S(1)}, u32[]{:S(2)}, u32[]{:S(2)}) %collective-permute-start.9) | collective-permute-done | bytes 442400 | tf_op jit(solution)/shard_map/ppermute | solution.py:87
  58.9 4.3 collective-permute-done.7
  64.3 2.6 broadcast_in_dim.57
  72.0 6.2 %collective-permute-done.14.refs_12_ = bf16[2,48,2304]{2,1,0:T(8,128)(2,1)S(1)} collective-permute-done((bf16[2,48,2304]{2,1,0:T(8,128)(2,1)S(1)}, bf16[2,48,2304]{2,1,0:T(8,128)(2,1)S(1)}, u32[]{:S(2)}, u32[]{:S(2)}) %collective-permute-start.14) | collective-permute-done | bytes 442400 | tf_op jit(solution)/shard_map/ppermute | solution.py:87
  80.0 5.4 %collective-permute-done.12 = bf16[144,2304]{1,0:T(8,128)(2,1)S(1)} collective-permute-done((bf16[144,2304]{1,0:T(8,128)(2,1)}, bf16[144,2304]{1,0:T(8,128)(2,1)S(1)}, u32[]{:S(2)}, u32[]{:S(2)}) %collective-permute-start.12) | collective-permute-done | bytes 663584 | tf_op jit(solution)/shard_map/ppermute | solution.py:87
  89.7 5.2 %all-to-all-start.2 = ((bf16[4,384,1536]{2,1,0:T(8,128)(2,1)}), bf16[4,384,1536]{2,1,0:T(8,128)(2,1)}, u32[]{:S(2)}, u32[]{:S(2)}) async-start(bf16[4,384,1536]{2,1,0:T(8,128)(2,1)} %broadcast_in_dim.57), calls=%async_computation.2 | async-start | bytes 9437184 | tf_op jit(solution)/shard_map/all_to_all | solution.py:90
  95.0 5.9 %collective-permute-done.20.refs_14_ = bf16[48,2304]{1,0:T(8,128)(2,1)} collective-permute-done((bf16[48,2304]{1,0:T(8,128)(2,1)S(1)}, bf16[48,2304]{1,0:T(8,128)(2,1)}, u32[]{:S(2)}, u32[]{:S(2)}) %collective-permute-start.20) | collective-permute-done | bytes 221216 | tf_op jit(solution)/shard_map/ppermute | solution.py:87
  103.5 5.7 %collective-permute-done.22.refs_19_ = bf16[48,2304]{1,0:T(8,128)(2,1)S(1)} collective-permute-done((bf16[48,2304]{1,0:T(8,128)(2,1)S(1)}, bf16[48,2304]{1,0:T(8,128)(2,1)S(1)}, u32[]{:S(2)}, u32[]{:S(2)}) %collective-permute-start.22) | collective-permute-done | bytes 221216 | tf_op jit(solution)/shard_map/ppermute | solution.py:87
  109.2 6.3 %collective-permute-done.21.refs_18_ = bf16[48,2304]{1,0:T(8,128)(2,1)S(1)} collective-permute-done((bf16[48,2304]{1,0:T(8,128)(2,1)S(1)}, bf16[48,2304]{1,0:T(8,128)(2,1)S(1)}, u32[]{:S(2)}, u32[]{:S(2)}) %collective-permute-start.21) | collective-permute-done | bytes 221216 | tf_op jit(solution)/shard_map/ppermute | solution.py:87
  123.0 24.1 %shard_map.282 = (bf16[1536,2304]{1,0:T(8,128)(2,1)}, bf16[4,320,1536]{2,1,0:T(8,128)(2,1)}, bf16[4,64,768]{2,1,0:T(8,128)(2,1)}, bf16[4,320,1536]{2,1,0:T(8,128...) custom-call(s32[32]{0:T(128)} %stack.324.places_ref, bf16[2,48,2304]{2,1,0:T(8,128)(2,1)} %copy-done.26, ...), custom_call_target="tpu_custom_call" | custom-call | flops 1 | bytes 1 | tf_op jit(solution)/shard_map/pallas_call | solution.py:491
  148.2 5.4 %shard_map.283 = (bf16[768,1536]{1,0:T(8,128)(2,1)S(1)}, f32[256,1536]{1,0:T(8,128)S(1)}) custom-call(s32[16]{0:T(128)S(1)} %stack.282.places_ref, bf16[4,48,1536]{2,1,0:T(8,128)(2,1)S(1)} %pad_maximum_fusion.4.refs_0_, bf16[4,48,1536]{2,1,0:T(8,128)(2,1)S(1)} %collective-permute-done.23.refs_1_, bf16[4,48,1536]{2,1,0:T(8,128)(2,1)S(1)} %collective-permute-done.24.refs_2_, ...), custom_call_target="tpu_custom_call" | custom-call | flops 1 | bytes 1 | tf_op jit(solution)/shard_map/pallas_call | solution.py:624
  163.2 6.7 %collective-permute-done.29 = bf16[2,64,1536]{2,1,0:T(8,128)(2,1)S(1)} collective-permute-done((bf16[2,64,1536]{2,1,0:T(8,128)(2,1)S(1)}, bf16[2,64,1536]{2,1,0:T(8,128)(2,1)S(1)}, u32[]{:S(2)}, u32[]{:S(2)}) %collective-permute-start.29) | collective-permute-done | bytes 393248 | tf_op jit(solution)/shard_map/ppermute | solution.py:87
  169.9 8.7 %collective-permute-done.30 = bf16[2,64,1536]{2,1,0:T(8,128)(2,1)S(1)} collective-permute-done((bf16[2,64,1536]{2,1,0:T(8,128)(2,1)S(1)}, bf16[2,64,1536]{2,1,0:T(8,128)(2,1)S(1)}, u32[]{:S(2)}, u32[]{:S(2)}) %collective-permute-start.30) | collective-permute-done | bytes 393248 | tf_op jit(solution)/shard_map/ppermute | solution.py:87
  180.2 2.2 collective-permute-done.32
  183.5 9.9 %all-to-all-done.2.refs_0_ = bf16[4,384,1536]{2,1,0:T(8,128)(2,1)} async-done(((bf16[4,384,1536]{2,1,0:T(8,128)(2,1)}), bf16[4,384,1536]{2,1,0:T(8,128)(2,1)}, u32[]{:S(2)}, u32[]{:S(2)}) %all-to-all-start.2) | async-done | bytes 4718624 | tf_op jit(solution)/shard_map/all_to_all | solution.py:90
  196.2 13.3 %shard_map.284 = (bf16[512,768]{1,0:T(8,128)(2,1)S(1)}, bf16[512,768]{1,0:T(8,128)(2,1)S(1)}, bf16[512,768]{1,0:T(8,128)(2,1)S(1)}, bf16[512,768]{1,0:T(8,128)(2...) custom-call(bf16[512,1536]{1,0:T(8,128)(2,1)S(1)} %bitcast.350, ...), custom_call_target="tpu_custom_call" | custom-call | flops 1 | bytes 1 | tf_op jit(solution)/shard_map/pallas_call | solution.py:728
  209.7 3.4 collective-permute-done.34
  217.4 11.0 %shard_map.285 = bf16[4,384,1536]{2,1,0:T(8,128)(2,1)} custom-call(bf16[512,1536]{1,0:T(8,128)(2,1)} %bitcast.351, bf16[512,1536]{1,0:T(8,128)(2,1)} %bitcast.358, bf16[512,1536]{1,0:T(8,128)(2,1)} %bitcast.349, bf16[512,1536]{1,0:T(8,128)(2,1)} %bitcast.356, bf16[512,768]{1,0:T(8,128)(2,1)} %copy-done.12, bf16[512,768]{1,0:T(8,128)(2,1)} %copy-done.13, ...), custom_call_target="tpu_custom_call" | custom-call | flops 1 | bytes 1 | tf_op jit(solution)/shard_map/pallas_call | solution.py:782
  228.5 5.9 %collective-permute-done.36 = bf16[2,64,1536]{2,1,0:T(8,128)(2,1)S(1)} collective-permute-done((bf16[2,64,1536]{2,1,0:T(8,128)(2,1)S(1)}, bf16[2,64,1536]{2,1,0:T(8,128)(2,1)S(1)}, u32[]{:S(2)}, u32[]{:S(2)}) %collective-permute-start.36) | collective-permute-done | bytes 393248 | tf_op jit(solution)/shard_map/ppermute | solution.py:87
  236.2 5.1 %all-to-all-start.3 = ((bf16[4,384,1536]{2,1,0:T(8,128)(2,1)}), bf16[4,384,1536]{2,1,0:T(8,128)(2,1)}, u32[]{:S(2)}, u32[]{:S(2)}) async-start(bf16[4,384,1536]{2,1,0:T(8,128)(2,1)} %shard_map.285), calls=%async_computation.3 | async-start | bytes 9437184 | tf_op jit(solution)/shard_map/all_to_all | solution.py:90
  247.5 6.0 %shard_map.286 = bf16[4,320,2304]{2,1,0:T(8,128)(2,1)S(1)} custom-call(bf16[4,64,768]{2,1,0:T(8,128)(2,1)S(1)} %fusion.8.d_ref, bf16[4,64,768]{2,1,0:T(8,128)(2,1)S(1)} %copy-done.18, bf16[4,320,1536]{2,1,0:T(8,128)(2,1)S(1)} %copy-done.8, f32[4,2,256,320]{3,2,1,0:T(8,128)S(1)} %copy-done.9), custom_call_target="tpu_custom_call" | custom-call | flops 1 | bytes 1 | tf_op jit(solution)/shard_map/pallas_call | solution.py:827
  256.6 2.5 convolution_convert_fusion
  259.1 2.5 convolution_convert_fusion.1
  261.7 2.5 convolution_convert_fusion.2
  264.2 2.5 convolution_convert_fusion.3
  266.8 6.1 %fusion.2 = bf16[2,320,1536]{2,1,0:T(8,128)(2,1)} fusion(bf16[4,320,2304]{2,1,0:T(8,128)(2,1)S(1)} %shard_map.286, bf16[1536,2304]{1,0:T(8,128)(2,1)S(1)} %bitcast.361), kind=kOutput, calls=%fused_computation.41 | convolution fusion | flops 4530831360 | bytes 14942208 | tf_op jit(solution)/shard_map/dot_general | solution.py:33
  278.5 4.0 collective-permute-done.40
  292.7 4.1 collective-permute-done.46
  296.9 10.1 %collective-permute-done.43 = bf16[48,3072]{1,0:T(8,128)(2,1)S(1)} collective-permute-done((bf16[48,3072]{1,0:T(8,128)(2,1)S(1)}, bf16[48,3072]{1,0:T(8,128)(2,1)S(1)}, u32[]{:S(2)}, u32[]{:S(2)}) %collective-permute-start.43) | collective-permute-done | bytes 294944 | tf_op jit(solution)/shard_map/ppermute | solution.py:87
  308.9 7.8 %collective-permute-done.44 = bf16[2,48,3072]{2,1,0:T(8,128)(2,1)S(1)} collective-permute-done((bf16[2,48,3072]{2,1,0:T(8,128)(2,1)S(1)}, bf16[2,48,3072]{2,1,0:T(8,128)(2,1)S(1)}, u32[]{:S(2)}, u32[]{:S(2)}) %collective-permute-start.44) | collective-permute-done | bytes 589856 | tf_op jit(solution)/shard_map/ppermute | solution.py:87
  323.1 5.2 %collective-permute-done.50 = bf16[48,3072]{1,0:T(8,128)(2,1)S(1)} collective-permute-done((bf16[48,3072]{1,0:T(8,128)(2,1)S(1)}, bf16[48,3072]{1,0:T(8,128)(2,1)S(1)}, u32[]{:S(2)}, u32[]{:S(2)}) %collective-permute-start.50) | collective-permute-done | bytes 294944 | tf_op jit(solution)/shard_map/ppermute | solution.py:87
  331.6 11.5 %shard_map.287 = (f32[2,256,1536]{2,1,0:T(8,128)}, f32[2,64,1536]{2,1,0:T(8,128)}, f32[2,8,1536]{2,1,0:T(8,128)S(1)}) custom-call(bf16[2,320,2304]{2,1,0:T(8,128)(2,1)} %slice.329.d_ref, bf16[1536,2304]{1,0:T(8,128)(2,1)} %get-tuple-element.145.w_ref, bf16[2,320,1536]{2,1,0:T(8,128)(2,1)S(1)} %collective-permute-done.52.far_ref, ...), custom_call_target="tpu_custom_call" | custom-call | flops 1 | bytes 1 | tf_op jit(solution)/shard_map/pallas_call | solution.py:563
  346.1 2.6 add_convert_fusion.1
  351.3 13.3 %collective-permute-start.53 = (bf16[2,48,3072]{2,1,0:T(8,128)(2,1)}, bf16[2,48,3072]{2,1,0:T(8,128)(2,1)}, u32[]{:S(2)}, u32[]{:S(2)}) collective-permute-start(bf16[2,48,3072]{2,1,0:T(8,128)(2,1)} %add_convert_fusion.1), channel_id=1, source_target_pairs={{0,8},{1,9},{2,10},{3,11},{4,12},{5,13},{6,14},{7,15},{8,16},{9,17... | collective-permute-start | bytes 1769480 | tf_op jit(solution)/shard_map/ppermute | solution.py:87
  366.5 3.3 convert_reduce_fusion
  370.9 9.2 %collective-permute-done.53 = bf16[2,48,3072]{2,1,0:T(8,128)(2,1)} collective-permute-done((bf16[2,48,3072]{2,1,0:T(8,128)(2,1)}, bf16[2,48,3072]{2,1,0:T(8,128)(2,1)}, u32[]{:S(2)}, u32[]{:S(2)}) %collective-permute-start.53) | collective-permute-done | bytes 589856 | tf_op jit(solution)/shard_map/ppermute | solution.py:87
  382.2 2.5 add_convert_fusion
  386.6 2.8 collective-permute-start.62
  389.5 4.2 all-to-all-start.4
  397.5 11.3 %all-to-all-done.4.in_ref = bf16[8,48,768]{2,1,0:T(8,128)(2,1)} async-done(((bf16[8,48,768]{2,1,0:T(8,128)(2,1)}), bf16[8,48,768]{2,1,0:T(8,128)(2,1)}, u32[]{:S(2)}, u32[]{:S(2)}) %all-to-all-start.4) | async-done | bytes 589856 | tf_op jit(solution)/shard_map/all_to_all | solution.py:90
  409.6 8.2 %all-to-all-start.5 = ((f32[32,1,672]{2,1,0:T(1,128)}), f32[32,1,672]{2,1,0:T(1,128)S(1)}, u32[]{:S(2)}, u32[]{:S(2)}) async-start(f32[32,1,672]{2,1,0:T(1,128)} %reshape.271), calls=%async_computation.5 | async-start | bytes 196608 | tf_op jit(solution)/shard_map/all_to_all | solution.py:1088
  417.8 2.4 shard_map.289
  422.8 3.0 all-to-all-done.5
  430.1 2.2 shard_map.288
  (382 shorter events, 135.7 us)
Async XLA Ops:
  5.8 14.7 %all-to-all-start = ((bf16[32,2,336]{2,1,0:T(2,128)(2,1)}), bf16[32,2,336]{2,1,0:T(2,128)(2,1)S(1)}, u32[]{:S(2)}, u32[]{:S(2)}) async-start(bf16[32,2,336]{2,1,0:T(2,128)(2,1)} %reshape.269), calls=%async_computation | async-start | bytes 98304 | tf_op jit(solution)/shard_map/all_to_all | solution.py:894
  21.6 15.1 %collective-permute-start.3 = (bf16[2,48,2304]{2,1,0:T(8,128)(2,1)S(1)}, bf16[2,48,2304]{2,1,0:T(8,128)(2,1)}, u32[]{:S(2)}, u32[]{:S(2)}) collective-permute-start(bf16[2,48,2304]{2,1,0:T(8,128)(2,1)S(1)} %maximum_select_fusion.refs_0_), channel_id=1, source_target_pairs={{0,1},{1,0},{2,3},{3,2},{4,5},{5,4},{6,7},{7,6},{8,9},{9,8},{10,11... | collective-permute-start | bytes 1327112 | tf_op jit(solution)/shard_map/ppermute | solution.py:87
  22.0 21.0 %collective-permute-start.5 = (bf16[2,64,1536]{2,1,0:T(8,128)(2,1)}, bf16[2,64,1536]{2,1,0:T(8,128)(2,1)S(1)}, u32[]{:S(2)}, u32[]{:S(2)}) collective-permute-start(bf16[2,64,1536]{2,1,0:T(8,128)(2,1)} %broadcast_multiply_fusion), channel_id=1, source_target_pairs={{0,1},{1,0},{2,3},{3,2},{4,5},{5,4},{6,7},{7,6},{8,9},{9,8},{10,11... | collective-permute-start | bytes 1179656 | tf_op jit(solution)/shard_map/ppermute | solution.py:87
  23.6 19.5 %collective-permute-start.6 = (bf16[2,64,1536]{2,1,0:T(8,128)(2,1)}, bf16[2,64,1536]{2,1,0:T(8,128)(2,1)}, u32[]{:S(2)}, u32[]{:S(2)}) collective-permute-start(bf16[2,64,1536]{2,1,0:T(8,128)(2,1)} %broadcast_multiply_fusion), channel_id=1, source_target_pairs={{0,2},{1,3},{2,0},{3,1},{4,6},{5,7},{6,4},{7,5},{8,10},{9,11},{10,... | collective-permute-start | bytes 1179656 | tf_op jit(solution)/shard_map/ppermute | solution.py:87
  24.1 18.0 %collective-permute-start.2 = (bf16[144,2304]{1,0:T(8,128)(2,1)}, bf16[144,2304]{1,0:T(8,128)(2,1)S(1)}, u32[]{:S(2)}, u32[]{:S(2)}) collective-permute-start(bf16[144,2304]{1,0:T(8,128)(2,1)} %fusion.23), channel_id=1, source_target_pairs={{0,8},{1,9},{2,10},{3,11},{4,12},{5,13},{6,14},{7,15},{8,16},{9,17... | collective-permute-start | bytes 1990664 | tf_op jit(solution)/shard_map/ppermute | solution.py:87
  31.2 18.3 %all-to-all-start.1 = ((bf16[8,48,768]{2,1,0:T(8,128)(2,1)}), bf16[8,48,768]{2,1,0:T(8,128)(2,1)S(1)}, u32[]{:S(2)}, u32[]{:S(2)}) async-start(bf16[8,48,768]{2,1,0:T(8,128)(2,1)} %shard_map.281), calls=%async_computation.1 | async-start | bytes 1179648 | tf_op jit(solution)/shard_map/all_to_all | solution.py:90
  43.8 14.1 %collective-permute-start.9 = (bf16[2,48,2304]{2,1,0:T(8,128)(2,1)S(1)}, bf16[2,48,2304]{2,1,0:T(8,128)(2,1)S(1)}, u32[]{:S(2)}, u32[]{:S(2)}) collective-permute-start(bf16[2,48,2304]{2,1,0:T(8,128)(2,1)S(1)} %bitcast.372), channel_id=1, source_target_pairs={{0,2},{1,3},{2,0},{3,1},{4,6},{5,7},{6,4},{7,5},{8,10},{9,11},{10,... | collective-permute-start | bytes 1327112 | tf_op jit(solution)/shard_map/ppermute | solution.py:87
  44.4 14.5 %collective-permute-start.8 = (bf16[2,48,2304]{2,1,0:T(8,128)(2,1)S(1)}, bf16[2,48,2304]{2,1,0:T(8,128)(2,1)S(1)}, u32[]{:S(2)}, u32[]{:S(2)}) collective-permute-start(bf16[2,48,2304]{2,1,0:T(8,128)(2,1)S(1)} %bitcast.373), channel_id=1, source_target_pairs={{0,1},{1,0},{2,3},{3,2},{4,5},{5,4},{6,7},{7,6},{8,9},{9,8},{10,11... | collective-permute-start | bytes 1327112 | tf_op jit(solution)/shard_map/ppermute | solution.py:87
  45.2 19.1 %collective-permute-start.11 = (bf16[48,2304]{1,0:T(8,128)(2,1)}, bf16[48,2304]{1,0:T(8,128)(2,1)}, u32[]{:S(2)}, u32[]{:S(2)}) collective-permute-start(bf16[48,2304]{1,0:T(8,128)(2,1)} %slice_bitcast_fusion.8), channel_id=1, source_target_pairs={{0,1},{1,0},{2,3},{3,2},{4,5},{5,4},{6,7},{7,6},{8,9},{9,8},{10,11... | collective-permute-start | bytes 663560 | tf_op jit(solution)/shard_map/ppermute | solution.py:87
  46.4 17.9 %collective-permute-start.10 = (bf16[48,2304]{1,0:T(8,128)(2,1)}, bf16[48,2304]{1,0:T(8,128)(2,1)}, u32[]{:S(2)}, u32[]{:S(2)}) collective-permute-start(bf16[48,2304]{1,0:T(8,128)(2,1)} %slice_bitcast_fusion.9), channel_id=1, source_target_pairs={{0,2},{1,3},{2,0},{3,1},{4,6},{5,7},{6,4},{7,5},{8,10},{9,11},{10,... | collective-permute-start | bytes 663560 | tf_op jit(solution)/shard_map/ppermute | solution.py:87
  47.9 15.4 %collective-permute-start.7 = (bf16[144,2304]{1,0:T(8,128)(2,1)}, bf16[144,2304]{1,0:T(8,128)(2,1)}, u32[]{:S(2)}, u32[]{:S(2)}) collective-permute-start(bf16[144,2304]{1,0:T(8,128)(2,1)} %copy-done.47), channel_id=1, source_target_pairs={{0,8},{1,9},{2,10},{3,11},{4,12},{5,13},{6,14},{7,15},{8,16},{9,17... | collective-permute-start | bytes 1990664 | tf_op jit(solution)/shard_map/ppermute | solution.py:87
  69.1 16.5 %collective-permute-start.16 = (bf16[48,2304]{1,0:T(8,128)(2,1)S(1)}, bf16[48,2304]{1,0:T(8,128)(2,1)S(1)}, u32[]{:S(2)}, u32[]{:S(2)}) collective-permute-start(bf16[48,2304]{1,0:T(8,128)(2,1)S(1)} %slice_bitcast_fusion.6), channel_id=1, source_target_pairs={{0,1},{1,0},{2,3},{3,2},{4,5},{5,4},{6,7},{7,6},{8,9},{9,8},{10,11... | collective-permute-start | bytes 663560 | tf_op jit(solution)/shard_map/ppermute | solution.py:87
  70.0 15.5 %collective-permute-start.15 = (bf16[48,2304]{1,0:T(8,128)(2,1)S(1)}, bf16[48,2304]{1,0:T(8,128)(2,1)S(1)}, u32[]{:S(2)}, u32[]{:S(2)}) collective-permute-start(bf16[48,2304]{1,0:T(8,128)(2,1)S(1)} %slice_bitcast_fusion.7), channel_id=1, source_target_pairs={{0,2},{1,3},{2,0},{3,1},{4,6},{5,7},{6,4},{7,5},{8,10},{9,11},{10,... | collective-permute-start | bytes 663560 | tf_op jit(solution)/shard_map/ppermute | solution.py:87
  71.0 14.5 %collective-permute-start.12 = (bf16[144,2304]{1,0:T(8,128)(2,1)}, bf16[144,2304]{1,0:T(8,128)(2,1)S(1)}, u32[]{:S(2)}, u32[]{:S(2)}) collective-permute-start(bf16[144,2304]{1,0:T(8,128)(2,1)} %collective-permute-done.7), channel_id=1, source_target_pairs={{0,8},{1,9},{2,10},{3,11},{4,12},{5,13},{6,14},{7,15},{8,16},{9,17... | collective-permute-start | bytes 1990664 | tf_op jit(solution)/shard_map/ppermute | solution.py:87
  86.9 14.0 %collective-permute-start.17 = (bf16[2,48,2304]{2,1,0:T(8,128)(2,1)S(1)}, bf16[2,48,2304]{2,1,0:T(8,128)(2,1)S(1)}, u32[]{:S(2)}, u32[]{:S(2)}) collective-permute-start(bf16[2,48,2304]{2,1,0:T(8,128)(2,1)S(1)} %bitcast.379), channel_id=1, source_target_pairs={{0,1},{1,0},{2,3},{3,2},{4,5},{5,4},{6,7},{7,6},{8,9},{9,8},{10,11... | collective-permute-start | bytes 1327112 | tf_op jit(solution)/shard_map/ppermute | solution.py:87
  87.6 13.3 %collective-permute-start.20 = (bf16[48,2304]{1,0:T(8,128)(2,1)S(1)}, bf16[48,2304]{1,0:T(8,128)(2,1)}, u32[]{:S(2)}, u32[]{:S(2)}) collective-permute-start(bf16[48,2304]{1,0:T(8,128)(2,1)S(1)} %slice_bitcast_fusion.3), channel_id=1, source_target_pairs={{0,1},{1,0},{2,3},{3,2},{4,5},{5,4},{6,7},{7,6},{8,9},{9,8},{10,11... | collective-permute-start | bytes 663560 | tf_op jit(solution)/shard_map/ppermute | solution.py:87
  89.7 103.7 %all-to-all-start.2 = ((bf16[4,384,1536]{2,1,0:T(8,128)(2,1)}), bf16[4,384,1536]{2,1,0:T(8,128)(2,1)}, u32[]{:S(2)}, u32[]{:S(2)}) async-start(bf16[4,384,1536]{2,1,0:T(8,128)(2,1)} %broadcast_in_dim.57), calls=%async_computation.2 | async-start | bytes 9437184 | tf_op jit(solution)/shard_map/all_to_all | solution.py:90
  101.5 14.0 %collective-permute-start.21 = (bf16[48,2304]{1,0:T(8,128)(2,1)S(1)}, bf16[48,2304]{1,0:T(8,128)(2,1)S(1)}, u32[]{:S(2)}, u32[]{:S(2)}) collective-permute-start(bf16[48,2304]{1,0:T(8,128)(2,1)S(1)} %slice_bitcast_fusion.5), channel_id=1, source_target_pairs={{0,2},{1,3},{2,0},{3,1},{4,6},{5,7},{6,4},{7,5},{8,10},{9,11},{10,... | collective-permute-start | bytes 663560 | tf_op jit(solution)/shard_map/ppermute | solution.py:87
  116.2 31.0 %collective-permute-start.23 = (bf16[4,48,1536]{2,1,0:T(8,128)(2,1)S(1)}, bf16[4,48,1536]{2,1,0:T(8,128)(2,1)S(1)}, u32[]{:S(2)}, u32[]{:S(2)}) collective-permute-start(bf16[4,48,1536]{2,1,0:T(8,128)(2,1)S(1)} %pad_maximum_fusion.4.refs_0_), channel_id=1, source_target_pairs={{0,3},{1,2},{2,1},{3,0},{4,7},{5,6},{6,5},{7,4},{8,11},{9,10},{10,... | collective-permute-start | bytes 1769480 | tf_op jit(solution)/shard_map/ppermute | solution.py:87
  117.8 29.4 %collective-permute-start.24 = (bf16[4,48,1536]{2,1,0:T(8,128)(2,1)S(1)}, bf16[4,48,1536]{2,1,0:T(8,128)(2,1)S(1)}, u32[]{:S(2)}, u32[]{:S(2)}) collective-permute-start(bf16[4,48,1536]{2,1,0:T(8,128)(2,1)S(1)} %pad_maximum_fusion.4.refs_0_), channel_id=1, source_target_pairs={{0,2},{1,3},{2,0},{3,1},{4,6},{5,7},{6,4},{7,5},{8,10},{9,11},{10,... | collective-permute-start | bytes 1769480 | tf_op jit(solution)/shard_map/ppermute | solution.py:87
  119.1 28.0 %collective-permute-start.25 = (bf16[4,48,1536]{2,1,0:T(8,128)(2,1)S(1)}, bf16[4,48,1536]{2,1,0:T(8,128)(2,1)S(1)}, u32[]{:S(2)}, u32[]{:S(2)}) collective-permute-start(bf16[4,48,1536]{2,1,0:T(8,128)(2,1)S(1)} %pad_maximum_fusion.4.refs_0_), channel_id=1, source_target_pairs={{0,1},{1,0},{2,3},{3,2},{4,5},{5,4},{6,7},{7,6},{8,9},{9,8},{10,11... | collective-permute-start | bytes 1769480 | tf_op jit(solution)/shard_map/ppermute | solution.py:87
  119.9 27.3 %collective-permute-start.27 = (bf16[2,64,1536]{2,1,0:T(8,128)(2,1)}, bf16[2,64,1536]{2,1,0:T(8,128)(2,1)}, u32[]{:S(2)}, u32[]{:S(2)}) collective-permute-start(bf16[2,64,1536]{2,1,0:T(8,128)(2,1)} %broadcast_multiply_fusion), channel_id=1, source_target_pairs={{0,3},{1,2},{2,1},{3,0},{4,7},{5,6},{6,5},{7,4},{8,11},{9,10},{10,... | collective-permute-start | bytes 1179656 | tf_op jit(solution)/shard_map/ppermute | solution.py:87
  159.3 19.3 %collective-permute-start.30 = (bf16[2,64,1536]{2,1,0:T(8,128)(2,1)S(1)}, bf16[2,64,1536]{2,1,0:T(8,128)(2,1)S(1)}, u32[]{:S(2)}, u32[]{:S(2)}) collective-permute-start(bf16[2,64,1536]{2,1,0:T(8,128)(2,1)S(1)} %add_convert_fusion.3), channel_id=1, source_target_pairs={{0,2},{1,3},{2,0},{3,1},{4,6},{5,7},{6,4},{7,5},{8,10},{9,11},{10,... | collective-permute-start | bytes 1179656 | tf_op jit(solution)/shard_map/ppermute | solution.py:87
  159.9 18.8 %collective-permute-start.31 = (bf16[2,64,1536]{2,1,0:T(8,128)(2,1)S(1)}, bf16[2,64,1536]{2,1,0:T(8,128)(2,1)S(1)}, u32[]{:S(2)}, u32[]{:S(2)}) collective-permute-start(bf16[2,64,1536]{2,1,0:T(8,128)(2,1)S(1)} %add_convert_fusion.3), channel_id=1, source_target_pairs={{0,3},{1,2},{2,1},{3,0},{4,7},{5,6},{6,5},{7,4},{8,11},{9,10},{10,... | collective-permute-start | bytes 1179656 | tf_op jit(solution)/shard_map/ppermute | solution.py:87
  162.9 16.0 %collective-permute-start.33 = (bf16[4,2,64,1536]{3,2,1,0:T(8,128)(2,1)S(1)}, bf16[4,2,64,1536]{3,2,1,0:T(8,128)(2,1)S(1)}, u32[]{:S(2)}, u32[]{:S(2)}) collective-permute-start(bf16[4,2,64,1536]{3,2,1,0:T(8,128)(2,1)S(1)} %pad_maximum_fusion.2), channel_id=1, source_target_pairs={{0,4},{1,5},{2,6},{3,7},{4,0},{5,1},{6,2},{7,3},{8,12},{9,13},{10,... | collective-permute-start | bytes 4718600 | tf_op jit(solution)/shard_map/ppermute | solution.py:87
  213.8 14.6 %collective-permute-start.35 = (bf16[2,64,1536]{2,1,0:T(8,128)(2,1)S(1)}, bf16[2,64,1536]{2,1,0:T(8,128)(2,1)S(1)}, u32[]{:S(2)}, u32[]{:S(2)}) collective-permute-start(bf16[2,64,1536]{2,1,0:T(8,128)(2,1)S(1)} %bitcast.391), channel_id=1, source_target_pairs={{0,3},{1,2},{2,1},{3,0},{4,7},{5,6},{6,5},{7,4},{8,11},{9,10},{10,... | collective-permute-start | bytes 1179656 | tf_op jit(solution)/shard_map/ppermute | solution.py:87
  215.4 19.0 %collective-permute-start.36 = (bf16[2,64,1536]{2,1,0:T(8,128)(2,1)S(1)}, bf16[2,64,1536]{2,1,0:T(8,128)(2,1)S(1)}, u32[]{:S(2)}, u32[]{:S(2)}) collective-permute-start(bf16[2,64,1536]{2,1,0:T(8,128)(2,1)S(1)} %bitcast.389), channel_id=1, source_target_pairs={{0,2},{1,3},{2,0},{3,1},{4,6},{5,7},{6,4},{7,5},{8,10},{9,11},{10,... | collective-permute-start | bytes 1179656 | tf_op jit(solution)/shard_map/ppermute | solution.py:87
  217.0 17.4 %collective-permute-start.37 = (bf16[2,64,1536]{2,1,0:T(8,128)(2,1)S(1)}, bf16[2,64,1536]{2,1,0:T(8,128)(2,1)S(1)}, u32[]{:S(2)}, u32[]{:S(2)}) collective-permute-start(bf16[2,64,1536]{2,1,0:T(8,128)(2,1)S(1)} %bitcast.388), channel_id=1, source_target_pairs={{0,1},{1,0},{2,3},{3,2},{4,5},{5,4},{6,7},{7,6},{8,9},{9,8},{10,11... | collective-permute-start | bytes 1179656 | tf_op jit(solution)/shard_map/ppermute | solution.py:87
  236.2 130.3 %all-to-all-start.3 = ((bf16[4,384,1536]{2,1,0:T(8,128)(2,1)}), bf16[4,384,1536]{2,1,0:T(8,128)(2,1)}, u32[]{:S(2)}, u32[]{:S(2)}) async-start(bf16[4,384,1536]{2,1,0:T(8,128)(2,1)} %shard_map.285), calls=%async_computation.3 | async-start | bytes 9437184 | tf_op jit(solution)/shard_map/all_to_all | solution.py:90
  288.6 18.4 %collective-permute-start.43 = (bf16[48,3072]{1,0:T(8,128)(2,1)S(1)}, bf16[48,3072]{1,0:T(8,128)(2,1)S(1)}, u32[]{:S(2)}, u32[]{:S(2)}) collective-permute-start(bf16[48,3072]{1,0:T(8,128)(2,1)S(1)} %get-tuple-element.147), channel_id=1, source_target_pairs={{0,2},{1,3},{2,0},{3,1},{4,6},{5,7},{6,4},{7,5},{8,10},{9,11},{10,... | collective-permute-start | bytes 884744 | tf_op jit(solution)/shard_map/ppermute | solution.py:87
  289.2 19.6 %collective-permute-start.42 = (bf16[2,64,1536]{2,1,0:T(8,128)(2,1)S(1)}, bf16[2,64,1536]{2,1,0:T(8,128)(2,1)S(1)}, u32[]{:S(2)}, u32[]{:S(2)}) collective-permute-start(bf16[2,64,1536]{2,1,0:T(8,128)(2,1)S(1)} %bitcast.387), channel_id=1, source_target_pairs={{0,3},{1,2},{2,1},{3,0},{4,7},{5,6},{6,5},{7,4},{8,11},{9,10},{10,... | collective-permute-start | bytes 1179656 | tf_op jit(solution)/shard_map/ppermute | solution.py:87
  290.5 26.1 %collective-permute-start.44 = (bf16[2,48,3072]{2,1,0:T(8,128)(2,1)S(1)}, bf16[2,48,3072]{2,1,0:T(8,128)(2,1)S(1)}, u32[]{:S(2)}, u32[]{:S(2)}) collective-permute-start(bf16[2,48,3072]{2,1,0:T(8,128)(2,1)S(1)} %fusion.27), channel_id=1, source_target_pairs={{0,1},{1,0},{2,3},{3,2},{4,5},{5,4},{6,7},{7,6},{8,9},{9,8},{10,11... | collective-permute-start | bytes 1769480 | tf_op jit(solution)/shard_map/ppermute | solution.py:87
  292.1 25.9 %collective-permute-start.45 = (bf16[2,48,3072]{2,1,0:T(8,128)(2,1)S(1)}, bf16[2,48,3072]{2,1,0:T(8,128)(2,1)S(1)}, u32[]{:S(2)}, u32[]{:S(2)}) collective-permute-start(bf16[2,48,3072]{2,1,0:T(8,128)(2,1)S(1)} %pad_maximum_fusion.5), channel_id=1, source_target_pairs={{0,2},{1,3},{2,0},{3,1},{4,6},{5,7},{6,4},{7,5},{8,10},{9,11},{10,... | collective-permute-start | bytes 1769480 | tf_op jit(solution)/shard_map/ppermute | solution.py:87
  318.0 13.6 %collective-permute-start.52 = (bf16[2,320,1536]{2,1,0:T(8,128)(2,1)S(1)}, bf16[2,320,1536]{2,1,0:T(8,128)(2,1)S(1)}, u32[]{:S(2)}, u32[]{:S(2)}) collective-permute-start(bf16[2,320,1536]{2,1,0:T(8,128)(2,1)S(1)} %copy-done.68), channel_id=1, source_target_pairs={{0,4},{1,5},{2,6},{3,7},{4,0},{5,1},{6,2},{7,3},{8,12},{9,13},{10,... | collective-permute-start | bytes 5898248 | tf_op jit(solution)/shard_map/ppermute | solution.py:87
  319.9 24.7 %collective-permute-start.47 = (bf16[2,48,3072]{2,1,0:T(8,128)(2,1)}, bf16[2,48,3072]{2,1,0:T(8,128)(2,1)}, u32[]{:S(2)}, u32[]{:S(2)}) collective-permute-start(bf16[2,48,3072]{2,1,0:T(8,128)(2,1)} %fusion.25), channel_id=1, source_target_pairs={{0,1},{1,0},{2,3},{3,2},{4,5},{5,4},{6,7},{7,6},{8,9},{9,8},{10,11... | collective-permute-start | bytes 1769480 | tf_op jit(solution)/shard_map/ppermute | solution.py:87
  320.6 23.9 %collective-permute-start.48 = (bf16[2,48,3072]{2,1,0:T(8,128)(2,1)}, bf16[2,48,3072]{2,1,0:T(8,128)(2,1)}, u32[]{:S(2)}, u32[]{:S(2)}) collective-permute-start(bf16[2,48,3072]{2,1,0:T(8,128)(2,1)} %pad_maximum_fusion.6), channel_id=1, source_target_pairs={{0,2},{1,3},{2,0},{3,1},{4,6},{5,7},{6,4},{7,5},{8,10},{9,11},{10,... | collective-permute-start | bytes 1769480 | tf_op jit(solution)/shard_map/ppermute | solution.py:87
  328.3 16.3 %collective-permute-start.49 = (bf16[2,48,3072]{2,1,0:T(8,128)(2,1)}, bf16[2,48,3072]{2,1,0:T(8,128)(2,1)}, u32[]{:S(2)}, u32[]{:S(2)}) collective-permute-start(bf16[2,48,3072]{2,1,0:T(8,128)(2,1)} %add_convert_fusion.2), channel_id=1, source_target_pairs={{0,8},{1,9},{2,10},{3,11},{4,12},{5,13},{6,14},{7,15},{8,16},{9,17... | collective-permute-start | bytes 1769480 | tf_op jit(solution)/shard_map/ppermute | solution.py:87
  344.6 20.0 %collective-permute-start.56 = (bf16[48,3072]{1,0:T(8,128)(2,1)}, bf16[48,3072]{1,0:T(8,128)(2,1)S(1)}, u32[]{:S(2)}, u32[]{:S(2)}) collective-permute-start(bf16[48,3072]{1,0:T(8,128)(2,1)} %get-tuple-element.163), channel_id=1, source_target_pairs={{0,2},{1,3},{2,0},{3,1},{4,6},{5,7},{6,4},{7,5},{8,10},{9,11},{10,... | collective-permute-start | bytes 884744 | tf_op jit(solution)/shard_map/ppermute | solution.py:87
  348.6 16.9 %collective-permute-start.57 = (bf16[48,3072]{1,0:T(8,128)(2,1)S(1)}, bf16[48,3072]{1,0:T(8,128)(2,1)S(1)}, u32[]{:S(2)}, u32[]{:S(2)}) collective-permute-start(bf16[48,3072]{1,0:T(8,128)(2,1)S(1)} %copy-done.53), channel_id=1, source_target_pairs={{0,1},{1,0},{2,3},{3,2},{4,5},{5,4},{6,7},{7,6},{8,9},{9,8},{10,11... | collective-permute-start | bytes 884744 | tf_op jit(solution)/shard_map/ppermute | solution.py:87
  349.4 21.5 %collective-permute-start.55 = (bf16[2,48,3072]{2,1,0:T(8,128)(2,1)}, bf16[2,48,3072]{2,1,0:T(8,128)(2,1)}, u32[]{:S(2)}, u32[]{:S(2)}) collective-permute-start(bf16[2,48,3072]{2,1,0:T(8,128)(2,1)} %pad_maximum_fusion.7), channel_id=1, source_target_pairs={{0,2},{1,3},{2,0},{3,1},{4,6},{5,7},{6,4},{7,5},{8,10},{9,11},{10,... | collective-permute-start | bytes 1769480 | tf_op jit(solution)/shard_map/ppermute | solution.py:87
  350.8 20.0 %collective-permute-start.54 = (bf16[2,48,3072]{2,1,0:T(8,128)(2,1)}, bf16[2,48,3072]{2,1,0:T(8,128)(2,1)}, u32[]{:S(2)}, u32[]{:S(2)}) collective-permute-start(bf16[2,48,3072]{2,1,0:T(8,128)(2,1)} %fusion.29), channel_id=1, source_target_pairs={{0,1},{1,0},{2,3},{3,2},{4,5},{5,4},{6,7},{7,6},{8,9},{9,8},{10,11... | collective-permute-start | bytes 1769480 | tf_op jit(solution)/shard_map/ppermute | solution.py:87
  351.3 28.8 %collective-permute-start.53 = (bf16[2,48,3072]{2,1,0:T(8,128)(2,1)}, bf16[2,48,3072]{2,1,0:T(8,128)(2,1)}, u32[]{:S(2)}, u32[]{:S(2)}) collective-permute-start(bf16[2,48,3072]{2,1,0:T(8,128)(2,1)} %add_convert_fusion.1), channel_id=1, source_target_pairs={{0,8},{1,9},{2,10},{3,11},{4,12},{5,13},{6,14},{7,15},{8,16},{9,17... | collective-permute-start | bytes 1769480 | tf_op jit(solution)/shard_map/ppermute | solution.py:87
  380.0 14.8 %collective-permute-start.58 = (bf16[2,64,1536]{2,1,0:T(8,128)(2,1)}, bf16[2,64,1536]{2,1,0:T(8,128)(2,1)}, u32[]{:S(2)}, u32[]{:S(2)}) collective-permute-start(bf16[2,64,1536]{2,1,0:T(8,128)(2,1)} %bitcast.111), channel_id=1, source_target_pairs={{0,1},{1,0},{2,3},{3,2},{4,5},{5,4},{6,7},{7,6},{8,9},{9,8},{10,11... | collective-permute-start | bytes 1179656 | tf_op jit(solution)/shard_map/ppermute | solution.py:87
  384.8 35.5 %collective-permute-start.60 = (bf16[2,48,3072]{2,1,0:T(8,128)(2,1)}, bf16[2,48,3072]{2,1,0:T(8,128)(2,1)}, u32[]{:S(2)}, u32[]{:S(2)}) collective-permute-start(bf16[2,48,3072]{2,1,0:T(8,128)(2,1)} %fusion.31), channel_id=1, source_target_pairs={{0,1},{1,0},{2,3},{3,2},{4,5},{5,4},{6,7},{7,6},{8,9},{9,8},{10,11... | collective-permute-start | bytes 1769480 | tf_op jit(solution)/shard_map/ppermute | solution.py:87
  386.0 34.2 %collective-permute-start.61 = (bf16[2,48,3072]{2,1,0:T(8,128)(2,1)}, bf16[2,48,3072]{2,1,0:T(8,128)(2,1)}, u32[]{:S(2)}, u32[]{:S(2)}) collective-permute-start(bf16[2,48,3072]{2,1,0:T(8,128)(2,1)} %pad_maximum_fusion.9), channel_id=1, source_target_pairs={{0,2},{1,3},{2,0},{3,1},{4,6},{5,7},{6,4},{7,5},{8,10},{9,11},{10,... | collective-permute-start | bytes 1769480 | tf_op jit(solution)/shard_map/ppermute | solution.py:87
  386.6 33.6 %collective-permute-start.62 = (bf16[2,48,3072]{2,1,0:T(8,128)(2,1)}, bf16[2,48,3072]{2,1,0:T(8,128)(2,1)}, u32[]{:S(2)}, u32[]{:S(2)}) collective-permute-start(bf16[2,48,3072]{2,1,0:T(8,128)(2,1)} %add_convert_fusion), channel_id=1, source_target_pairs={{0,8},{1,9},{2,10},{3,11},{4,12},{5,13},{6,14},{7,15},{8,16},{9,17... | collective-permute-start | bytes 1769480 | tf_op jit(solution)/shard_map/ppermute | solution.py:87
  389.5 19.3 %all-to-all-start.4 = ((bf16[8,48,768]{2,1,0:T(8,128)(2,1)}), bf16[8,48,768]{2,1,0:T(8,128)(2,1)}, u32[]{:S(2)}, u32[]{:S(2)}) async-start(bf16[8,48,768]{2,1,0:T(8,128)(2,1)} %bitcast.367), calls=%async_computation.4 | async-start | bytes 1179648 | tf_op jit(solution)/shard_map/all_to_all | solution.py:90
  409.6 16.1 %all-to-all-start.5 = ((f32[32,1,672]{2,1,0:T(1,128)}), f32[32,1,672]{2,1,0:T(1,128)S(1)}, u32[]{:S(2)}, u32[]{:S(2)}) async-start(f32[32,1,672]{2,1,0:T(1,128)} %reshape.271), calls=%async_computation.5 | async-start | bytes 196608 | tf_op jit(solution)/shard_map/all_to_all | solution.py:1088
  (94 other events, 623.6 us)

commit v4 on v3

--- a/solution.py
+++ b/solution.py
@@ -160,7 +160,7 @@
     multiple = sorted((m for m in wires.masks if m & (m - 1)), key=lambda m: -bin(m).count("1"))
     extra = [{} for _ in range(wires.deep)]
     before, total, clock = (), None, None
-    for step in range(wires.deep + 2):
+    for step in range(wires.deep + 3):
         now, ready = [], []
         ahead = (*(before if step else ()), *(pulls[step](clock) if step in pulls else ()))
 
@@ -171,7 +171,7 @@
             more = extra[block].get((mask, half), [])
             return sum([m.astype(WIDE) for m in more], mine).astype(LOW)
 
-        block = step - 2
+        block = step - 3
         if 0 <= block:
             total = (
                 sum([m.astype(WIDE) for m in extra[block][0, None]], part(block, 0).astype(WIDE))
@@ -1051,8 +1051,7 @@
 
     turning = [mask for mask in wires.masks if mask & (mask - 1)]
     riders = {
-        1: [send_result(mask) for mask in turning],
-        deep: [send_result(mask) for mask in wires.bits],
+        deep + 1: [send_result(mask) for mask in (*wires.bits, *turning)],
     }
 
     def partial_rows(step, d_rows):
@@ -1084,8 +1083,8 @@
     media_grad, latent_grad = kept["media"], kept["latent"]
     w_down_grad = kept["down"]
     up_sum = wires.swap_blocks(kept["up"], wires.planes)
-    w_up_grad = merge_units(up_sum, unit)
-    small_grads = lax.all_to_all(after(kept["small"], up_sum), AXES, 0, 0, tiled=True)
+    w_up_grad = merge_units(after(up_sum, result_got[0]), unit)
+    small_grads = lax.all_to_all(after(kept["small"], up_sum, result_got[0]), AXES, 0, 0, tiled=True)
     small_grads = jnp.sum(small_grads, axis=0)
     own_result = sum([rows.astype(WIDE) for rows in result_got], kept["own"])
     latents_out = ((middle + own_result) * live_mask).astype(LOW)

time: 438 us -> 426 us (0.973)
  starting transfers between devices: 105 us -> 87.1 us
    ppermute x64, waiting for transfers between devices: 124 us -> 139 us  [send(): return lax.ppermute(block, AXES, self.moves[kind])]
    ppermute x64, starting transfers between devices: 71.2 us -> 56 us  [send(): return lax.ppermute(block, AXES, self.moves[kind])]
    all_to_all x4, waiting for transfers between devices: 21.2 us -> 10.2 us  [swap_blocks(): lax.all_to_all(blocks, AXES, 0, 0, tiled=True, axis_index_groups=groups)]
  transfers between devices with their start and end apart: 70 -> 70, of which waited for: 31 -> 39; matrix products, arithmetic and copies ran while one was open for 17% -> 17% of each run, Pallas kernels for 14% -> 15%
where the time goes in v4:
time: 426 us; the launch traced here: 420 us
  waiting for transfers between devices  153 us (36%)
  starting transfers between devices  87.1 us (20%)
  Pallas kernels  79.9 us (19%)
  local copies, waits for them, and re-layouts  40.5 us (10%)
  other arithmetic  38.2 us (9%)
  matrix products  18.3 us (4%)
    ppermute x64, waiting for transfers between devices, send(): return lax.ppermute(block, AXES, self.moves[kind])  139 us
    ppermute x64, starting transfers between devices, send(): return lax.ppermute(block, AXES, self.moves[kind])  56 us
    pallas_call x1, Pallas kernels, attend(): pl.pallas_call(kernel, grid=(slots,), out_shape=(jax.ShapeDtypeStruct((mo...  24.1 us
    unnamed x149, local copies, waits for them, and re-layouts  18.9 us
    all_to_all x4, starting transfers between devices, swap_blocks(): lax.all_to_all(blocks, AXES, 0, 0, tiled=True, axis_index_groups=groups)  18.5 us
    dot_general x7, matrix products, dot(): lax.dot_general(left, right, (contract, ((), ())), preferred_element_type...  17.8 us
    pallas_call x1, Pallas kernels, ffn_rows_back(): pl.pallas_call(kernel, grid=(rows // block,), out_shape=(low, low, low, l...  13.3 us
    pallas_call x1, Pallas kernels, sources_back(): pl.pallas_call(kernel, grid=(images,), out_shape=(jax.ShapeDtypeStruct((i...  11.5 us
  transfers between devices with their start and end apart: 70, of which 39 were waited for; matrix products, arithmetic and copies ran while one was open for 17% of the time, Pallas kernels for 15%

profile of v4, /device:TPU:0, one launch (start us, length us, event | category | flops | bytes accessed | tf_op | source)
XLA Modules:
  0.0 420.3 jit_solution(10773203130524609421)
XLA Ops:
  5.8 7.3 %all-to-all-start = ((bf16[32,2,336]{2,1,0:T(2,128)(2,1)}), bf16[32,2,336]{2,1,0:T(2,128)(2,1)S(1)}, u32[]{:S(2)}, u32[]{:S(2)}) async-start(bf16[32,2,336]{2,1,0:T(2,128)(2,1)} %reshape.269), calls=%async_computation | async-start | bytes 98304 | tf_op jit(solution)/shard_map/all_to_all | solution.py:894
  24.7 4.4 %collective-permute-done.4.refs_2_ = bf16[2,48,2304]{2,1,0:T(8,128)(2,1)} collective-permute-done((bf16[2,48,2304]{2,1,0:T(8,128)(2,1)S(1)}, bf16[2,48,2304]{2,1,0:T(8,128)(2,1)}, u32[]{:S(2)}, u32[]{:S(2)}) %collective-permute-start.4) | collective-permute-done | bytes 442400 | tf_op jit(solution)/shard_map/ppermute | solution.py:87
  31.2 3.9 all-to-all-start.1
  38.3 3.8 collective-permute-done.2
  50.7 7.3 %collective-permute-done.9.refs_7_ = bf16[2,48,2304]{2,1,0:T(8,128)(2,1)S(1)} collective-permute-done((bf16[2,48,2304]{2,1,0:T(8,128)(2,1)S(1)}, bf16[2,48,2304]{2,1,0:T(8,128)(2,1)S(1)}, u32[]{:S(2)}, u32[]{:S(2)}) %collective-permute-start.9) | collective-permute-done | bytes 442400 | tf_op jit(solution)/shard_map/ppermute | solution.py:87
  58.9 4.3 %collective-permute-done.7 = bf16[144,2304]{1,0:T(8,128)(2,1)} collective-permute-done((bf16[144,2304]{1,0:T(8,128)(2,1)}, bf16[144,2304]{1,0:T(8,128)(2,1)}, u32[]{:S(2)}, u32[]{:S(2)}) %collective-permute-start.7) | collective-permute-done | bytes 663584 | tf_op jit(solution)/shard_map/ppermute | solution.py:87
  64.3 2.6 broadcast_in_dim.57
  72.0 6.2 %collective-permute-done.14.refs_12_ = bf16[2,48,2304]{2,1,0:T(8,128)(2,1)S(1)} collective-permute-done((bf16[2,48,2304]{2,1,0:T(8,128)(2,1)S(1)}, bf16[2,48,2304]{2,1,0:T(8,128)(2,1)S(1)}, u32[]{:S(2)}, u32[]{:S(2)}) %collective-permute-start.14) | collective-permute-done | bytes 442400 | tf_op jit(solution)/shard_map/ppermute | solution.py:87
  80.0 5.4 %collective-permute-done.12 = bf16[144,2304]{1,0:T(8,128)(2,1)S(1)} collective-permute-done((bf16[144,2304]{1,0:T(8,128)(2,1)}, bf16[144,2304]{1,0:T(8,128)(2,1)S(1)}, u32[]{:S(2)}, u32[]{:S(2)}) %collective-permute-start.12) | collective-permute-done | bytes 663584 | tf_op jit(solution)/shard_map/ppermute | solution.py:87
  89.7 5.2 %all-to-all-start.2 = ((bf16[4,384,1536]{2,1,0:T(8,128)(2,1)}), bf16[4,384,1536]{2,1,0:T(8,128)(2,1)}, u32[]{:S(2)}, u32[]{:S(2)}) async-start(bf16[4,384,1536]{2,1,0:T(8,128)(2,1)} %broadcast_in_dim.57), calls=%async_computation.2 | async-start | bytes 9437184 | tf_op jit(solution)/shard_map/all_to_all | solution.py:90
  95.0 5.9 %collective-permute-done.20.refs_14_ = bf16[48,2304]{1,0:T(8,128)(2,1)} collective-permute-done((bf16[48,2304]{1,0:T(8,128)(2,1)S(1)}, bf16[48,2304]{1,0:T(8,128)(2,1)}, u32[]{:S(2)}, u32[]{:S(2)}) %collective-permute-start.20) | collective-permute-done | bytes 221216 | tf_op jit(solution)/shard_map/ppermute | solution.py:87
  103.5 5.7 %collective-permute-done.22.refs_19_ = bf16[48,2304]{1,0:T(8,128)(2,1)S(1)} collective-permute-done((bf16[48,2304]{1,0:T(8,128)(2,1)S(1)}, bf16[48,2304]{1,0:T(8,128)(2,1)S(1)}, u32[]{:S(2)}, u32[]{:S(2)}) %collective-permute-start.22) | collective-permute-done | bytes 221216 | tf_op jit(solution)/shard_map/ppermute | solution.py:87
  109.2 6.3 %collective-permute-done.21.refs_18_ = bf16[48,2304]{1,0:T(8,128)(2,1)S(1)} collective-permute-done((bf16[48,2304]{1,0:T(8,128)(2,1)S(1)}, bf16[48,2304]{1,0:T(8,128)(2,1)S(1)}, u32[]{:S(2)}, u32[]{:S(2)}) %collective-permute-start.21) | collective-permute-done | bytes 221216 | tf_op jit(solution)/shard_map/ppermute | solution.py:87
  123.0 24.1 %shard_map.282 = (bf16[1536,2304]{1,0:T(8,128)(2,1)}, bf16[4,320,1536]{2,1,0:T(8,128)(2,1)}, bf16[4,64,768]{2,1,0:T(8,128)(2,1)}, bf16[4,320,1536]{2,1,0:T(8,128...) custom-call(s32[32]{0:T(128)} %stack.324.places_ref, bf16[2,48,2304]{2,1,0:T(8,128)(2,1)} %copy-done.26, ...), custom_call_target="tpu_custom_call" | custom-call | flops 1 | bytes 1 | tf_op jit(solution)/shard_map/pallas_call | solution.py:491
  148.2 5.4 %shard_map.283 = (bf16[768,1536]{1,0:T(8,128)(2,1)S(1)}, f32[256,1536]{1,0:T(8,128)S(1)}) custom-call(s32[16]{0:T(128)S(1)} %stack.282.places_ref, bf16[4,48,1536]{2,1,0:T(8,128)(2,1)S(1)} %pad_maximum_fusion.4.refs_0_, bf16[4,48,1536]{2,1,0:T(8,128)(2,1)S(1)} %collective-permute-done.23.refs_1_, bf16[4,48,1536]{2,1,0:T(8,128)(2,1)S(1)} %collective-permute-done.24.refs_2_, ...), custom_call_target="tpu_custom_call" | custom-call | flops 1 | bytes 1 | tf_op jit(solution)/shard_map/pallas_call | solution.py:624
  163.2 6.7 %collective-permute-done.29 = bf16[2,64,1536]{2,1,0:T(8,128)(2,1)S(1)} collective-permute-done((bf16[2,64,1536]{2,1,0:T(8,128)(2,1)S(1)}, bf16[2,64,1536]{2,1,0:T(8,128)(2,1)S(1)}, u32[]{:S(2)}, u32[]{:S(2)}) %collective-permute-start.29) | collective-permute-done | bytes 393248 | tf_op jit(solution)/shard_map/ppermute | solution.py:87
  169.9 8.7 %collective-permute-done.30 = bf16[2,64,1536]{2,1,0:T(8,128)(2,1)S(1)} collective-permute-done((bf16[2,64,1536]{2,1,0:T(8,128)(2,1)S(1)}, bf16[2,64,1536]{2,1,0:T(8,128)(2,1)S(1)}, u32[]{:S(2)}, u32[]{:S(2)}) %collective-permute-start.30) | collective-permute-done | bytes 393248 | tf_op jit(solution)/shard_map/ppermute | solution.py:87
  180.2 2.2 collective-permute-done.32
  183.5 9.9 %all-to-all-done.2.refs_0_ = bf16[4,384,1536]{2,1,0:T(8,128)(2,1)} async-done(((bf16[4,384,1536]{2,1,0:T(8,128)(2,1)}), bf16[4,384,1536]{2,1,0:T(8,128)(2,1)}, u32[]{:S(2)}, u32[]{:S(2)}) %all-to-all-start.2) | async-done | bytes 4718624 | tf_op jit(solution)/shard_map/all_to_all | solution.py:90
  196.2 13.3 %shard_map.284 = (bf16[512,768]{1,0:T(8,128)(2,1)S(1)}, bf16[512,768]{1,0:T(8,128)(2,1)S(1)}, bf16[512,768]{1,0:T(8,128)(2,1)S(1)}, bf16[512,768]{1,0:T(8,128)(2...) custom-call(bf16[512,1536]{1,0:T(8,128)(2,1)S(1)} %bitcast.350, ...), custom_call_target="tpu_custom_call" | custom-call | flops 1 | bytes 1 | tf_op jit(solution)/shard_map/pallas_call | solution.py:728
  209.7 3.4 collective-permute-done.34
  217.4 11.0 %shard_map.285 = bf16[4,384,1536]{2,1,0:T(8,128)(2,1)} custom-call(bf16[512,1536]{1,0:T(8,128)(2,1)} %bitcast.351, bf16[512,1536]{1,0:T(8,128)(2,1)} %bitcast.358, bf16[512,1536]{1,0:T(8,128)(2,1)} %bitcast.349, bf16[512,1536]{1,0:T(8,128)(2,1)} %bitcast.356, bf16[512,768]{1,0:T(8,128)(2,1)} %copy-done.12, bf16[512,768]{1,0:T(8,128)(2,1)} %copy-done.13, ...), custom_call_target="tpu_custom_call" | custom-call | flops 1 | bytes 1 | tf_op jit(solution)/shard_map/pallas_call | solution.py:782
  228.5 5.9 %collective-permute-done.36 = bf16[2,64,1536]{2,1,0:T(8,128)(2,1)S(1)} collective-permute-done((bf16[2,64,1536]{2,1,0:T(8,128)(2,1)S(1)}, bf16[2,64,1536]{2,1,0:T(8,128)(2,1)S(1)}, u32[]{:S(2)}, u32[]{:S(2)}) %collective-permute-start.36) | collective-permute-done | bytes 393248 | tf_op jit(solution)/shard_map/ppermute | solution.py:87
  236.2 5.1 %all-to-all-start.3 = ((bf16[4,384,1536]{2,1,0:T(8,128)(2,1)}), bf16[4,384,1536]{2,1,0:T(8,128)(2,1)}, u32[]{:S(2)}, u32[]{:S(2)}) async-start(bf16[4,384,1536]{2,1,0:T(8,128)(2,1)} %shard_map.285), calls=%async_computation.3 | async-start | bytes 9437184 | tf_op jit(solution)/shard_map/all_to_all | solution.py:90
  247.5 6.0 %shard_map.286 = bf16[4,320,2304]{2,1,0:T(8,128)(2,1)S(1)} custom-call(bf16[4,64,768]{2,1,0:T(8,128)(2,1)S(1)} %fusion.8.d_ref, bf16[4,64,768]{2,1,0:T(8,128)(2,1)S(1)} %copy-done.18, bf16[4,320,1536]{2,1,0:T(8,128)(2,1)S(1)} %copy-done.8, f32[4,2,256,320]{3,2,1,0:T(8,128)S(1)} %copy-done.9), custom_call_target="tpu_custom_call" | custom-call | flops 1 | bytes 1 | tf_op jit(solution)/shard_map/pallas_call | solution.py:827
  256.7 2.5 convolution_convert_fusion
  259.2 2.5 convolution_convert_fusion.1
  261.7 2.5 convolution_convert_fusion.2
  264.3 2.5 convolution_convert_fusion.3
  266.8 6.1 %fusion.2 = bf16[2,320,1536]{2,1,0:T(8,128)(2,1)} fusion(bf16[4,320,2304]{2,1,0:T(8,128)(2,1)S(1)} %shard_map.286, bf16[1536,2304]{1,0:T(8,128)(2,1)S(1)} %bitcast.361), kind=kOutput, calls=%fused_computation.41 | convolution fusion | flops 4530831360 | bytes 14942208 | tf_op jit(solution)/shard_map/dot_general | solution.py:33
  279.3 3.3 collective-permute-done.40
  291.3 5.7 %collective-permute-done.45 = bf16[48,3072]{1,0:T(8,128)(2,1)S(1)} collective-permute-done((bf16[48,3072]{1,0:T(8,128)(2,1)S(1)}, bf16[48,3072]{1,0:T(8,128)(2,1)S(1)}, u32[]{:S(2)}, u32[]{:S(2)}) %collective-permute-start.45) | collective-permute-done | bytes 294944 | tf_op jit(solution)/shard_map/ppermute | solution.py:87
  300.6 7.7 %collective-permute-done.43 = bf16[2,48,3072]{2,1,0:T(8,128)(2,1)S(1)} collective-permute-done((bf16[2,48,3072]{2,1,0:T(8,128)(2,1)S(1)}, bf16[2,48,3072]{2,1,0:T(8,128)(2,1)S(1)}, u32[]{:S(2)}, u32[]{:S(2)}) %collective-permute-start.43) | collective-permute-done | bytes 589856 | tf_op jit(solution)/shard_map/ppermute | solution.py:87
  314.8 4.7 %collective-permute-done.49 = bf16[48,3072]{1,0:T(8,128)(2,1)S(1)} collective-permute-done((bf16[48,3072]{1,0:T(8,128)(2,1)S(1)}, bf16[48,3072]{1,0:T(8,128)(2,1)S(1)}, u32[]{:S(2)}, u32[]{:S(2)}) %collective-permute-start.49) | collective-permute-done | bytes 294944 | tf_op jit(solution)/shard_map/ppermute | solution.py:87
  322.1 11.5 %shard_map.287 = (f32[2,256,1536]{2,1,0:T(8,128)}, f32[2,64,1536]{2,1,0:T(8,128)}, f32[2,8,1536]{2,1,0:T(8,128)S(1)}) custom-call(bf16[2,320,2304]{2,1,0:T(8,128)(2,1)} %slice.329.d_ref, bf16[1536,2304]{1,0:T(8,128)(2,1)} %get-tuple-element.146.w_ref, bf16[2,320,1536]{2,1,0:T(8,128)(2,1)S(1)} %collective-permute-done.50.far_ref, ...), custom_call_target="tpu_custom_call" | custom-call | flops 1 | bytes 1 | tf_op jit(solution)/shard_map/pallas_call | solution.py:563
  342.3 2.8 collective-permute-done.55
  345.2 2.1 collective-permute-done.54
  349.2 7.4 %collective-permute-done.51 = bf16[2,48,3072]{2,1,0:T(8,128)(2,1)S(1)} collective-permute-done((bf16[2,48,3072]{2,1,0:T(8,128)(2,1)}, bf16[2,48,3072]{2,1,0:T(8,128)(2,1)S(1)}, u32[]{:S(2)}, u32[]{:S(2)}) %collective-permute-start.51) | collective-permute-done | bytes 589856 | tf_op jit(solution)/shard_map/ppermute | solution.py:87
  356.6 2.4 add_convert_fusion.1
  359.2 3.3 convert_reduce_fusion
  366.8 4.3 %all-to-all-start.4 = ((bf16[8,48,768]{2,1,0:T(8,128)(2,1)}), bf16[8,48,768]{2,1,0:T(8,128)(2,1)}, u32[]{:S(2)}, u32[]{:S(2)}) async-start(bf16[8,48,768]{2,1,0:T(8,128)(2,1)} %bitcast.367), calls=%async_computation.4 | async-start | bytes 1179648 | tf_op jit(solution)/shard_map/all_to_all | solution.py:90
  372.3 7.9 %collective-permute-done.58 = bf16[2,48,3072]{2,1,0:T(8,128)(2,1)} collective-permute-done((bf16[2,48,3072]{2,1,0:T(8,128)(2,1)}, bf16[2,48,3072]{2,1,0:T(8,128)(2,1)}, u32[]{:S(2)}, u32[]{:S(2)}) %collective-permute-start.58) | collective-permute-done | bytes 589856 | tf_op jit(solution)/shard_map/ppermute | solution.py:87
  388.2 7.8 %collective-permute-done.59 = bf16[2,64,1536]{2,1,0:T(8,128)(2,1)} collective-permute-done((bf16[2,64,1536]{2,1,0:T(8,128)(2,1)}, bf16[2,64,1536]{2,1,0:T(8,128)(2,1)}, u32[]{:S(2)}, u32[]{:S(2)}) %collective-permute-start.59) | collective-permute-done | bytes 393248 | tf_op jit(solution)/shard_map/ppermute | solution.py:87
  397.0 5.4 %all-to-all-start.5 = ((f32[32,1,672]{2,1,0:T(1,128)}), f32[32,1,672]{2,1,0:T(1,128)S(1)}, u32[]{:S(2)}, u32[]{:S(2)}) async-start(f32[32,1,672]{2,1,0:T(1,128)} %reshape.271), calls=%async_computation.5 | async-start | bytes 196608 | tf_op jit(solution)/shard_map/all_to_all | solution.py:1087
  403.1 2.2 multiply_convert_fusion
  405.3 2.4 shard_map.289
  407.8 2.5 all-to-all-done.5
  417.9 2.2 shard_map.288
  (382 shorter events, 145.4 us)
Async XLA Ops:
  5.8 14.7 %all-to-all-start = ((bf16[32,2,336]{2,1,0:T(2,128)(2,1)}), bf16[32,2,336]{2,1,0:T(2,128)(2,1)S(1)}, u32[]{:S(2)}, u32[]{:S(2)}) async-start(bf16[32,2,336]{2,1,0:T(2,128)(2,1)} %reshape.269), calls=%async_computation | async-start | bytes 98304 | tf_op jit(solution)/shard_map/all_to_all | solution.py:894
  15.8 13.3 %collective-permute-start.4 = (bf16[2,48,2304]{2,1,0:T(8,128)(2,1)S(1)}, bf16[2,48,2304]{2,1,0:T(8,128)(2,1)}, u32[]{:S(2)}, u32[]{:S(2)}) collective-permute-start(bf16[2,48,2304]{2,1,0:T(8,128)(2,1)S(1)} %maximum_select_fusion.refs_0_), channel_id=1, source_target_pairs={{0,2},{1,3},{2,0},{3,1},{4,6},{5,7},{6,4},{7,5},{8,10},{9,11},{10,... | collective-permute-start | bytes 1327112 | tf_op jit(solution)/shard_map/ppermute | solution.py:87
  21.6 15.1 %collective-permute-start.3 = (bf16[2,48,2304]{2,1,0:T(8,128)(2,1)S(1)}, bf16[2,48,2304]{2,1,0:T(8,128)(2,1)}, u32[]{:S(2)}, u32[]{:S(2)}) collective-permute-start(bf16[2,48,2304]{2,1,0:T(8,128)(2,1)S(1)} %maximum_select_fusion.refs_0_), channel_id=1, source_target_pairs={{0,1},{1,0},{2,3},{3,2},{4,5},{5,4},{6,7},{7,6},{8,9},{9,8},{10,11... | collective-permute-start | bytes 1327112 | tf_op jit(solution)/shard_map/ppermute | solution.py:87
  22.0 21.0 %collective-permute-start.5 = (bf16[2,64,1536]{2,1,0:T(8,128)(2,1)}, bf16[2,64,1536]{2,1,0:T(8,128)(2,1)S(1)}, u32[]{:S(2)}, u32[]{:S(2)}) collective-permute-start(bf16[2,64,1536]{2,1,0:T(8,128)(2,1)} %broadcast_multiply_fusion), channel_id=1, source_target_pairs={{0,1},{1,0},{2,3},{3,2},{4,5},{5,4},{6,7},{7,6},{8,9},{9,8},{10,11... | collective-permute-start | bytes 1179656 | tf_op jit(solution)/shard_map/ppermute | solution.py:87
  23.6 19.5 %collective-permute-start.6 = (bf16[2,64,1536]{2,1,0:T(8,128)(2,1)}, bf16[2,64,1536]{2,1,0:T(8,128)(2,1)}, u32[]{:S(2)}, u32[]{:S(2)}) collective-permute-start(bf16[2,64,1536]{2,1,0:T(8,128)(2,1)} %broadcast_multiply_fusion), channel_id=1, source_target_pairs={{0,2},{1,3},{2,0},{3,1},{4,6},{5,7},{6,4},{7,5},{8,10},{9,11},{10,... | collective-permute-start | bytes 1179656 | tf_op jit(solution)/shard_map/ppermute | solution.py:87
  24.1 18.0 %collective-permute-start.2 = (bf16[144,2304]{1,0:T(8,128)(2,1)}, bf16[144,2304]{1,0:T(8,128)(2,1)S(1)}, u32[]{:S(2)}, u32[]{:S(2)}) collective-permute-start(bf16[144,2304]{1,0:T(8,128)(2,1)} %fusion.23), channel_id=1, source_target_pairs={{0,8},{1,9},{2,10},{3,11},{4,12},{5,13},{6,14},{7,15},{8,16},{9,17... | collective-permute-start | bytes 1990664 | tf_op jit(solution)/shard_map/ppermute | solution.py:87
  31.2 18.3 %all-to-all-start.1 = ((bf16[8,48,768]{2,1,0:T(8,128)(2,1)}), bf16[8,48,768]{2,1,0:T(8,128)(2,1)S(1)}, u32[]{:S(2)}, u32[]{:S(2)}) async-start(bf16[8,48,768]{2,1,0:T(8,128)(2,1)} %shard_map.281), calls=%async_computation.1 | async-start | bytes 1179648 | tf_op jit(solution)/shard_map/all_to_all | solution.py:90
  43.8 14.1 %collective-permute-start.9 = (bf16[2,48,2304]{2,1,0:T(8,128)(2,1)S(1)}, bf16[2,48,2304]{2,1,0:T(8,128)(2,1)S(1)}, u32[]{:S(2)}, u32[]{:S(2)}) collective-permute-start(bf16[2,48,2304]{2,1,0:T(8,128)(2,1)S(1)} %bitcast.372), channel_id=1, source_target_pairs={{0,2},{1,3},{2,0},{3,1},{4,6},{5,7},{6,4},{7,5},{8,10},{9,11},{10,... | collective-permute-start | bytes 1327112 | tf_op jit(solution)/shard_map/ppermute | solution.py:87
  44.4 14.5 %collective-permute-start.8 = (bf16[2,48,2304]{2,1,0:T(8,128)(2,1)S(1)}, bf16[2,48,2304]{2,1,0:T(8,128)(2,1)S(1)}, u32[]{:S(2)}, u32[]{:S(2)}) collective-permute-start(bf16[2,48,2304]{2,1,0:T(8,128)(2,1)S(1)} %bitcast.373), channel_id=1, source_target_pairs={{0,1},{1,0},{2,3},{3,2},{4,5},{5,4},{6,7},{7,6},{8,9},{9,8},{10,11... | collective-permute-start | bytes 1327112 | tf_op jit(solution)/shard_map/ppermute | solution.py:87
  45.2 19.1 %collective-permute-start.11 = (bf16[48,2304]{1,0:T(8,128)(2,1)}, bf16[48,2304]{1,0:T(8,128)(2,1)}, u32[]{:S(2)}, u32[]{:S(2)}) collective-permute-start(bf16[48,2304]{1,0:T(8,128)(2,1)} %slice_bitcast_fusion.8), channel_id=1, source_target_pairs={{0,1},{1,0},{2,3},{3,2},{4,5},{5,4},{6,7},{7,6},{8,9},{9,8},{10,11... | collective-permute-start | bytes 663560 | tf_op jit(solution)/shard_map/ppermute | solution.py:87
  46.4 17.9 %collective-permute-start.10 = (bf16[48,2304]{1,0:T(8,128)(2,1)}, bf16[48,2304]{1,0:T(8,128)(2,1)}, u32[]{:S(2)}, u32[]{:S(2)}) collective-permute-start(bf16[48,2304]{1,0:T(8,128)(2,1)} %slice_bitcast_fusion.9), channel_id=1, source_target_pairs={{0,2},{1,3},{2,0},{3,1},{4,6},{5,7},{6,4},{7,5},{8,10},{9,11},{10,... | collective-permute-start | bytes 663560 | tf_op jit(solution)/shard_map/ppermute | solution.py:87
  47.9 15.4 %collective-permute-start.7 = (bf16[144,2304]{1,0:T(8,128)(2,1)}, bf16[144,2304]{1,0:T(8,128)(2,1)}, u32[]{:S(2)}, u32[]{:S(2)}) collective-permute-start(bf16[144,2304]{1,0:T(8,128)(2,1)} %copy-done.49), channel_id=1, source_target_pairs={{0,8},{1,9},{2,10},{3,11},{4,12},{5,13},{6,14},{7,15},{8,16},{9,17... | collective-permute-start | bytes 1990664 | tf_op jit(solution)/shard_map/ppermute | solution.py:87
  69.1 16.5 %collective-permute-start.16 = (bf16[48,2304]{1,0:T(8,128)(2,1)S(1)}, bf16[48,2304]{1,0:T(8,128)(2,1)S(1)}, u32[]{:S(2)}, u32[]{:S(2)}) collective-permute-start(bf16[48,2304]{1,0:T(8,128)(2,1)S(1)} %slice_bitcast_fusion.6), channel_id=1, source_target_pairs={{0,1},{1,0},{2,3},{3,2},{4,5},{5,4},{6,7},{7,6},{8,9},{9,8},{10,11... | collective-permute-start | bytes 663560 | tf_op jit(solution)/shard_map/ppermute | solution.py:87
  70.0 15.5 %collective-permute-start.15 = (bf16[48,2304]{1,0:T(8,128)(2,1)S(1)}, bf16[48,2304]{1,0:T(8,128)(2,1)S(1)}, u32[]{:S(2)}, u32[]{:S(2)}) collective-permute-start(bf16[48,2304]{1,0:T(8,128)(2,1)S(1)} %slice_bitcast_fusion.7), channel_id=1, source_target_pairs={{0,2},{1,3},{2,0},{3,1},{4,6},{5,7},{6,4},{7,5},{8,10},{9,11},{10,... | collective-permute-start | bytes 663560 | tf_op jit(solution)/shard_map/ppermute | solution.py:87
  71.0 14.5 %collective-permute-start.12 = (bf16[144,2304]{1,0:T(8,128)(2,1)}, bf16[144,2304]{1,0:T(8,128)(2,1)S(1)}, u32[]{:S(2)}, u32[]{:S(2)}) collective-permute-start(bf16[144,2304]{1,0:T(8,128)(2,1)} %collective-permute-done.7), channel_id=1, source_target_pairs={{0,8},{1,9},{2,10},{3,11},{4,12},{5,13},{6,14},{7,15},{8,16},{9,17... | collective-permute-start | bytes 1990664 | tf_op jit(solution)/shard_map/ppermute | solution.py:87
  86.9 14.0 %collective-permute-start.17 = (bf16[2,48,2304]{2,1,0:T(8,128)(2,1)S(1)}, bf16[2,48,2304]{2,1,0:T(8,128)(2,1)S(1)}, u32[]{:S(2)}, u32[]{:S(2)}) collective-permute-start(bf16[2,48,2304]{2,1,0:T(8,128)(2,1)S(1)} %bitcast.379), channel_id=1, source_target_pairs={{0,1},{1,0},{2,3},{3,2},{4,5},{5,4},{6,7},{7,6},{8,9},{9,8},{10,11... | collective-permute-start | bytes 1327112 | tf_op jit(solution)/shard_map/ppermute | solution.py:87
  87.6 13.3 %collective-permute-start.20 = (bf16[48,2304]{1,0:T(8,128)(2,1)S(1)}, bf16[48,2304]{1,0:T(8,128)(2,1)}, u32[]{:S(2)}, u32[]{:S(2)}) collective-permute-start(bf16[48,2304]{1,0:T(8,128)(2,1)S(1)} %slice_bitcast_fusion.3), channel_id=1, source_target_pairs={{0,1},{1,0},{2,3},{3,2},{4,5},{5,4},{6,7},{7,6},{8,9},{9,8},{10,11... | collective-permute-start | bytes 663560 | tf_op jit(solution)/shard_map/ppermute | solution.py:87
  89.0 12.0 %collective-permute-start.19 = (bf16[48,2304]{1,0:T(8,128)(2,1)}, bf16[48,2304]{1,0:T(8,128)(2,1)}, u32[]{:S(2)}, u32[]{:S(2)}) collective-permute-start(bf16[48,2304]{1,0:T(8,128)(2,1)} %slice_bitcast_fusion.4), channel_id=1, source_target_pairs={{0,2},{1,3},{2,0},{3,1},{4,6},{5,7},{6,4},{7,5},{8,10},{9,11},{10,... | collective-permute-start | bytes 663560 | tf_op jit(solution)/shard_map/ppermute | solution.py:87
  89.7 103.7 %all-to-all-start.2 = ((bf16[4,384,1536]{2,1,0:T(8,128)(2,1)}), bf16[4,384,1536]{2,1,0:T(8,128)(2,1)}, u32[]{:S(2)}, u32[]{:S(2)}) async-start(bf16[4,384,1536]{2,1,0:T(8,128)(2,1)} %broadcast_in_dim.57), calls=%async_computation.2 | async-start | bytes 9437184 | tf_op jit(solution)/shard_map/all_to_all | solution.py:90
  101.5 14.0 %collective-permute-start.21 = (bf16[48,2304]{1,0:T(8,128)(2,1)S(1)}, bf16[48,2304]{1,0:T(8,128)(2,1)S(1)}, u32[]{:S(2)}, u32[]{:S(2)}) collective-permute-start(bf16[48,2304]{1,0:T(8,128)(2,1)S(1)} %slice_bitcast_fusion.5), channel_id=1, source_target_pairs={{0,2},{1,3},{2,0},{3,1},{4,6},{5,7},{6,4},{7,5},{8,10},{9,11},{10,... | collective-permute-start | bytes 663560 | tf_op jit(solution)/shard_map/ppermute | solution.py:87
  116.2 31.0 %collective-permute-start.23 = (bf16[4,48,1536]{2,1,0:T(8,128)(2,1)S(1)}, bf16[4,48,1536]{2,1,0:T(8,128)(2,1)S(1)}, u32[]{:S(2)}, u32[]{:S(2)}) collective-permute-start(bf16[4,48,1536]{2,1,0:T(8,128)(2,1)S(1)} %pad_maximum_fusion.4.refs_0_), channel_id=1, source_target_pairs={{0,3},{1,2},{2,1},{3,0},{4,7},{5,6},{6,5},{7,4},{8,11},{9,10},{10,... | collective-permute-start | bytes 1769480 | tf_op jit(solution)/shard_map/ppermute | solution.py:87
  117.8 29.4 %collective-permute-start.24 = (bf16[4,48,1536]{2,1,0:T(8,128)(2,1)S(1)}, bf16[4,48,1536]{2,1,0:T(8,128)(2,1)S(1)}, u32[]{:S(2)}, u32[]{:S(2)}) collective-permute-start(bf16[4,48,1536]{2,1,0:T(8,128)(2,1)S(1)} %pad_maximum_fusion.4.refs_0_), channel_id=1, source_target_pairs={{0,2},{1,3},{2,0},{3,1},{4,6},{5,7},{6,4},{7,5},{8,10},{9,11},{10,... | collective-permute-start | bytes 1769480 | tf_op jit(solution)/shard_map/ppermute | solution.py:87
  119.1 28.0 %collective-permute-start.25 = (bf16[4,48,1536]{2,1,0:T(8,128)(2,1)S(1)}, bf16[4,48,1536]{2,1,0:T(8,128)(2,1)S(1)}, u32[]{:S(2)}, u32[]{:S(2)}) collective-permute-start(bf16[4,48,1536]{2,1,0:T(8,128)(2,1)S(1)} %pad_maximum_fusion.4.refs_0_), channel_id=1, source_target_pairs={{0,1},{1,0},{2,3},{3,2},{4,5},{5,4},{6,7},{7,6},{8,9},{9,8},{10,11... | collective-permute-start | bytes 1769480 | tf_op jit(solution)/shard_map/ppermute | solution.py:87
  119.9 27.3 %collective-permute-start.27 = (bf16[2,64,1536]{2,1,0:T(8,128)(2,1)}, bf16[2,64,1536]{2,1,0:T(8,128)(2,1)}, u32[]{:S(2)}, u32[]{:S(2)}) collective-permute-start(bf16[2,64,1536]{2,1,0:T(8,128)(2,1)} %broadcast_multiply_fusion), channel_id=1, source_target_pairs={{0,3},{1,2},{2,1},{3,0},{4,7},{5,6},{6,5},{7,4},{8,11},{9,10},{10,... | collective-permute-start | bytes 1179656 | tf_op jit(solution)/shard_map/ppermute | solution.py:87
  157.9 12.0 %collective-permute-start.29 = (bf16[2,64,1536]{2,1,0:T(8,128)(2,1)S(1)}, bf16[2,64,1536]{2,1,0:T(8,128)(2,1)S(1)}, u32[]{:S(2)}, u32[]{:S(2)}) collective-permute-start(bf16[2,64,1536]{2,1,0:T(8,128)(2,1)S(1)} %add_convert_fusion.3), channel_id=1, source_target_pairs={{0,1},{1,0},{2,3},{3,2},{4,5},{5,4},{6,7},{7,6},{8,9},{9,8},{10,11... | collective-permute-start | bytes 1179656 | tf_op jit(solution)/shard_map/ppermute | solution.py:87
  159.3 19.3 %collective-permute-start.30 = (bf16[2,64,1536]{2,1,0:T(8,128)(2,1)S(1)}, bf16[2,64,1536]{2,1,0:T(8,128)(2,1)S(1)}, u32[]{:S(2)}, u32[]{:S(2)}) collective-permute-start(bf16[2,64,1536]{2,1,0:T(8,128)(2,1)S(1)} %add_convert_fusion.3), channel_id=1, source_target_pairs={{0,2},{1,3},{2,0},{3,1},{4,6},{5,7},{6,4},{7,5},{8,10},{9,11},{10,... | collective-permute-start | bytes 1179656 | tf_op jit(solution)/shard_map/ppermute | solution.py:87
  159.9 18.8 %collective-permute-start.31 = (bf16[2,64,1536]{2,1,0:T(8,128)(2,1)S(1)}, bf16[2,64,1536]{2,1,0:T(8,128)(2,1)S(1)}, u32[]{:S(2)}, u32[]{:S(2)}) collective-permute-start(bf16[2,64,1536]{2,1,0:T(8,128)(2,1)S(1)} %add_convert_fusion.3), channel_id=1, source_target_pairs={{0,3},{1,2},{2,1},{3,0},{4,7},{5,6},{6,5},{7,4},{8,11},{9,10},{10,... | collective-permute-start | bytes 1179656 | tf_op jit(solution)/shard_map/ppermute | solution.py:87
  162.9 16.0 %collective-permute-start.33 = (bf16[4,2,64,1536]{3,2,1,0:T(8,128)(2,1)S(1)}, bf16[4,2,64,1536]{3,2,1,0:T(8,128)(2,1)S(1)}, u32[]{:S(2)}, u32[]{:S(2)}) collective-permute-start(bf16[4,2,64,1536]{3,2,1,0:T(8,128)(2,1)S(1)} %pad_maximum_fusion.2), channel_id=1, source_target_pairs={{0,4},{1,5},{2,6},{3,7},{4,0},{5,1},{6,2},{7,3},{8,12},{9,13},{10,... | collective-permute-start | bytes 4718600 | tf_op jit(solution)/shard_map/ppermute | solution.py:87
  213.8 14.6 %collective-permute-start.35 = (bf16[2,64,1536]{2,1,0:T(8,128)(2,1)S(1)}, bf16[2,64,1536]{2,1,0:T(8,128)(2,1)S(1)}, u32[]{:S(2)}, u32[]{:S(2)}) collective-permute-start(bf16[2,64,1536]{2,1,0:T(8,128)(2,1)S(1)} %bitcast.390), channel_id=1, source_target_pairs={{0,3},{1,2},{2,1},{3,0},{4,7},{5,6},{6,5},{7,4},{8,11},{9,10},{10,... | collective-permute-start | bytes 1179656 | tf_op jit(solution)/shard_map/ppermute | solution.py:87
  215.4 19.0 %collective-permute-start.36 = (bf16[2,64,1536]{2,1,0:T(8,128)(2,1)S(1)}, bf16[2,64,1536]{2,1,0:T(8,128)(2,1)S(1)}, u32[]{:S(2)}, u32[]{:S(2)}) collective-permute-start(bf16[2,64,1536]{2,1,0:T(8,128)(2,1)S(1)} %bitcast.388), channel_id=1, source_target_pairs={{0,2},{1,3},{2,0},{3,1},{4,6},{5,7},{6,4},{7,5},{8,10},{9,11},{10,... | collective-permute-start | bytes 1179656 | tf_op jit(solution)/shard_map/ppermute | solution.py:87
  217.0 17.4 %collective-permute-start.37 = (bf16[2,64,1536]{2,1,0:T(8,128)(2,1)S(1)}, bf16[2,64,1536]{2,1,0:T(8,128)(2,1)S(1)}, u32[]{:S(2)}, u32[]{:S(2)}) collective-permute-start(bf16[2,64,1536]{2,1,0:T(8,128)(2,1)S(1)} %bitcast.387), channel_id=1, source_target_pairs={{0,1},{1,0},{2,3},{3,2},{4,5},{5,4},{6,7},{7,6},{8,9},{9,8},{10,11... | collective-permute-start | bytes 1179656 | tf_op jit(solution)/shard_map/ppermute | solution.py:87
  236.2 123.0 %all-to-all-start.3 = ((bf16[4,384,1536]{2,1,0:T(8,128)(2,1)}), bf16[4,384,1536]{2,1,0:T(8,128)(2,1)}, u32[]{:S(2)}, u32[]{:S(2)}) async-start(bf16[4,384,1536]{2,1,0:T(8,128)(2,1)} %shard_map.285), calls=%async_computation.3 | async-start | bytes 9437184 | tf_op jit(solution)/shard_map/all_to_all | solution.py:90
  289.4 18.9 %collective-permute-start.43 = (bf16[2,48,3072]{2,1,0:T(8,128)(2,1)S(1)}, bf16[2,48,3072]{2,1,0:T(8,128)(2,1)S(1)}, u32[]{:S(2)}, u32[]{:S(2)}) collective-permute-start(bf16[2,48,3072]{2,1,0:T(8,128)(2,1)S(1)} %fusion.27), channel_id=1, source_target_pairs={{0,1},{1,0},{2,3},{3,2},{4,5},{5,4},{6,7},{7,6},{8,9},{9,8},{10,11... | collective-permute-start | bytes 1769480 | tf_op jit(solution)/shard_map/ppermute | solution.py:87
  290.7 19.1 %collective-permute-start.44 = (bf16[2,48,3072]{2,1,0:T(8,128)(2,1)S(1)}, bf16[2,48,3072]{2,1,0:T(8,128)(2,1)S(1)}, u32[]{:S(2)}, u32[]{:S(2)}) collective-permute-start(bf16[2,48,3072]{2,1,0:T(8,128)(2,1)S(1)} %pad_maximum_fusion.5), channel_id=1, source_target_pairs={{0,2},{1,3},{2,0},{3,1},{4,6},{5,7},{6,4},{7,5},{8,10},{9,11},{10,... | collective-permute-start | bytes 1769480 | tf_op jit(solution)/shard_map/ppermute | solution.py:87
  311.6 23.4 %collective-permute-start.47 = (bf16[2,48,3072]{2,1,0:T(8,128)(2,1)}, bf16[2,48,3072]{2,1,0:T(8,128)(2,1)}, u32[]{:S(2)}, u32[]{:S(2)}) collective-permute-start(bf16[2,48,3072]{2,1,0:T(8,128)(2,1)} %pad_maximum_fusion.6), channel_id=1, source_target_pairs={{0,2},{1,3},{2,0},{3,1},{4,6},{5,7},{6,4},{7,5},{8,10},{9,11},{10,... | collective-permute-start | bytes 1769480 | tf_op jit(solution)/shard_map/ppermute | solution.py:87
  312.2 22.8 %collective-permute-start.46 = (bf16[2,48,3072]{2,1,0:T(8,128)(2,1)}, bf16[2,48,3072]{2,1,0:T(8,128)(2,1)}, u32[]{:S(2)}, u32[]{:S(2)}) collective-permute-start(bf16[2,48,3072]{2,1,0:T(8,128)(2,1)} %fusion.25), channel_id=1, source_target_pairs={{0,1},{1,0},{2,3},{3,2},{4,5},{5,4},{6,7},{7,6},{8,9},{9,8},{10,11... | collective-permute-start | bytes 1769480 | tf_op jit(solution)/shard_map/ppermute | solution.py:87
  338.8 24.8 %collective-permute-start.53 = (bf16[2,48,3072]{2,1,0:T(8,128)(2,1)}, bf16[2,48,3072]{2,1,0:T(8,128)(2,1)}, u32[]{:S(2)}, u32[]{:S(2)}) collective-permute-start(bf16[2,48,3072]{2,1,0:T(8,128)(2,1)} %pad_maximum_fusion.7), channel_id=1, source_target_pairs={{0,2},{1,3},{2,0},{3,1},{4,6},{5,7},{6,4},{7,5},{8,10},{9,11},{10,... | collective-permute-start | bytes 1769480 | tf_op jit(solution)/shard_map/ppermute | solution.py:87
  339.4 24.2 %collective-permute-start.52 = (bf16[2,48,3072]{2,1,0:T(8,128)(2,1)}, bf16[2,48,3072]{2,1,0:T(8,128)(2,1)}, u32[]{:S(2)}, u32[]{:S(2)}) collective-permute-start(bf16[2,48,3072]{2,1,0:T(8,128)(2,1)} %fusion.29), channel_id=1, source_target_pairs={{0,1},{1,0},{2,3},{3,2},{4,5},{5,4},{6,7},{7,6},{8,9},{9,8},{10,11... | collective-permute-start | bytes 1769480 | tf_op jit(solution)/shard_map/ppermute | solution.py:87
  340.9 15.7 %collective-permute-start.51 = (bf16[2,48,3072]{2,1,0:T(8,128)(2,1)}, bf16[2,48,3072]{2,1,0:T(8,128)(2,1)S(1)}, u32[]{:S(2)}, u32[]{:S(2)}) collective-permute-start(bf16[2,48,3072]{2,1,0:T(8,128)(2,1)} %add_convert_fusion.2), channel_id=1, source_target_pairs={{0,8},{1,9},{2,10},{3,11},{4,12},{5,13},{6,14},{7,15},{8,16},{9,17... | collective-permute-start | bytes 1769480 | tf_op jit(solution)/shard_map/ppermute | solution.py:87
  363.6 16.6 %collective-permute-start.58 = (bf16[2,48,3072]{2,1,0:T(8,128)(2,1)}, bf16[2,48,3072]{2,1,0:T(8,128)(2,1)}, u32[]{:S(2)}, u32[]{:S(2)}) collective-permute-start(bf16[2,48,3072]{2,1,0:T(8,128)(2,1)} %pad_maximum_fusion.9), channel_id=1, source_target_pairs={{0,2},{1,3},{2,0},{3,1},{4,6},{5,7},{6,4},{7,5},{8,10},{9,11},{10,... | collective-permute-start | bytes 1769480 | tf_op jit(solution)/shard_map/ppermute | solution.py:87
  365.0 16.6 %collective-permute-start.57 = (bf16[2,48,3072]{2,1,0:T(8,128)(2,1)}, bf16[2,48,3072]{2,1,0:T(8,128)(2,1)}, u32[]{:S(2)}, u32[]{:S(2)}) collective-permute-start(bf16[2,48,3072]{2,1,0:T(8,128)(2,1)} %fusion.31), channel_id=1, source_target_pairs={{0,1},{1,0},{2,3},{3,2},{4,5},{5,4},{6,7},{7,6},{8,9},{9,8},{10,11... | collective-permute-start | bytes 1769480 | tf_op jit(solution)/shard_map/ppermute | solution.py:87
  365.8 17.1 %collective-permute-start.56 = (bf16[2,48,3072]{2,1,0:T(8,128)(2,1)}, bf16[2,48,3072]{2,1,0:T(8,128)(2,1)}, u32[]{:S(2)}, u32[]{:S(2)}) collective-permute-start(bf16[2,48,3072]{2,1,0:T(8,128)(2,1)} %add_convert_fusion.1), channel_id=1, source_target_pairs={{0,8},{1,9},{2,10},{3,11},{4,12},{5,13},{6,14},{7,15},{8,16},{9,17... | collective-permute-start | bytes 1769480 | tf_op jit(solution)/shard_map/ppermute | solution.py:87
  366.8 21.4 %all-to-all-start.4 = ((bf16[8,48,768]{2,1,0:T(8,128)(2,1)}), bf16[8,48,768]{2,1,0:T(8,128)(2,1)}, u32[]{:S(2)}, u32[]{:S(2)}) async-start(bf16[8,48,768]{2,1,0:T(8,128)(2,1)} %bitcast.367), calls=%async_computation.4 | async-start | bytes 1179648 | tf_op jit(solution)/shard_map/all_to_all | solution.py:90
  382.9 13.2 %collective-permute-start.59 = (bf16[2,64,1536]{2,1,0:T(8,128)(2,1)}, bf16[2,64,1536]{2,1,0:T(8,128)(2,1)}, u32[]{:S(2)}, u32[]{:S(2)}) collective-permute-start(bf16[2,64,1536]{2,1,0:T(8,128)(2,1)} %bitcast.109), channel_id=1, source_target_pairs={{0,1},{1,0},{2,3},{3,2},{4,5},{5,4},{6,7},{7,6},{8,9},{9,8},{10,11... | collective-permute-start | bytes 1179656 | tf_op jit(solution)/shard_map/ppermute | solution.py:87
  384.1 18.2 %collective-permute-start.60 = (bf16[2,64,1536]{2,1,0:T(8,128)(2,1)}, bf16[2,64,1536]{2,1,0:T(8,128)(2,1)}, u32[]{:S(2)}, u32[]{:S(2)}) collective-permute-start(bf16[2,64,1536]{2,1,0:T(8,128)(2,1)} %bitcast.120), channel_id=1, source_target_pairs={{0,2},{1,3},{2,0},{3,1},{4,6},{5,7},{6,4},{7,5},{8,10},{9,11},{10,... | collective-permute-start | bytes 1179656 | tf_op jit(solution)/shard_map/ppermute | solution.py:87
  384.6 18.5 %collective-permute-start.61 = (bf16[2,64,1536]{2,1,0:T(8,128)(2,1)}, bf16[2,64,1536]{2,1,0:T(8,128)(2,1)}, u32[]{:S(2)}, u32[]{:S(2)}) collective-permute-start(bf16[2,64,1536]{2,1,0:T(8,128)(2,1)} %bitcast.121), channel_id=1, source_target_pairs={{0,3},{1,2},{2,1},{3,0},{4,7},{5,6},{6,5},{7,4},{8,11},{9,10},{10,... | collective-permute-start | bytes 1179656 | tf_op jit(solution)/shard_map/ppermute | solution.py:87
  388.2 24.8 %collective-permute-start.62 = (bf16[2,48,3072]{2,1,0:T(8,128)(2,1)S(1)}, bf16[2,48,3072]{2,1,0:T(8,128)(2,1)S(1)}, u32[]{:S(2)}, u32[]{:S(2)}) collective-permute-start(bf16[2,48,3072]{2,1,0:T(8,128)(2,1)S(1)} %add_convert_fusion), channel_id=1, source_target_pairs={{0,8},{1,9},{2,10},{3,11},{4,12},{5,13},{6,14},{7,15},{8,16},{9,17... | collective-permute-start | bytes 1769480 | tf_op jit(solution)/shard_map/ppermute | solution.py:87
  397.0 13.3 %all-to-all-start.5 = ((f32[32,1,672]{2,1,0:T(1,128)}), f32[32,1,672]{2,1,0:T(1,128)S(1)}, u32[]{:S(2)}, u32[]{:S(2)}) async-start(f32[32,1,672]{2,1,0:T(1,128)} %reshape.271), calls=%async_computation.5 | async-start | bytes 196608 | tf_op jit(solution)/shard_map/all_to_all | solution.py:1087
  (94 other events, 608.1 us)

commit v5 on v4

--- a/solution.py
+++ b/solution.py
@@ -1009,9 +1009,12 @@
         kept["low"] = {mask: rows.astype(LOW) for mask, rows in result_sums.items()}
         return arrived
 
-    def far_back(_):
-        kept["far"] = rows_back(d_projected[images:], qkv_full).astype(LOW)
-        return (kept["far"], *kept["low"].values())
+    def far_back(clock):
+        kept["far"] = rows_back(after(d_projected, clock)[images:], qkv_full).astype(LOW)
+        d_rows = after(d_projected_rows, clock)
+        for step in range(1, deep):
+            partials[step] = partial_rows(step, d_rows)
+        return (kept["far"], partials[1][0], *kept["low"].values())
 
     def far_clock(*ahead):
         kept["far"] = wires.send(kept["far"], "core", *ahead)
@@ -1060,7 +1063,7 @@
         block = outer(rows, d_rows).astype(LOW).reshape(2, flat, shard, wide)
         return block, at(out_partial, at_plane, 0)
 
-    partials = [partial_rows(step, d_projected_rows) for step in range(deep)]
+    partials = {0: partial_rows(0, d_projected_rows)}
 
     def part(step, mask):
         block, out_block = partials[step]

time: 426 us -> 426 us (level)
  starting transfers between devices: 87.1 us -> 82.8 us
    unnamed x149 -> x173, local copies, waits for them, and re-layouts: 18.9 us -> 20.5 us
  transfers between devices with their start and end apart: 70 -> 70, of which waited for: 39 -> 36; matrix products, arithmetic and copies ran while one was open for 17% -> 18% of each run, Pallas kernels for 15% -> 15%
where the time goes in v5:
time: 426 us; the launch traced here: 421 us
  waiting for transfers between devices  153 us (36%)
  starting transfers between devices  82.8 us (19%)
  Pallas kernels  79.8 us (19%)
  local copies, waits for them, and re-layouts  42 us (10%)
  other arithmetic  40 us (9%)
  matrix products  20.7 us (5%)
    ppermute x64, waiting for transfers between devices, send(): return lax.ppermute(block, AXES, self.moves[kind])  140 us
    ppermute x64, starting transfers between devices, send(): return lax.ppermute(block, AXES, self.moves[kind])  54.5 us
    pallas_call x1, Pallas kernels, attend(): pl.pallas_call(kernel, grid=(slots,), out_shape=(jax.ShapeDtypeStruct((mo...  24.1 us
    unnamed x173, local copies, waits for them, and re-layouts  20.5 us
    dot_general x7, matrix products, dot(): lax.dot_general(left, right, (contract, ((), ())), preferred_element_type...  20.2 us
    all_to_all x4, starting transfers between devices, swap_blocks(): lax.all_to_all(blocks, AXES, 0, 0, tiled=True, axis_index_groups=groups)  18.4 us
    pallas_call x1, Pallas kernels, ffn_rows_back(): pl.pallas_call(kernel, grid=(rows // block,), out_shape=(low, low, low, l...  13.3 us
    pallas_call x1, Pallas kernels, sources_back(): pl.pallas_call(kernel, grid=(images,), out_shape=(jax.ShapeDtypeStruct((i...  11.5 us
  transfers between devices with their start and end apart: 70, of which 36 were waited for; matrix products, arithmetic and copies ran while one was open for 18% of the time, Pallas kernels for 15%

profile of v5, /device:TPU:0, one launch (start us, length us, event | category | flops | bytes accessed | tf_op | source)
XLA Modules:
  0.0 421.1 jit_solution(6889555810032769783)
XLA Ops:
  5.8 7.3 %all-to-all-start = ((bf16[32,2,336]{2,1,0:T(2,128)(2,1)}), bf16[32,2,336]{2,1,0:T(2,128)(2,1)S(1)}, u32[]{:S(2)}, u32[]{:S(2)}) async-start(bf16[32,2,336]{2,1,0:T(2,128)(2,1)} %reshape.269), calls=%async_computation | async-start | bytes 98304 | tf_op jit(solution)/shard_map/all_to_all | solution.py:894
  24.7 4.4 %collective-permute-done.4.refs_2_ = bf16[2,48,2304]{2,1,0:T(8,128)(2,1)} collective-permute-done((bf16[2,48,2304]{2,1,0:T(8,128)(2,1)S(1)}, bf16[2,48,2304]{2,1,0:T(8,128)(2,1)}, u32[]{:S(2)}, u32[]{:S(2)}) %collective-permute-start.4) | collective-permute-done | bytes 442400 | tf_op jit(solution)/shard_map/ppermute | solution.py:87
  29.1 2.0 shard_map.281
  31.2 3.9 all-to-all-start.1
  38.3 3.8 collective-permute-done.2
  50.7 7.2 %collective-permute-done.9.refs_7_ = bf16[2,48,2304]{2,1,0:T(8,128)(2,1)S(1)} collective-permute-done((bf16[2,48,2304]{2,1,0:T(8,128)(2,1)S(1)}, bf16[2,48,2304]{2,1,0:T(8,128)(2,1)S(1)}, u32[]{:S(2)}, u32[]{:S(2)}) %collective-permute-start.9) | collective-permute-done | bytes 442400 | tf_op jit(solution)/shard_map/ppermute | solution.py:87
  58.9 4.3 %collective-permute-done.7 = bf16[144,2304]{1,0:T(8,128)(2,1)} collective-permute-done((bf16[144,2304]{1,0:T(8,128)(2,1)}, bf16[144,2304]{1,0:T(8,128)(2,1)}, u32[]{:S(2)}, u32[]{:S(2)}) %collective-permute-start.7) | collective-permute-done | bytes 663584 | tf_op jit(solution)/shard_map/ppermute | solution.py:87
  64.3 2.6 broadcast_in_dim.57
  71.9 6.2 %collective-permute-done.14.refs_12_ = bf16[2,48,2304]{2,1,0:T(8,128)(2,1)S(1)} collective-permute-done((bf16[2,48,2304]{2,1,0:T(8,128)(2,1)S(1)}, bf16[2,48,2304]{2,1,0:T(8,128)(2,1)S(1)}, u32[]{:S(2)}, u32[]{:S(2)}) %collective-permute-start.14) | collective-permute-done | bytes 442400 | tf_op jit(solution)/shard_map/ppermute | solution.py:87
  80.0 5.5 %collective-permute-done.12 = bf16[144,2304]{1,0:T(8,128)(2,1)S(1)} collective-permute-done((bf16[144,2304]{1,0:T(8,128)(2,1)}, bf16[144,2304]{1,0:T(8,128)(2,1)S(1)}, u32[]{:S(2)}, u32[]{:S(2)}) %collective-permute-start.12) | collective-permute-done | bytes 663584 | tf_op jit(solution)/shard_map/ppermute | solution.py:87
  89.7 5.1 %all-to-all-start.2 = ((bf16[4,384,1536]{2,1,0:T(8,128)(2,1)}), bf16[4,384,1536]{2,1,0:T(8,128)(2,1)}, u32[]{:S(2)}, u32[]{:S(2)}) async-start(bf16[4,384,1536]{2,1,0:T(8,128)(2,1)} %broadcast_in_dim.57), calls=%async_computation.2 | async-start | bytes 9437184 | tf_op jit(solution)/shard_map/all_to_all | solution.py:90
  94.9 5.9 %collective-permute-done.20.refs_14_ = bf16[48,2304]{1,0:T(8,128)(2,1)} collective-permute-done((bf16[48,2304]{1,0:T(8,128)(2,1)S(1)}, bf16[48,2304]{1,0:T(8,128)(2,1)}, u32[]{:S(2)}, u32[]{:S(2)}) %collective-permute-start.20) | collective-permute-done | bytes 221216 | tf_op jit(solution)/shard_map/ppermute | solution.py:87
  103.4 5.7 %collective-permute-done.22.refs_19_ = bf16[48,2304]{1,0:T(8,128)(2,1)S(1)} collective-permute-done((bf16[48,2304]{1,0:T(8,128)(2,1)S(1)}, bf16[48,2304]{1,0:T(8,128)(2,1)S(1)}, u32[]{:S(2)}, u32[]{:S(2)}) %collective-permute-start.22) | collective-permute-done | bytes 221216 | tf_op jit(solution)/shard_map/ppermute | solution.py:87
  109.2 6.3 %collective-permute-done.21.refs_18_ = bf16[48,2304]{1,0:T(8,128)(2,1)S(1)} collective-permute-done((bf16[48,2304]{1,0:T(8,128)(2,1)S(1)}, bf16[48,2304]{1,0:T(8,128)(2,1)S(1)}, u32[]{:S(2)}, u32[]{:S(2)}) %collective-permute-start.21) | collective-permute-done | bytes 221216 | tf_op jit(solution)/shard_map/ppermute | solution.py:87
  122.9 24.1 %shard_map.282 = (bf16[1536,2304]{1,0:T(8,128)(2,1)}, bf16[4,320,1536]{2,1,0:T(8,128)(2,1)}, bf16[4,64,768]{2,1,0:T(8,128)(2,1)}, bf16[4,320,1536]{2,1,0:T(8,128...) custom-call(s32[32]{0:T(128)} %stack.324.places_ref, bf16[2,48,2304]{2,1,0:T(8,128)(2,1)} %copy-done.26, ...), custom_call_target="tpu_custom_call" | custom-call | flops 1 | bytes 1 | tf_op jit(solution)/shard_map/pallas_call | solution.py:491
  148.0 5.4 %shard_map.283 = (bf16[768,1536]{1,0:T(8,128)(2,1)S(1)}, f32[256,1536]{1,0:T(8,128)S(1)}) custom-call(s32[16]{0:T(128)S(1)} %stack.282.places_ref, bf16[4,48,1536]{2,1,0:T(8,128)(2,1)S(1)} %pad_maximum_fusion.4.refs_0_, bf16[4,48,1536]{2,1,0:T(8,128)(2,1)S(1)} %collective-permute-done.23.refs_1_, bf16[4,48,1536]{2,1,0:T(8,128)(2,1)S(1)} %collective-permute-done.24.refs_2_, ...), custom_call_target="tpu_custom_call" | custom-call | flops 1 | bytes 1 | tf_op jit(solution)/shard_map/pallas_call | solution.py:624
  163.1 6.7 %collective-permute-done.29 = bf16[2,64,1536]{2,1,0:T(8,128)(2,1)S(1)} collective-permute-done((bf16[2,64,1536]{2,1,0:T(8,128)(2,1)S(1)}, bf16[2,64,1536]{2,1,0:T(8,128)(2,1)S(1)}, u32[]{:S(2)}, u32[]{:S(2)}) %collective-permute-start.29) | collective-permute-done | bytes 393248 | tf_op jit(solution)/shard_map/ppermute | solution.py:87
  169.8 8.7 %collective-permute-done.30 = bf16[2,64,1536]{2,1,0:T(8,128)(2,1)S(1)} collective-permute-done((bf16[2,64,1536]{2,1,0:T(8,128)(2,1)S(1)}, bf16[2,64,1536]{2,1,0:T(8,128)(2,1)S(1)}, u32[]{:S(2)}, u32[]{:S(2)}) %collective-permute-start.30) | collective-permute-done | bytes 393248 | tf_op jit(solution)/shard_map/ppermute | solution.py:87
  180.1 2.2 collective-permute-done.32
  183.4 9.9 %all-to-all-done.2.refs_0_ = bf16[4,384,1536]{2,1,0:T(8,128)(2,1)} async-done(((bf16[4,384,1536]{2,1,0:T(8,128)(2,1)}), bf16[4,384,1536]{2,1,0:T(8,128)(2,1)}, u32[]{:S(2)}, u32[]{:S(2)}) %all-to-all-start.2) | async-done | bytes 4718624 | tf_op jit(solution)/shard_map/all_to_all | solution.py:90
  196.2 13.3 %shard_map.284 = (bf16[512,768]{1,0:T(8,128)(2,1)S(1)}, bf16[512,768]{1,0:T(8,128)(2,1)S(1)}, bf16[512,768]{1,0:T(8,128)(2,1)S(1)}, bf16[512,768]{1,0:T(8,128)(2...) custom-call(bf16[512,1536]{1,0:T(8,128)(2,1)S(1)} %bitcast.350, ...), custom_call_target="tpu_custom_call" | custom-call | flops 1 | bytes 1 | tf_op jit(solution)/shard_map/pallas_call | solution.py:728
  209.7 3.4 collective-permute-done.34
  217.3 11.0 %shard_map.285 = bf16[4,384,1536]{2,1,0:T(8,128)(2,1)} custom-call(bf16[512,1536]{1,0:T(8,128)(2,1)} %bitcast.351, bf16[512,1536]{1,0:T(8,128)(2,1)} %bitcast.358, bf16[512,1536]{1,0:T(8,128)(2,1)} %bitcast.349, bf16[512,1536]{1,0:T(8,128)(2,1)} %bitcast.356, bf16[512,768]{1,0:T(8,128)(2,1)} %copy-done.12, bf16[512,768]{1,0:T(8,128)(2,1)} %copy-done.13, ...), custom_call_target="tpu_custom_call" | custom-call | flops 1 | bytes 1 | tf_op jit(solution)/shard_map/pallas_call | solution.py:782
  228.4 5.9 %collective-permute-done.36 = bf16[2,64,1536]{2,1,0:T(8,128)(2,1)S(1)} collective-permute-done((bf16[2,64,1536]{2,1,0:T(8,128)(2,1)S(1)}, bf16[2,64,1536]{2,1,0:T(8,128)(2,1)S(1)}, u32[]{:S(2)}, u32[]{:S(2)}) %collective-permute-start.36) | collective-permute-done | bytes 393248 | tf_op jit(solution)/shard_map/ppermute | solution.py:87
  236.1 5.1 %all-to-all-start.3 = ((bf16[4,384,1536]{2,1,0:T(8,128)(2,1)}), bf16[4,384,1536]{2,1,0:T(8,128)(2,1)}, u32[]{:S(2)}, u32[]{:S(2)}) async-start(bf16[4,384,1536]{2,1,0:T(8,128)(2,1)} %shard_map.285), calls=%async_computation.3 | async-start | bytes 9437184 | tf_op jit(solution)/shard_map/all_to_all | solution.py:90
  247.8 6.0 %shard_map.286 = bf16[4,320,2304]{2,1,0:T(8,128)(2,1)S(1)} custom-call(bf16[4,64,768]{2,1,0:T(8,128)(2,1)S(1)} %fusion.8.d_ref, bf16[4,64,768]{2,1,0:T(8,128)(2,1)S(1)} %copy-done.18, bf16[4,320,1536]{2,1,0:T(8,128)(2,1)S(1)} %copy-done.8, f32[4,2,256,320]{3,2,1,0:T(8,128)S(1)} %copy-done.9), custom_call_target="tpu_custom_call" | custom-call | flops 1 | bytes 1 | tf_op jit(solution)/shard_map/pallas_call | solution.py:827
  257.0 2.5 convolution_convert_fusion.3
  262.0 7.1 %collective-permute-done.40 = bf16[48,3072]{1,0:T(8,128)(2,1)S(1)} collective-permute-done((bf16[48,3072]{1,0:T(8,128)(2,1)S(1)}, bf16[48,3072]{1,0:T(8,128)(2,1)S(1)}, u32[]{:S(2)}, u32[]{:S(2)}) %collective-permute-start.40) | collective-permute-done | bytes 294944 | tf_op jit(solution)/shard_map/ppermute | solution.py:87
  271.1 3.7 convolution_convert_fusion
  274.9 3.7 convolution_convert_fusion.1
  278.6 2.5 convolution_convert_fusion.2
  285.8 6.1 %fusion.2 = bf16[2,320,1536]{2,1,0:T(8,128)(2,1)} fusion(bf16[4,320,2304]{2,1,0:T(8,128)(2,1)S(1)} %shard_map.286, bf16[1536,2304]{1,0:T(8,128)(2,1)S(1)} %bitcast.361), kind=kOutput, calls=%fused_computation.41 | convolution fusion | flops 4530831360 | bytes 14942208 | tf_op jit(solution)/shard_map/dot_general | solution.py:33
  299.7 2.2 collective-permute-done.45
  305.1 7.9 %collective-permute-done.43 = bf16[2,48,3072]{2,1,0:T(8,128)(2,1)S(1)} collective-permute-done((bf16[2,48,3072]{2,1,0:T(8,128)(2,1)S(1)}, bf16[2,48,3072]{2,1,0:T(8,128)(2,1)S(1)}, u32[]{:S(2)}, u32[]{:S(2)}) %collective-permute-start.43) | collective-permute-done | bytes 589856 | tf_op jit(solution)/shard_map/ppermute | solution.py:87
  319.3 4.7 %collective-permute-done.49 = bf16[48,3072]{1,0:T(8,128)(2,1)S(1)} collective-permute-done((bf16[48,3072]{1,0:T(8,128)(2,1)S(1)}, bf16[48,3072]{1,0:T(8,128)(2,1)S(1)}, u32[]{:S(2)}, u32[]{:S(2)}) %collective-permute-start.49) | collective-permute-done | bytes 294944 | tf_op jit(solution)/shard_map/ppermute | solution.py:87
  326.6 11.5 %shard_map.287 = (f32[2,256,1536]{2,1,0:T(8,128)}, f32[2,64,1536]{2,1,0:T(8,128)}, f32[2,8,1536]{2,1,0:T(8,128)S(1)}) custom-call(bf16[2,320,2304]{2,1,0:T(8,128)(2,1)} %slice.329.d_ref, bf16[1536,2304]{1,0:T(8,128)(2,1)} %get-tuple-element.150.w_ref, bf16[2,320,1536]{2,1,0:T(8,128)(2,1)S(1)} %collective-permute-done.50.far_ref, ...), custom_call_target="tpu_custom_call" | custom-call | flops 1 | bytes 1 | tf_op jit(solution)/shard_map/pallas_call | solution.py:563
  346.8 2.8 collective-permute-done.55
  349.7 2.4 collective-permute-done.54
  353.9 7.1 %collective-permute-done.51 = bf16[2,48,3072]{2,1,0:T(8,128)(2,1)S(1)} collective-permute-done((bf16[2,48,3072]{2,1,0:T(8,128)(2,1)}, bf16[2,48,3072]{2,1,0:T(8,128)(2,1)S(1)}, u32[]{:S(2)}, u32[]{:S(2)}) %collective-permute-start.51) | collective-permute-done | bytes 589856 | tf_op jit(solution)/shard_map/ppermute | solution.py:87
  361.0 2.4 add_convert_fusion.1
  363.4 3.3 convert_reduce_fusion
  369.6 4.3 %all-to-all-start.4 = ((bf16[8,48,768]{2,1,0:T(8,128)(2,1)}), bf16[8,48,768]{2,1,0:T(8,128)(2,1)}, u32[]{:S(2)}, u32[]{:S(2)}) async-start(bf16[8,48,768]{2,1,0:T(8,128)(2,1)} %bitcast.367), calls=%async_computation.4 | async-start | bytes 1179648 | tf_op jit(solution)/shard_map/all_to_all | solution.py:90
  375.1 8.1 %collective-permute-done.58 = bf16[2,48,3072]{2,1,0:T(8,128)(2,1)} collective-permute-done((bf16[2,48,3072]{2,1,0:T(8,128)(2,1)}, bf16[2,48,3072]{2,1,0:T(8,128)(2,1)}, u32[]{:S(2)}, u32[]{:S(2)}) %collective-permute-start.58) | collective-permute-done | bytes 589856 | tf_op jit(solution)/shard_map/ppermute | solution.py:87
  390.3 9.4 %collective-permute-done.59 = bf16[2,64,1536]{2,1,0:T(8,128)(2,1)} collective-permute-done((bf16[2,64,1536]{2,1,0:T(8,128)(2,1)}, bf16[2,64,1536]{2,1,0:T(8,128)(2,1)}, u32[]{:S(2)}, u32[]{:S(2)}) %collective-permute-start.59) | collective-permute-done | bytes 393248 | tf_op jit(solution)/shard_map/ppermute | solution.py:87
  400.6 2.6 all-to-all-start.5
  405.1 2.2 multiply_convert_fusion
  407.3 2.4 shard_map.289
  418.8 2.2 shard_map.288
  (407 shorter events, 145.1 us)
Async XLA Ops:
  5.8 14.7 %all-to-all-start = ((bf16[32,2,336]{2,1,0:T(2,128)(2,1)}), bf16[32,2,336]{2,1,0:T(2,128)(2,1)S(1)}, u32[]{:S(2)}, u32[]{:S(2)}) async-start(bf16[32,2,336]{2,1,0:T(2,128)(2,1)} %reshape.269), calls=%async_computation | async-start | bytes 98304 | tf_op jit(solution)/shard_map/all_to_all | solution.py:894
  15.8 13.3 %collective-permute-start.4 = (bf16[2,48,2304]{2,1,0:T(8,128)(2,1)S(1)}, bf16[2,48,2304]{2,1,0:T(8,128)(2,1)}, u32[]{:S(2)}, u32[]{:S(2)}) collective-permute-start(bf16[2,48,2304]{2,1,0:T(8,128)(2,1)S(1)} %maximum_select_fusion.refs_0_), channel_id=1, source_target_pairs={{0,2},{1,3},{2,0},{3,1},{4,6},{5,7},{6,4},{7,5},{8,10},{9,11},{10,... | collective-permute-start | bytes 1327112 | tf_op jit(solution)/shard_map/ppermute | solution.py:87
  21.6 15.1 %collective-permute-start.3 = (bf16[2,48,2304]{2,1,0:T(8,128)(2,1)S(1)}, bf16[2,48,2304]{2,1,0:T(8,128)(2,1)}, u32[]{:S(2)}, u32[]{:S(2)}) collective-permute-start(bf16[2,48,2304]{2,1,0:T(8,128)(2,1)S(1)} %maximum_select_fusion.refs_0_), channel_id=1, source_target_pairs={{0,1},{1,0},{2,3},{3,2},{4,5},{5,4},{6,7},{7,6},{8,9},{9,8},{10,11... | collective-permute-start | bytes 1327112 | tf_op jit(solution)/shard_map/ppermute | solution.py:87
  22.0 21.0 %collective-permute-start.5 = (bf16[2,64,1536]{2,1,0:T(8,128)(2,1)}, bf16[2,64,1536]{2,1,0:T(8,128)(2,1)S(1)}, u32[]{:S(2)}, u32[]{:S(2)}) collective-permute-start(bf16[2,64,1536]{2,1,0:T(8,128)(2,1)} %broadcast_multiply_fusion), channel_id=1, source_target_pairs={{0,1},{1,0},{2,3},{3,2},{4,5},{5,4},{6,7},{7,6},{8,9},{9,8},{10,11... | collective-permute-start | bytes 1179656 | tf_op jit(solution)/shard_map/ppermute | solution.py:87
  23.6 19.5 %collective-permute-start.6 = (bf16[2,64,1536]{2,1,0:T(8,128)(2,1)}, bf16[2,64,1536]{2,1,0:T(8,128)(2,1)}, u32[]{:S(2)}, u32[]{:S(2)}) collective-permute-start(bf16[2,64,1536]{2,1,0:T(8,128)(2,1)} %broadcast_multiply_fusion), channel_id=1, source_target_pairs={{0,2},{1,3},{2,0},{3,1},{4,6},{5,7},{6,4},{7,5},{8,10},{9,11},{10,... | collective-permute-start | bytes 1179656 | tf_op jit(solution)/shard_map/ppermute | solution.py:87
  24.1 18.0 %collective-permute-start.2 = (bf16[144,2304]{1,0:T(8,128)(2,1)}, bf16[144,2304]{1,0:T(8,128)(2,1)S(1)}, u32[]{:S(2)}, u32[]{:S(2)}) collective-permute-start(bf16[144,2304]{1,0:T(8,128)(2,1)} %fusion.23), channel_id=1, source_target_pairs={{0,8},{1,9},{2,10},{3,11},{4,12},{5,13},{6,14},{7,15},{8,16},{9,17... | collective-permute-start | bytes 1990664 | tf_op jit(solution)/shard_map/ppermute | solution.py:87
  31.2 18.3 %all-to-all-start.1 = ((bf16[8,48,768]{2,1,0:T(8,128)(2,1)}), bf16[8,48,768]{2,1,0:T(8,128)(2,1)S(1)}, u32[]{:S(2)}, u32[]{:S(2)}) async-start(bf16[8,48,768]{2,1,0:T(8,128)(2,1)} %shard_map.281), calls=%async_computation.1 | async-start | bytes 1179648 | tf_op jit(solution)/shard_map/all_to_all | solution.py:90
  43.9 14.1 %collective-permute-start.9 = (bf16[2,48,2304]{2,1,0:T(8,128)(2,1)S(1)}, bf16[2,48,2304]{2,1,0:T(8,128)(2,1)S(1)}, u32[]{:S(2)}, u32[]{:S(2)}) collective-permute-start(bf16[2,48,2304]{2,1,0:T(8,128)(2,1)S(1)} %bitcast.372), channel_id=1, source_target_pairs={{0,2},{1,3},{2,0},{3,1},{4,6},{5,7},{6,4},{7,5},{8,10},{9,11},{10,... | collective-permute-start | bytes 1327112 | tf_op jit(solution)/shard_map/ppermute | solution.py:87
  44.4 14.5 %collective-permute-start.8 = (bf16[2,48,2304]{2,1,0:T(8,128)(2,1)S(1)}, bf16[2,48,2304]{2,1,0:T(8,128)(2,1)S(1)}, u32[]{:S(2)}, u32[]{:S(2)}) collective-permute-start(bf16[2,48,2304]{2,1,0:T(8,128)(2,1)S(1)} %bitcast.373), channel_id=1, source_target_pairs={{0,1},{1,0},{2,3},{3,2},{4,5},{5,4},{6,7},{7,6},{8,9},{9,8},{10,11... | collective-permute-start | bytes 1327112 | tf_op jit(solution)/shard_map/ppermute | solution.py:87
  45.2 19.1 %collective-permute-start.11 = (bf16[48,2304]{1,0:T(8,128)(2,1)}, bf16[48,2304]{1,0:T(8,128)(2,1)}, u32[]{:S(2)}, u32[]{:S(2)}) collective-permute-start(bf16[48,2304]{1,0:T(8,128)(2,1)} %slice_bitcast_fusion.8), channel_id=1, source_target_pairs={{0,1},{1,0},{2,3},{3,2},{4,5},{5,4},{6,7},{7,6},{8,9},{9,8},{10,11... | collective-permute-start | bytes 663560 | tf_op jit(solution)/shard_map/ppermute | solution.py:87
  46.4 17.9 %collective-permute-start.10 = (bf16[48,2304]{1,0:T(8,128)(2,1)}, bf16[48,2304]{1,0:T(8,128)(2,1)}, u32[]{:S(2)}, u32[]{:S(2)}) collective-permute-start(bf16[48,2304]{1,0:T(8,128)(2,1)} %slice_bitcast_fusion.9), channel_id=1, source_target_pairs={{0,2},{1,3},{2,0},{3,1},{4,6},{5,7},{6,4},{7,5},{8,10},{9,11},{10,... | collective-permute-start | bytes 663560 | tf_op jit(solution)/shard_map/ppermute | solution.py:87
  47.9 15.3 %collective-permute-start.7 = (bf16[144,2304]{1,0:T(8,128)(2,1)}, bf16[144,2304]{1,0:T(8,128)(2,1)}, u32[]{:S(2)}, u32[]{:S(2)}) collective-permute-start(bf16[144,2304]{1,0:T(8,128)(2,1)} %copy-done.60), channel_id=1, source_target_pairs={{0,8},{1,9},{2,10},{3,11},{4,12},{5,13},{6,14},{7,15},{8,16},{9,17... | collective-permute-start | bytes 1990664 | tf_op jit(solution)/shard_map/ppermute | solution.py:87
  69.1 16.5 %collective-permute-start.16 = (bf16[48,2304]{1,0:T(8,128)(2,1)S(1)}, bf16[48,2304]{1,0:T(8,128)(2,1)S(1)}, u32[]{:S(2)}, u32[]{:S(2)}) collective-permute-start(bf16[48,2304]{1,0:T(8,128)(2,1)S(1)} %slice_bitcast_fusion.6), channel_id=1, source_target_pairs={{0,1},{1,0},{2,3},{3,2},{4,5},{5,4},{6,7},{7,6},{8,9},{9,8},{10,11... | collective-permute-start | bytes 663560 | tf_op jit(solution)/shard_map/ppermute | solution.py:87
  70.0 15.5 %collective-permute-start.15 = (bf16[48,2304]{1,0:T(8,128)(2,1)S(1)}, bf16[48,2304]{1,0:T(8,128)(2,1)S(1)}, u32[]{:S(2)}, u32[]{:S(2)}) collective-permute-start(bf16[48,2304]{1,0:T(8,128)(2,1)S(1)} %slice_bitcast_fusion.7), channel_id=1, source_target_pairs={{0,2},{1,3},{2,0},{3,1},{4,6},{5,7},{6,4},{7,5},{8,10},{9,11},{10,... | collective-permute-start | bytes 663560 | tf_op jit(solution)/shard_map/ppermute | solution.py:87
  71.0 14.5 %collective-permute-start.12 = (bf16[144,2304]{1,0:T(8,128)(2,1)}, bf16[144,2304]{1,0:T(8,128)(2,1)S(1)}, u32[]{:S(2)}, u32[]{:S(2)}) collective-permute-start(bf16[144,2304]{1,0:T(8,128)(2,1)} %collective-permute-done.7), channel_id=1, source_target_pairs={{0,8},{1,9},{2,10},{3,11},{4,12},{5,13},{6,14},{7,15},{8,16},{9,17... | collective-permute-start | bytes 1990664 | tf_op jit(solution)/shard_map/ppermute | solution.py:87
  86.9 14.0 %collective-permute-start.17 = (bf16[2,48,2304]{2,1,0:T(8,128)(2,1)S(1)}, bf16[2,48,2304]{2,1,0:T(8,128)(2,1)S(1)}, u32[]{:S(2)}, u32[]{:S(2)}) collective-permute-start(bf16[2,48,2304]{2,1,0:T(8,128)(2,1)S(1)} %bitcast.379), channel_id=1, source_target_pairs={{0,1},{1,0},{2,3},{3,2},{4,5},{5,4},{6,7},{7,6},{8,9},{9,8},{10,11... | collective-permute-start | bytes 1327112 | tf_op jit(solution)/shard_map/ppermute | solution.py:87
  87.6 13.2 %collective-permute-start.20 = (bf16[48,2304]{1,0:T(8,128)(2,1)S(1)}, bf16[48,2304]{1,0:T(8,128)(2,1)}, u32[]{:S(2)}, u32[]{:S(2)}) collective-permute-start(bf16[48,2304]{1,0:T(8,128)(2,1)S(1)} %slice_bitcast_fusion.3), channel_id=1, source_target_pairs={{0,1},{1,0},{2,3},{3,2},{4,5},{5,4},{6,7},{7,6},{8,9},{9,8},{10,11... | collective-permute-start | bytes 663560 | tf_op jit(solution)/shard_map/ppermute | solution.py:87
  88.9 11.9 %collective-permute-start.19 = (bf16[48,2304]{1,0:T(8,128)(2,1)}, bf16[48,2304]{1,0:T(8,128)(2,1)}, u32[]{:S(2)}, u32[]{:S(2)}) collective-permute-start(bf16[48,2304]{1,0:T(8,128)(2,1)} %slice_bitcast_fusion.4), channel_id=1, source_target_pairs={{0,2},{1,3},{2,0},{3,1},{4,6},{5,7},{6,4},{7,5},{8,10},{9,11},{10,... | collective-permute-start | bytes 663560 | tf_op jit(solution)/shard_map/ppermute | solution.py:87
  89.7 103.7 %all-to-all-start.2 = ((bf16[4,384,1536]{2,1,0:T(8,128)(2,1)}), bf16[4,384,1536]{2,1,0:T(8,128)(2,1)}, u32[]{:S(2)}, u32[]{:S(2)}) async-start(bf16[4,384,1536]{2,1,0:T(8,128)(2,1)} %broadcast_in_dim.57), calls=%async_computation.2 | async-start | bytes 9437184 | tf_op jit(solution)/shard_map/all_to_all | solution.py:90
  101.4 14.0 %collective-permute-start.21 = (bf16[48,2304]{1,0:T(8,128)(2,1)S(1)}, bf16[48,2304]{1,0:T(8,128)(2,1)S(1)}, u32[]{:S(2)}, u32[]{:S(2)}) collective-permute-start(bf16[48,2304]{1,0:T(8,128)(2,1)S(1)} %slice_bitcast_fusion.5), channel_id=1, source_target_pairs={{0,2},{1,3},{2,0},{3,1},{4,6},{5,7},{6,4},{7,5},{8,10},{9,11},{10,... | collective-permute-start | bytes 663560 | tf_op jit(solution)/shard_map/ppermute | solution.py:87
  116.1 30.9 %collective-permute-start.23 = (bf16[4,48,1536]{2,1,0:T(8,128)(2,1)S(1)}, bf16[4,48,1536]{2,1,0:T(8,128)(2,1)S(1)}, u32[]{:S(2)}, u32[]{:S(2)}) collective-permute-start(bf16[4,48,1536]{2,1,0:T(8,128)(2,1)S(1)} %pad_maximum_fusion.4.refs_0_), channel_id=1, source_target_pairs={{0,3},{1,2},{2,1},{3,0},{4,7},{5,6},{6,5},{7,4},{8,11},{9,10},{10,... | collective-permute-start | bytes 1769480 | tf_op jit(solution)/shard_map/ppermute | solution.py:87
  117.7 29.3 %collective-permute-start.24 = (bf16[4,48,1536]{2,1,0:T(8,128)(2,1)S(1)}, bf16[4,48,1536]{2,1,0:T(8,128)(2,1)S(1)}, u32[]{:S(2)}, u32[]{:S(2)}) collective-permute-start(bf16[4,48,1536]{2,1,0:T(8,128)(2,1)S(1)} %pad_maximum_fusion.4.refs_0_), channel_id=1, source_target_pairs={{0,2},{1,3},{2,0},{3,1},{4,6},{5,7},{6,4},{7,5},{8,10},{9,11},{10,... | collective-permute-start | bytes 1769480 | tf_op jit(solution)/shard_map/ppermute | solution.py:87
  119.1 28.0 %collective-permute-start.25 = (bf16[4,48,1536]{2,1,0:T(8,128)(2,1)S(1)}, bf16[4,48,1536]{2,1,0:T(8,128)(2,1)S(1)}, u32[]{:S(2)}, u32[]{:S(2)}) collective-permute-start(bf16[4,48,1536]{2,1,0:T(8,128)(2,1)S(1)} %pad_maximum_fusion.4.refs_0_), channel_id=1, source_target_pairs={{0,1},{1,0},{2,3},{3,2},{4,5},{5,4},{6,7},{7,6},{8,9},{9,8},{10,11... | collective-permute-start | bytes 1769480 | tf_op jit(solution)/shard_map/ppermute | solution.py:87
  119.8 27.2 %collective-permute-start.27 = (bf16[2,64,1536]{2,1,0:T(8,128)(2,1)}, bf16[2,64,1536]{2,1,0:T(8,128)(2,1)}, u32[]{:S(2)}, u32[]{:S(2)}) collective-permute-start(bf16[2,64,1536]{2,1,0:T(8,128)(2,1)} %broadcast_multiply_fusion), channel_id=1, source_target_pairs={{0,3},{1,2},{2,1},{3,0},{4,7},{5,6},{6,5},{7,4},{8,11},{9,10},{10,... | collective-permute-start | bytes 1179656 | tf_op jit(solution)/shard_map/ppermute | solution.py:87
  157.8 12.0 %collective-permute-start.29 = (bf16[2,64,1536]{2,1,0:T(8,128)(2,1)S(1)}, bf16[2,64,1536]{2,1,0:T(8,128)(2,1)S(1)}, u32[]{:S(2)}, u32[]{:S(2)}) collective-permute-start(bf16[2,64,1536]{2,1,0:T(8,128)(2,1)S(1)} %add_convert_fusion.3), channel_id=1, source_target_pairs={{0,1},{1,0},{2,3},{3,2},{4,5},{5,4},{6,7},{7,6},{8,9},{9,8},{10,11... | collective-permute-start | bytes 1179656 | tf_op jit(solution)/shard_map/ppermute | solution.py:87
  159.2 19.3 %collective-permute-start.30 = (bf16[2,64,1536]{2,1,0:T(8,128)(2,1)S(1)}, bf16[2,64,1536]{2,1,0:T(8,128)(2,1)S(1)}, u32[]{:S(2)}, u32[]{:S(2)}) collective-permute-start(bf16[2,64,1536]{2,1,0:T(8,128)(2,1)S(1)} %add_convert_fusion.3), channel_id=1, source_target_pairs={{0,2},{1,3},{2,0},{3,1},{4,6},{5,7},{6,4},{7,5},{8,10},{9,11},{10,... | collective-permute-start | bytes 1179656 | tf_op jit(solution)/shard_map/ppermute | solution.py:87
  159.8 18.8 %collective-permute-start.31 = (bf16[2,64,1536]{2,1,0:T(8,128)(2,1)S(1)}, bf16[2,64,1536]{2,1,0:T(8,128)(2,1)S(1)}, u32[]{:S(2)}, u32[]{:S(2)}) collective-permute-start(bf16[2,64,1536]{2,1,0:T(8,128)(2,1)S(1)} %add_convert_fusion.3), channel_id=1, source_target_pairs={{0,3},{1,2},{2,1},{3,0},{4,7},{5,6},{6,5},{7,4},{8,11},{9,10},{10,... | collective-permute-start | bytes 1179656 | tf_op jit(solution)/shard_map/ppermute | solution.py:87
  162.8 16.1 %collective-permute-start.33 = (bf16[4,2,64,1536]{3,2,1,0:T(8,128)(2,1)S(1)}, bf16[4,2,64,1536]{3,2,1,0:T(8,128)(2,1)S(1)}, u32[]{:S(2)}, u32[]{:S(2)}) collective-permute-start(bf16[4,2,64,1536]{3,2,1,0:T(8,128)(2,1)S(1)} %pad_maximum_fusion.2), channel_id=1, source_target_pairs={{0,4},{1,5},{2,6},{3,7},{4,0},{5,1},{6,2},{7,3},{8,12},{9,13},{10,... | collective-permute-start | bytes 4718600 | tf_op jit(solution)/shard_map/ppermute | solution.py:87
  213.8 14.6 %collective-permute-start.35 = (bf16[2,64,1536]{2,1,0:T(8,128)(2,1)S(1)}, bf16[2,64,1536]{2,1,0:T(8,128)(2,1)S(1)}, u32[]{:S(2)}, u32[]{:S(2)}) collective-permute-start(bf16[2,64,1536]{2,1,0:T(8,128)(2,1)S(1)} %bitcast.390), channel_id=1, source_target_pairs={{0,3},{1,2},{2,1},{3,0},{4,7},{5,6},{6,5},{7,4},{8,11},{9,10},{10,... | collective-permute-start | bytes 1179656 | tf_op jit(solution)/shard_map/ppermute | solution.py:87
  215.3 19.1 %collective-permute-start.36 = (bf16[2,64,1536]{2,1,0:T(8,128)(2,1)S(1)}, bf16[2,64,1536]{2,1,0:T(8,128)(2,1)S(1)}, u32[]{:S(2)}, u32[]{:S(2)}) collective-permute-start(bf16[2,64,1536]{2,1,0:T(8,128)(2,1)S(1)} %bitcast.388), channel_id=1, source_target_pairs={{0,2},{1,3},{2,0},{3,1},{4,6},{5,7},{6,4},{7,5},{8,10},{9,11},{10,... | collective-permute-start | bytes 1179656 | tf_op jit(solution)/shard_map/ppermute | solution.py:87
  216.9 17.4 %collective-permute-start.37 = (bf16[2,64,1536]{2,1,0:T(8,128)(2,1)S(1)}, bf16[2,64,1536]{2,1,0:T(8,128)(2,1)S(1)}, u32[]{:S(2)}, u32[]{:S(2)}) collective-permute-start(bf16[2,64,1536]{2,1,0:T(8,128)(2,1)S(1)} %bitcast.387), channel_id=1, source_target_pairs={{0,1},{1,0},{2,3},{3,2},{4,5},{5,4},{6,7},{7,6},{8,9},{9,8},{10,11... | collective-permute-start | bytes 1179656 | tf_op jit(solution)/shard_map/ppermute | solution.py:87
  236.1 127.2 %all-to-all-start.3 = ((bf16[4,384,1536]{2,1,0:T(8,128)(2,1)}), bf16[4,384,1536]{2,1,0:T(8,128)(2,1)}, u32[]{:S(2)}, u32[]{:S(2)}) async-start(bf16[4,384,1536]{2,1,0:T(8,128)(2,1)} %shard_map.285), calls=%async_computation.3 | async-start | bytes 9437184 | tf_op jit(solution)/shard_map/all_to_all | solution.py:90
  294.1 18.9 %collective-permute-start.43 = (bf16[2,48,3072]{2,1,0:T(8,128)(2,1)S(1)}, bf16[2,48,3072]{2,1,0:T(8,128)(2,1)S(1)}, u32[]{:S(2)}, u32[]{:S(2)}) collective-permute-start(bf16[2,48,3072]{2,1,0:T(8,128)(2,1)S(1)} %copy-done.59), channel_id=1, source_target_pairs={{0,1},{1,0},{2,3},{3,2},{4,5},{5,4},{6,7},{7,6},{8,9},{9,8},{10,11... | collective-permute-start | bytes 1769480 | tf_op jit(solution)/shard_map/ppermute | solution.py:87
  295.2 19.0 %collective-permute-start.44 = (bf16[2,48,3072]{2,1,0:T(8,128)(2,1)S(1)}, bf16[2,48,3072]{2,1,0:T(8,128)(2,1)S(1)}, u32[]{:S(2)}, u32[]{:S(2)}) collective-permute-start(bf16[2,48,3072]{2,1,0:T(8,128)(2,1)S(1)} %copy-done.58), channel_id=1, source_target_pairs={{0,2},{1,3},{2,0},{3,1},{4,6},{5,7},{6,4},{7,5},{8,10},{9,11},{10,... | collective-permute-start | bytes 1769480 | tf_op jit(solution)/shard_map/ppermute | solution.py:87
  314.2 11.6 %collective-permute-start.50 = (bf16[2,320,1536]{2,1,0:T(8,128)(2,1)S(1)}, bf16[2,320,1536]{2,1,0:T(8,128)(2,1)S(1)}, u32[]{:S(2)}, u32[]{:S(2)}) collective-permute-start(bf16[2,320,1536]{2,1,0:T(8,128)(2,1)S(1)} %copy-done.80), channel_id=1, source_target_pairs={{0,4},{1,5},{2,6},{3,7},{4,0},{5,1},{6,2},{7,3},{8,12},{9,13},{10,... | collective-permute-start | bytes 5898248 | tf_op jit(solution)/shard_map/ppermute | solution.py:87
  316.1 23.3 %collective-permute-start.47 = (bf16[2,48,3072]{2,1,0:T(8,128)(2,1)}, bf16[2,48,3072]{2,1,0:T(8,128)(2,1)}, u32[]{:S(2)}, u32[]{:S(2)}) collective-permute-start(bf16[2,48,3072]{2,1,0:T(8,128)(2,1)} %pad_maximum_fusion.6), channel_id=1, source_target_pairs={{0,2},{1,3},{2,0},{3,1},{4,6},{5,7},{6,4},{7,5},{8,10},{9,11},{10,... | collective-permute-start | bytes 1769480 | tf_op jit(solution)/shard_map/ppermute | solution.py:87
  316.7 22.7 %collective-permute-start.46 = (bf16[2,48,3072]{2,1,0:T(8,128)(2,1)}, bf16[2,48,3072]{2,1,0:T(8,128)(2,1)}, u32[]{:S(2)}, u32[]{:S(2)}) collective-permute-start(bf16[2,48,3072]{2,1,0:T(8,128)(2,1)} %fusion.25), channel_id=1, source_target_pairs={{0,1},{1,0},{2,3},{3,2},{4,5},{5,4},{6,7},{7,6},{8,9},{9,8},{10,11... | collective-permute-start | bytes 1769480 | tf_op jit(solution)/shard_map/ppermute | solution.py:87
  343.3 24.5 %collective-permute-start.53 = (bf16[2,48,3072]{2,1,0:T(8,128)(2,1)}, bf16[2,48,3072]{2,1,0:T(8,128)(2,1)}, u32[]{:S(2)}, u32[]{:S(2)}) collective-permute-start(bf16[2,48,3072]{2,1,0:T(8,128)(2,1)} %pad_maximum_fusion.7), channel_id=1, source_target_pairs={{0,2},{1,3},{2,0},{3,1},{4,6},{5,7},{6,4},{7,5},{8,10},{9,11},{10,... | collective-permute-start | bytes 1769480 | tf_op jit(solution)/shard_map/ppermute | solution.py:87
  343.9 23.8 %collective-permute-start.52 = (bf16[2,48,3072]{2,1,0:T(8,128)(2,1)}, bf16[2,48,3072]{2,1,0:T(8,128)(2,1)}, u32[]{:S(2)}, u32[]{:S(2)}) collective-permute-start(bf16[2,48,3072]{2,1,0:T(8,128)(2,1)} %fusion.29), channel_id=1, source_target_pairs={{0,1},{1,0},{2,3},{3,2},{4,5},{5,4},{6,7},{7,6},{8,9},{9,8},{10,11... | collective-permute-start | bytes 1769480 | tf_op jit(solution)/shard_map/ppermute | solution.py:87
  345.4 15.6 %collective-permute-start.51 = (bf16[2,48,3072]{2,1,0:T(8,128)(2,1)}, bf16[2,48,3072]{2,1,0:T(8,128)(2,1)S(1)}, u32[]{:S(2)}, u32[]{:S(2)}) collective-permute-start(bf16[2,48,3072]{2,1,0:T(8,128)(2,1)} %add_convert_fusion.2), channel_id=1, source_target_pairs={{0,8},{1,9},{2,10},{3,11},{4,12},{5,13},{6,14},{7,15},{8,16},{9,17... | collective-permute-start | bytes 1769480 | tf_op jit(solution)/shard_map/ppermute | solution.py:87
  367.7 15.5 %collective-permute-start.58 = (bf16[2,48,3072]{2,1,0:T(8,128)(2,1)}, bf16[2,48,3072]{2,1,0:T(8,128)(2,1)}, u32[]{:S(2)}, u32[]{:S(2)}) collective-permute-start(bf16[2,48,3072]{2,1,0:T(8,128)(2,1)} %pad_maximum_fusion.9), channel_id=1, source_target_pairs={{0,2},{1,3},{2,0},{3,1},{4,6},{5,7},{6,4},{7,5},{8,10},{9,11},{10,... | collective-permute-start | bytes 1769480 | tf_op jit(solution)/shard_map/ppermute | solution.py:87
  368.4 16.6 %collective-permute-start.57 = (bf16[2,48,3072]{2,1,0:T(8,128)(2,1)}, bf16[2,48,3072]{2,1,0:T(8,128)(2,1)}, u32[]{:S(2)}, u32[]{:S(2)}) collective-permute-start(bf16[2,48,3072]{2,1,0:T(8,128)(2,1)} %fusion.31), channel_id=1, source_target_pairs={{0,1},{1,0},{2,3},{3,2},{4,5},{5,4},{6,7},{7,6},{8,9},{9,8},{10,11... | collective-permute-start | bytes 1769480 | tf_op jit(solution)/shard_map/ppermute | solution.py:87
  369.6 15.3 %collective-permute-start.56 = (bf16[2,48,3072]{2,1,0:T(8,128)(2,1)}, bf16[2,48,3072]{2,1,0:T(8,128)(2,1)}, u32[]{:S(2)}, u32[]{:S(2)}) collective-permute-start(bf16[2,48,3072]{2,1,0:T(8,128)(2,1)} %add_convert_fusion.1), channel_id=1, source_target_pairs={{0,8},{1,9},{2,10},{3,11},{4,12},{5,13},{6,14},{7,15},{8,16},{9,17... | collective-permute-start | bytes 1769480 | tf_op jit(solution)/shard_map/ppermute | solution.py:87
  369.6 20.7 %all-to-all-start.4 = ((bf16[8,48,768]{2,1,0:T(8,128)(2,1)}), bf16[8,48,768]{2,1,0:T(8,128)(2,1)}, u32[]{:S(2)}, u32[]{:S(2)}) async-start(bf16[8,48,768]{2,1,0:T(8,128)(2,1)} %bitcast.367), calls=%async_computation.4 | async-start | bytes 1179648 | tf_op jit(solution)/shard_map/all_to_all | solution.py:90
  384.9 14.7 %collective-permute-start.59 = (bf16[2,64,1536]{2,1,0:T(8,128)(2,1)}, bf16[2,64,1536]{2,1,0:T(8,128)(2,1)}, u32[]{:S(2)}, u32[]{:S(2)}) collective-permute-start(bf16[2,64,1536]{2,1,0:T(8,128)(2,1)} %bitcast.109), channel_id=1, source_target_pairs={{0,1},{1,0},{2,3},{3,2},{4,5},{5,4},{6,7},{7,6},{8,9},{9,8},{10,11... | collective-permute-start | bytes 1179656 | tf_op jit(solution)/shard_map/ppermute | solution.py:87
  386.2 16.9 %collective-permute-start.60 = (bf16[2,64,1536]{2,1,0:T(8,128)(2,1)}, bf16[2,64,1536]{2,1,0:T(8,128)(2,1)}, u32[]{:S(2)}, u32[]{:S(2)}) collective-permute-start(bf16[2,64,1536]{2,1,0:T(8,128)(2,1)} %bitcast.120), channel_id=1, source_target_pairs={{0,2},{1,3},{2,0},{3,1},{4,6},{5,7},{6,4},{7,5},{8,10},{9,11},{10,... | collective-permute-start | bytes 1179656 | tf_op jit(solution)/shard_map/ppermute | solution.py:87
  386.6 18.5 %collective-permute-start.61 = (bf16[2,64,1536]{2,1,0:T(8,128)(2,1)}, bf16[2,64,1536]{2,1,0:T(8,128)(2,1)}, u32[]{:S(2)}, u32[]{:S(2)}) collective-permute-start(bf16[2,64,1536]{2,1,0:T(8,128)(2,1)} %bitcast.121), channel_id=1, source_target_pairs={{0,3},{1,2},{2,1},{3,0},{4,7},{5,6},{6,5},{7,4},{8,11},{9,10},{10,... | collective-permute-start | bytes 1179656 | tf_op jit(solution)/shard_map/ppermute | solution.py:87
  390.2 23.6 %collective-permute-start.62 = (bf16[2,48,3072]{2,1,0:T(8,128)(2,1)S(1)}, bf16[2,48,3072]{2,1,0:T(8,128)(2,1)S(1)}, u32[]{:S(2)}, u32[]{:S(2)}) collective-permute-start(bf16[2,48,3072]{2,1,0:T(8,128)(2,1)S(1)} %add_convert_fusion), channel_id=1, source_target_pairs={{0,8},{1,9},{2,10},{3,11},{4,12},{5,13},{6,14},{7,15},{8,16},{9,17... | collective-permute-start | bytes 1769480 | tf_op jit(solution)/shard_map/ppermute | solution.py:87
  (106 other events, 682.8 us)
